TPU v7x, 512 devices: a whole 4x8x8 slice. The times are simulated.
512 devices in a mesh: gx: 8 (over z), gy: 8 (over y_hi, core), af: 8 (over y_lo, x).
Axes of the slice: x: 4, y: 8 (y_hi: 4, y_lo: 2; y = y_hi * 2 + y_lo), z: 8, core: 2. Of those that a mesh axis runs over, the one named last changes fastest.
Arguments:
- volume: bfloat16 [1, 64, 64, 16, 128], P(None, 'gx', 'gy', None, 'af'), may hold values from -6 to 6
- first_filter: bfloat16 [128, 27, 128], P('af'), may hold values from -0.109375 to 0.109375
- second_filter: bfloat16 [128, 27, 128], P('af'), may hold values from -0.109375 to 0.109375
- out_grad: bfloat16 [1, 64, 64, 16, 128], P(None, 'gx', 'gy', None, 'af'), may hold values from -6 to 6
Outputs:
- output: bfloat16 [1, 64, 64, 16, 128], P(None, 'gx', 'gy', None, 'af')
- volume_grad: bfloat16 [1, 64, 64, 16, 128], P(None, 'gx', 'gy', None, 'af')
- first_grad: float32 [128, 27, 128], P('af')
- second_grad: float32 [128, 27, 128], P('af')
All inputs are finite; a program needn't handle non-finite values.
Results may differ from a plain program's by a relative error of at most 0.017.
Values may be sent and summed in bfloat16 or wider, within the bound.
No kernel may reach another device: no remote copies, remote signals or barrier semaphores. Data moves between devices by JAX's collectives and lax.ppermute only.
A program may use at most 192 MiB of HBM per device.

v0:
```python
import math

import jax
import jax.numpy as jnp
from jax import lax
from jax.sharding import PartitionSpec as P


def with_halo(shard, sides, width):
    for axis, dim in sides:
        size, length = (lax.axis_size(axis), shard.shape[dim])
        up = [(i, (i + 1) % size) for i in range(size - 1)]
        down = [(j, i) for i, j in up]
        last = lax.slice_in_dim(shard, length - width, length, axis=dim)
        leading = lax.slice_in_dim(shard, 0, width, axis=dim)
        before = lax.ppermute(last, axis, up)
        after = lax.ppermute(leading, axis, down)
        shard = jnp.concatenate([before, shard, after], axis=dim)
    return shard


def conv_valid(padded, kernel, spec):
    return lax.conv_general_dilated(
        padded,
        kernel,
        (1, 1, 1),
        "VALID",
        dimension_numbers=("NDHWC", spec, "NDHWC"),
        preferred_element_type=jnp.float32,
    )


def pad_depth(field):
    return jnp.pad(field, ((0, 0), (0, 0), (0, 0), (1, 1), (0, 0)))


def flipped(weight):
    kernel = weight.reshape(weight.shape[0], 3, 3, 3, weight.shape[2])
    return kernel[:, ::-1, ::-1, ::-1, :]


def forward_layer(act, weight):
    rimmed = with_halo(act, (("gx", 1), ("gy", 2)), 1)
    full = lax.all_gather(pad_depth(rimmed), "af", axis=4, tiled=True)
    kernel = weight.reshape(weight.shape[0], 3, 3, 3, weight.shape[2])
    return (conv_valid(full, kernel, "ODHWI"), full)


def backward_input(grad, weight):
    rimmed = pad_depth(with_halo(grad, (("gx", 1), ("gy", 2)), 1))
    term = conv_valid(rimmed, flipped(weight), "IDHWO")
    return lax.psum_scatter(term, "af", scatter_dimension=4, tiled=True)


def filter_grad(full, grad):
    sx, sy, sz = (grad.shape[1], grad.shape[2], grad.shape[3])
    taps = []
    for first in range(3):
        for second in range(3):
            for third in range(3):
                piece = full[:, first : first + sx, second : second + sy, third : third + sz, :]
                taps.append(
                    jnp.einsum("bxyzi,bxyzo->oi", piece, grad, preferred_element_type=jnp.float32)
                )
    return jnp.stack(taps, axis=1)


def on_device(volume, first_filter, second_filter, out_grad):
    count = (
        volume.shape[0]
        * volume.shape[1]
        * lax.axis_size("gx")
        * volume.shape[2]
        * lax.axis_size("gy")
        * volume.shape[3]
    )
    factor = 1.0 / math.sqrt(count)
    pre_raw, volume_full = forward_layer(volume, first_filter)
    pre = pre_raw.astype(jnp.bfloat16)
    pref = pre.astype(jnp.float32)
    hidden = jax.nn.silu(pref).astype(jnp.bfloat16)
    out_raw, hidden_full = forward_layer(hidden, second_filter)
    output = out_raw.astype(jnp.bfloat16)
    second_grad = filter_grad(hidden_full, out_grad)
    second_grad = lax.psum(second_grad, ("gx", "gy"))
    hidden_grad = backward_input(out_grad, second_filter)
    sig = jax.nn.sigmoid(pref)
    pre_grad = (hidden_grad * sig * (1.0 + pref * (1.0 - sig))).astype(jnp.bfloat16)
    volume_grad = backward_input(pre_grad, first_filter).astype(jnp.bfloat16)
    first_grad = filter_grad(volume_full, pre_grad)
    first_grad = lax.psum(first_grad, ("gx", "gy"))
    return (output, volume_grad, first_grad * factor, second_grad * factor)


def solution(mesh):
    placed = (
        P(None, "gx", "gy", None, "af"),
        P("af", None, None),
        P("af", None, None),
        P(None, "gx", "gy", None, "af"),
    )
    return jax.shard_map(
        on_device,
        mesh=mesh,
        in_specs=placed,
        out_specs=(
            P(None, "gx", "gy", None, "af"),
            P(None, "gx", "gy", None, "af"),
            P("af", None, None),
            P("af", None, None),
        ),
        check_vma=False,
    )
```

profile of v0, /device:TPU:16, one launch (start us, length us, event | category | flops | bytes accessed | tf_op | source)
XLA Modules:
  0.0 927.7 jit_solution(7994995733269547308)
XLA Ops:
  8.4 4.3 collective-permute-start
  16.0 5.5 collective-permute-start.8
  23.5 4.5 collective-permute-start.3
  29.2 3.2 collective-permute-start.10
  32.4 3.3 collective-permute-start.11
  35.9 39.1 %all_gather.6 = bf16[1,10,10,18,128]{3,4,2,1,0:T(8,128)(2,1)S(1)} all-gather(bf16[1,10,10,18,16]{3,4,2,1,0:T(8,128)(2,1)S(1)} %select_maximum_fusion), channel_id=1, replica_groups=mesh['gx'=8,'gy'=8,'af'=8] {'af'}, dimensions={4}, use_global_device_ids=true | all-gather | bytes 518400 | tf_op jit(solution)/shard_map/all_gather | solution.py:44
  75.0 7.5 fusion.246
  82.5 14.6 %fusion.245 = (bf16[1,8,8,16,128]{3,4,2,1,0:T(8,128)(2,1)}, bf16[1,8,8,16,128]{3,4,2,1,0:T(8,128)(2,1)}, bf16[1,8,8,16,128]{3,4,2,1,0:T(8,128)(2,1)}, bf16[1,8,8...) fusion(bf16[1,10,10,18,128]{3,4,2,1,0:T(8,128)(2,1)S(1)} %all_g, ...), kind=kLoop, calls=%fused_computation.333 | loop fusion | bytes 9961472 | tf_op jit(solution)/shard_map/slice | solution.py:61
  97.2 2.9 copy.359
  101.9 4.1 add_divide_fusion
  107.0 4.3 collective-permute-start.4
  114.1 4.6 collective-permute-done.5
  121.4 4.9 collective-permute-start.7
  128.5 7.4 copy.301
  135.9 7.6 reshape.412
  143.6 2.7 copy.312
  150.3 2.7 copy.309
  157.1 2.7 copy.306
  177.2 2.7 copy.324
  183.9 2.7 copy.321
  190.7 2.7 copy.318
  197.4 2.7 copy.315
  205.2 37.2 %all_gather.7 = bf16[1,10,10,18,128]{3,4,2,1,0:T(8,128)(2,1)S(1)} all-gather(bf16[1,10,10,18,16]{3,4,2,1,0:T(8,128)(2,1)S(1)} %pad.10.clone), channel_id=1, replica_groups=mesh['gx'=8,'gy'=8,'af'=8] {'af'}, dimensions={4}, use_global_device_ids=true | all-gather | bytes 518400 | tf_op jit(solution)/shard_map/all_gather | solution.py:44
  291.2 5.3 collective-permute-start.12
  323.2 4.8 collective-permute-start.15
  328.9 4.4 collective-permute-done.15
  337.5 8.3 copy.303
  345.8 7.6 reshape.414
  353.4 2.9 copy.361
  358.4 2.9 fusion.33
  362.1 511.8 %all-reduce.5.cloned.1.call-done = (f32[16,27,128]{2,0,1:T(8,128)}, f32[16,27,128]{2,0,1:T(8,128)}) async-done(((f32[16,27,128]{2,0,1:T(8,128)}, f32[16,27,128]{2,0,1:T(8,128)}), (f32[16,27,128]{2,0,1:T(8,128)}, f32[16,27,128]{2,0,1:T(8,128)})) %all-reduce.5.cloned.1.call-update) | async-done | bytes 442384 | tf_op jit(solution)/shard_map/psum | solution.py:91
  875.8 42.2 %reduce-scatter.9.cloned.1.call-done = f32[16,1024]{1,0:T(8,128)} async-done(((f32[128,1024]{1,0:T(8,128)}), f32[16,1024]{1,0:T(8,128)}) %reduce-scatter.9.cloned.1.call-update) | async-done | bytes 65552
  (247 shorter events, 148.7 us)
Async XLA Ops:
  7.2 94.6 %copy-start = (bf16[16,27,128]{2,0,1:T(8,128)(2,1)S(1)}, bf16[16,27,128]{2,0,1:T(8,128)(2,1)}, u32[]{:S(2)}) copy-start(bf16[16,27,128]{2,0,1:T(8,128)(2,1)} %param.5) | copy-start | bytes 331780
  7.2 277.4 %reduce-scatter.7.cloned.1.call-start = ((), (), s32[]{:S(2)}) async-start(), calls=%async_computation.2 | async-start | bytes 589824
  8.4 13.2 %collective-permute-start = (bf16[1,1,8,16,16]{3,4,2,1,0:T(8,128)(2,1)S(1)}, bf16[1,1,8,16,16]{3,4,2,1,0:T(8,128)(2,1)S(1)}, u32[]{:S(2)}, u32[]{:S(2)}) collective-permute-start(bf16[1,1,8,16,16]{3,4,2,1,0:T(8,128)(2,1)S(1)} %get-tuple-element.58), channel_id=1, source_target_pairs={{0,64},{64,128},{128,192},{192,256},{256,320},{320,384},{384,448},... | collective-permute-start | bytes 12296 | tf_op jit(solution)/shard_map/ppermute | solution.py:16
  12.6 8.9 collective-permute-start.1
  14.7 14.4 %collective-permute-start.9 = (bf16[1,1,8,16,16]{4,3,2,1,0:T(8,128)(2,1)S(1)}, bf16[1,1,8,16,16]{4,3,2,1,0:T(8,128)(2,1)S(1)}, u32[]{:S(2)}, u32[]{:S(2)}) collective-permute-start(bf16[1,1,8,16,16]{4,3,2,1,0:T(8,128)(2,1)S(1)} %get-tuple-element.56), channel_id=1, source_target_pairs={{64,0},{128,64},{192,128},{256,192},{320,256},{384,320},{448,384},... | collective-permute-start | bytes 12296 | tf_op jit(solution)/shard_map/ppermute | solution.py:17
  16.0 12.1 %collective-permute-start.8 = (bf16[1,1,8,16,16]{4,3,2,1,0:T(8,128)(2,1)S(1)}, bf16[1,1,8,16,16]{4,3,2,1,0:T(8,128)(2,1)S(1)}, u32[]{:S(2)}, u32[]{:S(2)}) collective-permute-start(bf16[1,1,8,16,16]{4,3,2,1,0:T(8,128)(2,1)S(1)} %get-tuple-element.57), channel_id=1, source_target_pairs={{0,64},{64,128},{128,192},{192,256},{256,320},{320,384},{384,448},... | collective-permute-start | bytes 12296 | tf_op jit(solution)/shard_map/ppermute | solution.py:16
  21.6 14.0 %collective-permute-start.2 = (bf16[1,10,1,16,16]{3,4,2,1,0:T(8,128)(2,1)S(1)}, bf16[1,10,1,16,16]{3,4,2,1,0:T(8,128)(2,1)S(1)}, u32[]{:S(2)}, u32[]{:S(2)}) collective-permute-start(bf16[1,10,1,16,16]{3,4,2,1,0:T(8,128)(2,1)S(1)} %get-tuple-element.52), channel_id=1, source_target_pairs={{0,8},{8,16},{16,24},{24,32},{32,40},{40,48},{48,56},{1,9},{9,17},... | collective-permute-start | bytes 15368 | tf_op jit(solution)/shard_map/ppermute | solution.py:16
  23.5 12.1 %collective-permute-start.3 = (bf16[1,10,1,16,16]{3,4,2,1,0:T(8,128)(2,1)S(1)}, bf16[1,10,1,16,16]{3,4,2,1,0:T(8,128)(2,1)S(1)}, u32[]{:S(2)}, u32[]{:S(2)}) collective-permute-start(bf16[1,10,1,16,16]{3,4,2,1,0:T(8,128)(2,1)S(1)} %get-tuple-element.53), channel_id=1, source_target_pairs={{8,0},{16,8},{24,16},{32,24},{40,32},{48,40},{56,48},{9,1},{17,9},... | collective-permute-start | bytes 15368 | tf_op jit(solution)/shard_map/ppermute | solution.py:17
  29.2 76.9 %collective-permute-start.10 = (bf16[1,10,1,16,16]{4,3,2,1,0:T(8,128)(2,1)S(1)}, bf16[1,10,1,16,16]{4,3,2,1,0:T(8,128)(2,1)S(1)}, u32[]{:S(2)}, u32[]{:S(2)}) collective-permute-start(bf16[1,10,1,16,16]{4,3,2,1,0:T(8,128)(2,1)S(1)} %get-tuple-element.48), channel_id=1, source_target_pairs={{0,8},{8,16},{16,24},{24,32},{32,40},{40,48},{48,56},{1,9},{9,17},... | collective-permute-start | bytes 15368 | tf_op jit(solution)/shard_map/ppermute | solution.py:16
  32.4 73.7 %collective-permute-start.11 = (bf16[1,10,1,16,16]{4,3,2,1,0:T(8,128)(2,1)S(1)}, bf16[1,10,1,16,16]{4,3,2,1,0:T(8,128)(2,1)S(1)}, u32[]{:S(2)}, u32[]{:S(2)}) collective-permute-start(bf16[1,10,1,16,16]{4,3,2,1,0:T(8,128)(2,1)S(1)} %get-tuple-element.49), channel_id=1, source_target_pairs={{8,0},{16,8},{24,16},{32,24},{40,32},{48,40},{56,48},{9,1},{17,9},... | collective-permute-start | bytes 15368 | tf_op jit(solution)/shard_map/ppermute | solution.py:17
  107.0 7.1 collective-permute-start.4
  111.3 7.4 collective-permute-start.5
  113.9 12.5 %copy-start.38 = (f32[8,8,8,3,16]{4,2,3,1,0:T(8,128)S(1)}, f32[8,8,8,3,16]{4,2,3,1,0:T(8,128)}, u32[]{:S(2)}) copy-start(f32[8,8,8,3,16]{4,2,3,1,0:T(8,128)} %get-tuple-element.41) | copy-start | bytes 294916
  119.5 84.6 %collective-permute-start.6 = (bf16[1,10,1,16,16]{4,2,3,1,0:T(2,128)(2,1)}, bf16[1,10,1,16,16]{4,2,3,1,0:T(2,128)(2,1)S(1)}, u32[]{:S(2)}, u32[]{:S(2)}) collective-permute-start(bf16[1,10,1,16,16]{4,2,3,1,0:T(2,128)(2,1)} %get-tuple-element.50), channel_id=1, source_target_pairs={{0,8},{8,16},{16,24},{24,32},{32,40},{40,48},{48,56},{1,9},{9,17},... | collective-permute-start | bytes 15368 | tf_op jit(solution)/shard_map/ppermute | solution.py:16
  121.4 82.7 %collective-permute-start.7 = (bf16[1,10,1,16,16]{4,2,3,1,0:T(2,128)(2,1)}, bf16[1,10,1,16,16]{4,2,3,1,0:T(2,128)(2,1)S(1)}, u32[]{:S(2)}, u32[]{:S(2)}) collective-permute-start(bf16[1,10,1,16,16]{4,2,3,1,0:T(2,128)(2,1)} %get-tuple-element.51), channel_id=1, source_target_pairs={{8,0},{16,8},{24,16},{32,24},{40,32},{48,40},{56,48},{9,1},{17,9},... | collective-permute-start | bytes 15368 | tf_op jit(solution)/shard_map/ppermute | solution.py:17
  143.5 730.4 %all-reduce.5.cloned.1.call-start = ((), (), s32[]{:S(2)}) async-start(), calls=%async_computation.4 | async-start | bytes 884736 | tf_op jit(solution)/shard_map/psum | solution.py:91
  205.0 37.4 %copy-start.2 = (bf16[1,8,8,16,16]{4,3,2,1,0:T(8,128)(2,1)S(1)}, bf16[1,8,8,16,16]{4,3,2,1,0:T(8,128)(2,1)}, u32[]{:S(2)}) copy-start(bf16[1,8,8,16,16]{4,3,2,1,0:T(8,128)(2,1)} %param.7) | copy-start | bytes 98308
  289.5 10.1 %copy-start.32 = (bf16[1,8,8,16,128]{4,2,3,1,0:T(8,128)(2,1)S(1)}, bf16[1,8,8,16,128]{4,2,3,1,0:T(8,128)(2,1)}, u32[]{:S(2)}) copy-start(bf16[1,8,8,16,128]{4,2,3,1,0:T(8,128)(2,1)} %copy.306) | copy-start | bytes 786436
  289.5 10.9 %copy-start.30 = (bf16[1,8,8,16,128]{4,2,3,1,0:T(8,128)(2,1)S(1)}, bf16[1,8,8,16,128]{4,2,3,1,0:T(8,128)(2,1)}, u32[]{:S(2)}) copy-start(bf16[1,8,8,16,128]{4,2,3,1,0:T(8,128)(2,1)} %copy.307) | copy-start | bytes 786436
  289.5 11.8 %copy-start.28 = (bf16[1,8,8,16,128]{4,2,3,1,0:T(8,128)(2,1)S(1)}, bf16[1,8,8,16,128]{4,2,3,1,0:T(8,128)(2,1)}, u32[]{:S(2)}) copy-start(bf16[1,8,8,16,128]{4,2,3,1,0:T(8,128)(2,1)} %copy.308) | copy-start | bytes 786436
  289.5 12.6 %copy-start.26 = (bf16[1,8,8,16,128]{4,2,3,1,0:T(8,128)(2,1)S(1)}, bf16[1,8,8,16,128]{4,2,3,1,0:T(8,128)(2,1)}, u32[]{:S(2)}) copy-start(bf16[1,8,8,16,128]{4,2,3,1,0:T(8,128)(2,1)} %copy.309) | copy-start | bytes 786436
  289.5 13.4 %copy-start.24 = (bf16[1,8,8,16,128]{4,2,3,1,0:T(8,128)(2,1)S(1)}, bf16[1,8,8,16,128]{4,2,3,1,0:T(8,128)(2,1)}, u32[]{:S(2)}) copy-start(bf16[1,8,8,16,128]{4,2,3,1,0:T(8,128)(2,1)} %copy.310) | copy-start | bytes 786436
  291.1 36.9 %copy-start.1 = (bf16[1,8,8,16,16]{4,2,3,1,0:T(8,128)(2,1)}, bf16[1,8,8,16,16]{4,2,3,1,0:T(8,128)(2,1)S(1)}, u32[]{:S(2)}) copy-start(bf16[1,8,8,16,16]{4,2,3,1,0:T(8,128)(2,1)S(1)} %fusion.141) | copy-start | bytes 98308
  291.1 12.7 %copy-start.22 = (bf16[1,8,8,16,128]{4,2,3,1,0:T(8,128)(2,1)S(1)}, bf16[1,8,8,16,128]{4,2,3,1,0:T(8,128)(2,1)}, u32[]{:S(2)}) copy-start(bf16[1,8,8,16,128]{4,2,3,1,0:T(8,128)(2,1)} %copy.311) | copy-start | bytes 786436
  291.1 13.5 %copy-start.20 = (bf16[1,8,8,16,128]{4,2,3,1,0:T(8,128)(2,1)S(1)}, bf16[1,8,8,16,128]{4,2,3,1,0:T(8,128)(2,1)}, u32[]{:S(2)}) copy-start(bf16[1,8,8,16,128]{4,2,3,1,0:T(8,128)(2,1)} %copy.312) | copy-start | bytes 786436
  291.2 29.3 %collective-permute-start.12 = (bf16[1,1,8,16,16]{4,2,3,1,0:T(8,128)(2,1)S(1)}, bf16[1,1,8,16,16]{4,2,3,1,0:T(8,128)(2,1)S(1)}, u32[]{:S(2)}, u32[]{:S(2)}) collective-permute-start(bf16[1,1,8,16,16]{4,2,3,1,0:T(8,128)(2,1)S(1)} %get-tuple-element.54), channel_id=1, source_target_pairs={{0,64},{64,128},{128,192},{192,256},{256,320},{320,384},{384,448},... | collective-permute-start | bytes 12296 | tf_op jit(solution)/shard_map/ppermute | solution.py:16
  296.4 9.0 copy-start.37
  296.4 24.0 %collective-permute-start.13 = (bf16[1,1,8,16,16]{4,2,3,1,0:T(8,128)(2,1)S(1)}, bf16[1,1,8,16,16]{4,2,3,1,0:T(8,128)(2,1)S(1)}, u32[]{:S(2)}, u32[]{:S(2)}) collective-permute-start(bf16[1,1,8,16,16]{4,2,3,1,0:T(8,128)(2,1)S(1)} %get-tuple-element.55), channel_id=1, source_target_pairs={{64,0},{128,64},{192,128},{256,192},{320,256},{384,320},{448,384},... | collective-permute-start | bytes 12296 | tf_op jit(solution)/shard_map/ppermute | solution.py:17
  314.6 13.4 %copy-start.12 = (bf16[1,8,8,16,128]{4,2,3,1,0:T(8,128)(2,1)S(1)}, bf16[1,8,8,16,128]{4,2,3,1,0:T(8,128)(2,1)}, u32[]{:S(2)}) copy-start(bf16[1,8,8,16,128]{4,2,3,1,0:T(8,128)(2,1)} %copy.331) | copy-start | bytes 786436
  321.3 7.6 collective-permute-start.14
  323.2 10.2 %collective-permute-start.15 = (bf16[1,10,1,16,16]{4,2,3,1,0:T(2,128)(2,1)}, bf16[1,10,1,16,16]{4,2,3,1,0:T(2,128)(2,1)}, u32[]{:S(2)}, u32[]{:S(2)}) collective-permute-start(bf16[1,10,1,16,16]{4,2,3,1,0:T(2,128)(2,1)} %get-tuple-element.47), channel_id=1, source_target_pairs={{8,0},{16,8},{24,16},{32,24},{40,32},{48,40},{56,48},{9,1},{17,9},... | collective-permute-start | bytes 15368 | tf_op jit(solution)/shard_map/ppermute | solution.py:17
  328.9 589.1 %reduce-scatter.9.cloned.1.call-start = ((), (), s32[]{:S(2)}) async-start(), calls=%async_computation.3 | async-start | bytes 589824
  (31 other events, 179.2 us)
Sparse Core Ops, SparseCore 0:
  143.6 46.6 reduce-scatter.6
  329.0 544.9 all-reduce.4
  876.7 41.1 reduce-scatter.8
where the time goes:
time: 938 us; the launch traced here: 928 us
  waiting for transfers between devices  563 us (60%)
  local copies, waits for them, and re-layouts  140 us (15%)
  blocking collectives  76.3 us (8%)
  matrix products  74.9 us (8%)
  starting transfers between devices  51.2 us (5%)
  between operations  14.9 us (2%)
    psum x1, waiting for transfers between devices, on_device(): first_grad = lax.psum(first_grad, ('gx', 'gy'))  512 us
    unnamed x131, local copies, waits for them, and re-layouts  109 us
    all_gather x2, blocking collectives, forward_layer(): full = lax.all_gather(pad_depth(rimmed), 'af', axis=4, tiled=True)  76.3 us
    dot_general x54, matrix products, filter_grad(): jnp.einsum('bxyzi,bxyzo->oi', piece, grad, preferred_element_type=jnp.flo...  65.4 us
    unnamed x5, waiting for transfers between devices  42.2 us
    ppermute x8, starting transfers between devices, with_halo(): before = lax.ppermute(last, axis, up)  28.3 us
    ppermute x8, starting transfers between devices, with_halo(): after = lax.ppermute(leading, axis, down)  22.8 us
    slice x2, local copies, waits for them, and re-layouts, filter_grad(): piece = full[:, first:first + sx, second:second + sy, third:third + sz, :]  22.1 us
  transfers between devices with their start and end apart: 19, of which 4 were waited for; matrix products, arithmetic and copies ran while one was open for 22% of the time, Pallas kernels for 0%

commit v1 on v0

v1 whole, which is shorter than its diff:
```python
import functools
import math

import jax
import jax.numpy as jnp
from jax import lax
from jax.experimental import pallas as pl
from jax.experimental.pallas import tpu as pltpu
from jax.sharding import PartitionSpec as P

BF = jnp.bfloat16
F32 = jnp.float32
T = 128
VMEM = pl.BlockSpec(memory_space=pltpu.VMEM)
SMEM = pl.BlockSpec(memory_space=pltpu.SMEM)
GY = ("yh", "co")
EXT = 25 * T
MID = 21 * T
OWN = 17 * T


def call(kernel, outs, scratch=(), scalars=False):
    def run(*args):
        return pl.pallas_call(
            kernel,
            out_shape=outs,
            in_specs=[SMEM if scalars and k == 0 else VMEM for k in range(len(args))],
            scratch_shapes=scratch,
            compiler_params=pltpu.CompilerParams(vmem_limit_bytes=48 << 20),
        )(*args)

    return run


def lanes(rows=16):
    return lax.broadcasted_iota(jnp.int32, (rows, T), 1)


def rolled(x, shift):
    size = x.shape[1]
    return pltpu.roll(x, shift % size, 1) if shift % size else x


def regroup(tiles):
    lane = lanes()
    tiles = list(tiles)
    for bit in (1, 2, 4):
        clear = (lane // (16 * bit)) % 2 == 0
        for u in range(8):
            if u & bit:
                continue
            first, second = tiles[u], tiles[u + bit]
            tiles[u] = jnp.where(clear, first, rolled(second, 16 * bit))
            tiles[u + bit] = jnp.where(clear, rolled(first, -16 * bit), second)
    return tiles


def pack_kernel(vol_hbm, grad_hbm, w1_hbm, w2_hbm, send, w1, w2, vol, grad, sems):
    copies = [
        pltpu.make_async_copy(source, target, sems.at[k])
        for k, (source, target) in enumerate(((vol_hbm, vol), (grad_hbm, grad), (w1_hbm, w1), (w2_hbm, w2)))
    ]
    for copy in copies:
        copy.start()
    for a, ref in enumerate((vol, grad)):
        copies[a].wait()
        for x in range(8):
            tile = ref[0, x].reshape(T, 16).astype(F32).T.astype(BF)
            for j in range(8):
                send[j, a * 8 + x] = tile
    for f, ref in enumerate((w1, w2)):
        copies[2 + f].wait()
        for m in range(4):
            tiles = [ref[8 * m + u].astype(F32) if 8 * m + u < 27 else jnp.zeros((16, T), F32) for u in range(8)]
            for j, tile in enumerate(regroup(tiles)):
                send[j, 16 + 4 * f + m] = tile.astype(BF)


def gathered(ref, k):
    return ref[:, k].reshape(T, T)


def face_kernel(block, low, high):
    for a in range(2):
        for p in range(2):
            low[2 * a + p] = gathered(block, 8 * a + p)
            high[2 * a + p] = gathered(block, 8 * a + 6 + p)


def edge_kernel(block, before, after, low, high):
    group = lanes(T) // 32
    for a in range(2):
        lows, highs = [None] * 3, [None] * 3
        for r in range(12):
            if r < 2:
                row = before[2 * a + r]
            elif r < 10:
                row = gathered(block, 8 * a + r - 2)
            else:
                row = after[2 * a + r - 10]
            row = row.astype(F32)
            for tiles, slot, off in ((lows, (r + 1) % 12, 0), (highs, r, 3)):
                q, k = slot // 4, slot % 4
                moved = rolled(row, 32 * k)
                tiles[q] = moved if tiles[q] is None else jnp.where(group == (k + off) % 4, moved, tiles[q])
        for q in range(3):
            low[a, q] = lows[q].astype(BF)
            high[a, q] = highs[q].astype(BF)


def product(left, right, out, width):
    for n in range(0, width, 640):
        size = min(640, width - n)
        out[:, n : n + size] = jnp.dot(left, right[:, n : n + size], preferred_element_type=F32)


def combine(prods, sign, width):
    depth = lax.broadcasted_iota(jnp.int32, (16, width), 1) % 16
    total = None
    for e in range(3):
        part = None
        for c in range(3):
            term = None
            for a in range(3):
                t = 9 * a + 3 * c + e
                start = 256 * a if sign > 0 else 256 * (2 - a)
                piece = prods[t * 16 : t * 16 + 16, start : start + width]
                term = piece if term is None else term + piece
            term = rolled(term, -sign * (c - 1) * 16)
            part = term if part is None else part + term
        step = sign * (e - 1)
        if step:
            part = rolled(part, -step)
            part = jnp.where(depth != (15 if step > 0 else 0), part, 0.0)
        total = part if total is None else total + part
    return total


def shifted(field, sign, out):
    depth = lax.broadcasted_iota(jnp.int32, (16, OWN), 1) % 16
    for c in range(3):
        moved = rolled(field, sign * (c - 1) * 16)
        for e in range(3):
            step = sign * (e - 1)
            piece = rolled(moved, step)
            if step:
                piece = jnp.where(depth != (0 if step > 0 else 15), piece, 0.0)
            k = (c * 3 + e) * 16
            out[k : k + 16, :] = piece.astype(BF)


def correlate(shifts, field, sign, out):
    for a in range(3):
        start = 2 * T + 256 * (a if sign > 0 else 2 - a)
        out[a * 144 : a * 144 + 144, :] = lax.dot_general(
            shifts[...],
            field[:, start : start + OWN],
            (((1,), (1,)), ((), ())),
            preferred_element_type=F32,
        )


def gathered_filter(ref, first):
    parts = [gathered(ref, first + m).astype(F32).T.astype(BF) for m in range(4)]
    return jnp.concatenate(parts, axis=0)[0:432]


def first_kernel(place, block, before, after, ybefore, yafter, w1rows, send, keep_out, give_out, vol, grad, prods1, prods2, shifts, sums, halves):
    for a, ref in enumerate((vol, grad)):
        def put(tile, value):
            ref[:, tile * T : tile * T + T] = value

        for r in range(12):
            if r < 2:
                value = before[2 * a + r]
            elif r < 10:
                value = gathered(block, 8 * a + r - 2)
            else:
                value = after[2 * a + r - 10]
            put(2 * r + 1, value)
        for q in range(3):
            late, early = yafter[a, q].astype(F32), ybefore[a, q].astype(F32)
            for k in range(4):
                value = rolled(jnp.where(lanes(T) // 32 == k, late, early), -32 * k).astype(BF)
                put(2 * (4 * q + k), value)
                if q + k == 0:
                    put(2 * 12, value)
    product(w1rows[...].reshape(432, T), vol, prods1, EXT)
    product(gathered_filter(block, 20), grad, prods2, EXT)

    lane = lax.broadcasted_iota(jnp.int32, (16, MID), 1)
    tile = lane // T
    low_x, high_x = place[0] == 0, place[0] == 7
    low_y, high_y = place[1] == 0, place[1] == 7
    halo = tile % 2 == 0
    early = halo & (lane % T >= 64)
    late = halo & (lane % T < 64)
    row = jnp.where(early, tile // 2 + 1, tile // 2 + jnp.where(halo, 0, 1))
    bad = (row <= 1) & low_x
    bad = bad | ((row >= 10) & high_x)
    bad = bad | (early & low_y) | (late & high_y)
    keep = jnp.logical_not(bad)

    pre = combine(prods1, 1, MID).astype(BF).astype(F32)
    sig = jax.nn.sigmoid(pre)
    hidden = jnp.where(keep, pre * sig, 0.0).astype(BF).astype(F32)
    back = combine(prods2, -1, MID)
    back = jnp.where(keep, back * sig * (1.0 + pre * (1.0 - sig)), 0.0).astype(BF).astype(F32)

    narrow = lanes()
    for a, field in enumerate((hidden, back)):
        for r in range(10):
            tile_r = field[:, (2 * r + 1) * T : (2 * r + 2) * T].astype(BF)
            for j in range(8):
                send[j, a * 13 + r] = tile_r
        for q in range(3):
            packed = jnp.zeros((16, T), F32)
            for k in range(4):
                h = 4 * q + k
                if h > 10:
                    continue
                here = ((narrow + 16) % T) // 32 == k
                packed = jnp.where(here, rolled(field[:, 2 * h * T : 2 * h * T + T], 32 * k), packed)
            packed = packed.astype(BF)
            for j in range(8):
                send[j, a * 13 + 10 + q] = packed

    mine = lax.broadcasted_iota(jnp.int32, (16, OWN), 1) // T % 2 == 1
    shifted(jnp.where(mine, back[:, 2 * T : 2 * T + OWN], 0.0), 1, shifts)
    correlate(shifts, vol, 1, sums)
    for n in range(32):
        for h in range(2):
            value = sums[n * 16 + 8 * h : n * 16 + 8 * h + 8, :] if n < 27 else jnp.zeros((8, T), F32)
            halves[h, n, 0:8, :] = value
    shifted(jnp.where(mine, hidden[:, 2 * T : 2 * T + OWN], 0.0), -1, shifts)
    correlate(shifts, grad, -1, sums)
    sums[432:512, :] = jnp.zeros((80, T), F32)
    for m in range(4):
        block = sums[T * m : T * m + T, :].T
        for k in range(8):
            for h in range(2):
                row = 16 * k + 8 * h
                halves[h, 4 * k + m, 8:16, :] = block[row : row + 8]
    keep_out[...] = halves[place[2]]
    give_out[...] = halves[1 - place[2]]


def second_kernel(block, middle, w2rows, out, vgrad, hid, pre, prods):
    for a, ref in enumerate((hid, pre)):
        for r in range(10):
            ref[:, (2 * r + 1) * T : (2 * r + 2) * T] = gathered(middle, a * 13 + r)
        for h in range(11):
            value = gathered(middle, a * 13 + 10 + h // 4)
            if h % 4:
                value = rolled(value.astype(F32), -32 * (h % 4)).astype(BF)
            ref[:, 2 * h * T : 2 * h * T + T] = value

    def store(ref, value):
        for x in range(8):
            tile = value[:, (2 * x + 1) * T : (2 * x + 2) * T]
            ref[0, x] = tile.T.astype(BF).reshape(8, 16, 16)

    product(w2rows[...].reshape(432, T), hid, prods, MID)
    store(out, combine(prods, 1, OWN))
    product(gathered_filter(block, 16), pre, prods, MID)
    store(vgrad, combine(prods, -1, OWN))


def pair_kernel(mine, other, out):
    out[...] = mine[...] + other[...]


def sum_kernel(factor, parts, out):
    total = parts[0]
    for k in range(1, 32):
        total = total + parts[k]
    out[...] = total * factor


def merge_kernel(place, mine, other, first, second):
    mine, other = mine[...], other[...]
    even = place[2] == 0
    low, high = jnp.where(even, mine, other), jnp.where(even, other, mine)
    first[...] = jnp.concatenate([low[0:8], high[0:8]], axis=0).astype(BF)
    second[...] = jnp.concatenate([low[8:16], high[8:16]], axis=0).astype(BF)


def spread_kernel(first, second, out):
    for j in range(32):
        out[j, 0:16, :] = first[...]
        out[j, 16:32, :] = second[...]


def last_kernel(parts, first, second):
    for t in range(27):
        first[t] = parts[t, 0:16, :].astype(F32)
    for m in range(4):
        tiles = regroup([parts[4 * k + m, 16:32, :].astype(F32) for k in range(8)])
        for u in range(8):
            if 8 * m + u < 27:
                second[8 * m + u] = tiles[u]


def shape(*dims, dtype=BF):
    return jax.ShapeDtypeStruct(dims, dtype)


def neighbours(low, high, axis):
    size = lax.axis_size(axis)
    up = [(i, i + 1) for i in range(size - 1)]
    before = lax.ppermute(high, axis, up)
    after = lax.ppermute(low, axis, [(j, i) for i, j in up])
    return before, after


def on_device(volume, first_filter, second_filter, out_grad):
    factor = 1.0 / math.sqrt(64 * 64 * 16)
    place = jnp.stack([lax.axis_index("gx"), lax.axis_index(GY), lax.axis_index("co")]).astype(jnp.int32)
    w1 = first_filter.transpose(1, 0, 2)
    w2 = second_filter.transpose(1, 0, 2)
    filters = shape(27, 16, T)
    send, w1, w2 = pl.pallas_call(
        pack_kernel,
        out_shape=(shape(8, 24, 16, T), filters, filters),
        in_specs=[pl.BlockSpec(memory_space=pltpu.HBM)] * 4,
        scratch_shapes=[pltpu.VMEM((1, 8, 8, 16, 16), BF)] * 2 + [pltpu.SemaphoreType.DMA((4,))],
    )(volume, out_grad, w1, w2)
    block = lax.all_to_all(send, "af", 0, 0)
    face = shape(4, T, T)
    low, high = call(face_kernel, (face, face))(block)
    before, after = neighbours(low, high, "gx")
    edge = shape(2, 3, T, T)
    low, high = call(edge_kernel, (edge, edge))(block, before, after)
    ybefore, yafter = neighbours(low, high, GY)
    middle, keep, give = call(
        first_kernel,
        (shape(8, 26, 16, T), shape(32, 16, T, dtype=F32), shape(32, 16, T, dtype=F32)),
        [
            pltpu.VMEM((T, EXT), BF),
            pltpu.VMEM((T, EXT), BF),
            pltpu.VMEM((432, EXT), F32),
            pltpu.VMEM((432, EXT), F32),
            pltpu.VMEM((144, OWN), BF),
            pltpu.VMEM((512, T), F32),
            pltpu.VMEM((2, 32, 16, T), F32),
        ],
        scalars=True,
    )(place, block, before, after, ybefore, yafter, w1)
    swap = [(0, 1), (1, 0)]
    other = lax.ppermute(give, "co", swap)
    parts = call(pair_kernel, shape(32, 16, T, dtype=F32))(keep, other)
    parts = lax.all_to_all(parts, ("gx", "yh"), 0, 0)
    parts, middle = lax.optimization_barrier((parts, middle))
    middle = lax.all_to_all(middle, "af", 0, 0)
    part = call(functools.partial(sum_kernel, factor), shape(16, T, dtype=F32))(parts)
    other = lax.ppermute(part, "co", swap)
    first, second = call(merge_kernel, (shape(16, T), shape(16, T)), scalars=True)(place, part, other)
    second = lax.ppermute(second, ("gx", "af"), [(a * 8 + k, k * 8 + a) for a in range(8) for k in range(8)])
    first, second, middle = lax.optimization_barrier((first, second, middle))
    parts = call(spread_kernel, shape(32, 32, T))(first, second)
    parts = lax.all_to_all(parts, ("gx", "yh"), 0, 0)
    output, volume_grad = call(
        second_kernel,
        (shape(1, 8, 8, 16, 16), shape(1, 8, 8, 16, 16)),
        [pltpu.VMEM((T, MID), BF), pltpu.VMEM((T, MID), BF), pltpu.VMEM((432, MID), F32)],
    )(block, middle, w2)
    wide = shape(27, 16, T, dtype=F32)
    first_grad, second_grad = call(last_kernel, (wide, wide))(parts)
    return output, volume_grad, first_grad.transpose(1, 0, 2), second_grad.transpose(1, 0, 2)


def solution(mesh):
    split = jax.sharding.Mesh(mesh.devices.reshape(8, 4, 2, 8), ("gx", "yh", "co", "af"))
    cells = P(None, "gx", GY, None, "af")
    weights = P("af", None, None)
    return jax.shard_map(
        on_device,
        mesh=split,
        in_specs=(cells, weights, weights, cells),
        out_specs=(cells, cells, weights, weights),
        check_vma=False,
    )
```

time: 938 us -> 123 us (0.13)
  the two profiles are of different devices: /device:TPU:16 before, /device:TPU:4 now
where the time goes in v1:
time: 123 us; the launch traced here: 122 us
  blocking collectives  43.6 us (35%)
  starting transfers between devices  35.5 us (29%)
  waiting for transfers between devices  28.8 us (23%)
  Pallas kernels  13.3 us (11%)
    all_to_all x1, blocking collectives, on_device(): parts = lax.all_to_all(parts, ('gx', 'yh'), 0, 0)  26.8 us
    all_to_all x1, blocking collectives, on_device(): block = lax.all_to_all(send, 'af', 0, 0)  16.8 us
    all_to_all x1, waiting for transfers between devices, on_device(): parts = lax.all_to_all(parts, ('gx', 'yh'), 0, 0)  10.9 us
    pallas_call x9, Pallas kernels, run(): pl.pallas_call(kernel, out_shape=outs, in_specs=[SMEM if scalars and k ==...  10.7 us
    ppermute x2, waiting for transfers between devices, neighbours(): after = lax.ppermute(low, axis, [(j, i) for i, j in up])  9.48 us
    ppermute x1, starting transfers between devices, on_device(): other = lax.ppermute(give, 'co', swap)  9.05 us
    all_to_all x1, starting transfers between devices, on_device(): parts = lax.all_to_all(parts, ('gx', 'yh'), 0, 0)  7.01 us
    all_to_all x1, starting transfers between devices, on_device(): middle = lax.all_to_all(middle, 'af', 0, 0)  6.07 us
  transfers between devices with their start and end apart: 9, of which 7 were waited for; matrix products, arithmetic and copies ran while one was open for 0% of the time, Pallas kernels for 3%

profile of v1, /device:TPU:4, one launch (start us, length us, event | category | flops | bytes accessed | tf_op | source)
XLA Modules:
  0.0 122.1 jit_solution(5987996490312853229)
XLA Ops:
  0.6 2.7 %shard_map.75 = (bf16[8,24,16,128]{3,2,1,0:T(8,128)(2,1)}, bf16[27,16,128]{2,1,0:T(8,128)(2,1)}, bf16[27,16,128]{2,1,0:T(8,128)(2,1)}) custom-call(bf16[1,8,8,16,16]{4,3,2,1,0:T(8,128)(2,1)} %vol_hbm.1, bf16[1,8,8,16,16]{4,3,2,1,0:T(8,128)(2,1)} %grad_hbm.1, bf16[27,16,128]{2,1,0:T(8,128)(2,1)} %bitcast.7, bf16[27,16,128]{2,1,0:T(8,128)(2,1)} %bitcast.8), custom_call_target="tpu_custom_call" | custom-call | tf_op jit(solution)/shard_map/pallas_call | solution.py:322
  3.3 16.8 %all_to_all.20.block = bf16[8,24,16,128]{3,2,1,0:T(8,128)(2,1)S(1)} all-to-all(bf16[8,24,16,128]{3,2,1,0:T(8,128)(2,1)} %get-tuple-element.25), channel_id=1, replica_groups=mesh['gx'=8,'yh'=4,'co'=2,'af'=8] {'af'}, dimensions={0} | all-to-all | bytes 1572864 | tf_op jit(solution)/shard_map/all_to_all | solution.py:328
  20.1 3.7 %collective-permute-start = (bf16[4,128,128]{2,1,0:T(8,128)(2,1)S(1)}, bf16[4,128,128]{2,1,0:T(8,128)(2,1)S(1)}, u32[]{:S(2)}, u32[]{:S(2)}) collective-permute-start(bf16[4,128,128]{2,1,0:T(8,128)(2,1)S(1)} %get-tuple-element.26), channel_id=1, source_target_pairs={{0,64},{64,128},{128,192},{192,256},{256,320},{320,384},{384,448},... | collective-permute-start | bytes 393224 | tf_op jit(solution)/shard_map/ppermute | solution.py:311
  23.7 1.3 %collective-permute-start.1 = (bf16[4,128,128]{2,1,0:T(8,128)(2,1)S(1)}, bf16[4,128,128]{2,1,0:T(8,128)(2,1)S(1)}, u32[]{:S(2)}, u32[]{:S(2)}) collective-permute-start(bf16[4,128,128]{2,1,0:T(8,128)(2,1)S(1)} %get-tuple-element.27), channel_id=1, source_target_pairs={{64,0},{128,64},{192,128},{256,192},{320,256},{384,320},{448,384},... | collective-permute-start | bytes 393224 | tf_op jit(solution)/shard_map/ppermute | solution.py:312
  25.0 1.2 collective-permute-done.before
  26.2 4.7 %collective-permute-done.1.after = bf16[4,128,128]{2,1,0:T(8,128)(2,1)S(1)} collective-permute-done((bf16[4,128,128]{2,1,0:T(8,128)(2,1)S(1)}, bf16[4,128,128]{2,1,0:T(8,128)(2,1)S(1)}, u32[]{:S(2)}, u32[]{:S(2)}) %collective-permute-start.1) | collective-permute-done | bytes 131104 | tf_op jit(solution)/shard_map/ppermute | solution.py:312
  31.0 0.0 copy-start
  31.0 0.4 shard_map.77
  31.4 1.3 %collective-permute-start.2 = (bf16[2,3,128,128]{3,2,1,0:T(8,128)(2,1)S(1)}, bf16[2,3,128,128]{3,2,1,0:T(8,128)(2,1)S(1)}, u32[]{:S(2)}, u32[]{:S(2)}) collective-permute-start(bf16[2,3,128,128]{3,2,1,0:T(8,128)(2,1)S(1)} %get-tuple-element.28), channel_id=1, source_target_pairs={{0,8},{8,16},{16,24},{24,32},{32,40},{40,48},{48,56},{1,9},{9,17},... | collective-permute-start | bytes 589832 | tf_op jit(solution)/shard_map/ppermute | solution.py:311
  32.7 1.3 %collective-permute-start.3 = (bf16[2,3,128,128]{3,2,1,0:T(8,128)(2,1)S(1)}, bf16[2,3,128,128]{3,2,1,0:T(8,128)(2,1)S(1)}, u32[]{:S(2)}, u32[]{:S(2)}) collective-permute-start(bf16[2,3,128,128]{3,2,1,0:T(8,128)(2,1)S(1)} %get-tuple-element.29), channel_id=1, source_target_pairs={{8,0},{16,8},{24,16},{32,24},{40,32},{48,40},{56,48},{9,1},{17,9},... | collective-permute-start | bytes 589832 | tf_op jit(solution)/shard_map/ppermute | solution.py:312
  34.0 0.1 pad_add_fusion.place
  34.0 0.0 collective-permute-done.2.ybefore
  34.1 4.8 %collective-permute-done.3.yafter = bf16[2,3,128,128]{3,2,1,0:T(8,128)(2,1)S(1)} collective-permute-done((bf16[2,3,128,128]{3,2,1,0:T(8,128)(2,1)S(1)}, bf16[2,3,128,128]{3,2,1,0:T(8,128)(2,1)S(1)}, u32[]{:S(2)}, u32[]{:S(2)}) %collective-permute-start.3) | collective-permute-done | bytes 196640 | tf_op jit(solution)/shard_map/ppermute | solution.py:312
  38.8 0.0 copy-done
  38.8 5.3 %shard_map.78 = (bf16[8,26,16,128]{3,2,1,0:T(8,128)(2,1)}, f32[32,16,128]{2,1,0:T(8,128)S(1)}, f32[32,16,128]{2,1,0:T(8,128)S(1)}) custom-call(s32[3]{0:T(128)S(1)} %pad_add_fusion.place, bf16[8,24,16,128]{3,2,1,0:T(8,128)(2,1)S(1)} %all_to_all.20.block, bf16[4,128,128]{2,1,0:T(8,128)(2,1)S(1)} %collective-permute-done.before, ...), custom_call_target="tpu_custom_call" | custom-call | tf_op jit(solution)/shard_map/pallas_call | solution.py:24
  44.1 9.1 %collective-permute-start.4 = (f32[32,16,128]{2,1,0:T(8,128)S(1)}, f32[32,16,128]{2,1,0:T(8,128)S(1)}, u32[]{:S(2)}, u32[]{:S(2)}) collective-permute-start(f32[32,16,128]{2,1,0:T(8,128)S(1)} %get-tuple-element.32), channel_id=1, source_target_pairs={{0,8},{8,0},{1,9},{9,1},{2,10},{10,2},{3,11},{11,3},{4,12},{12,4},... | collective-permute-start | bytes 786440 | tf_op jit(solution)/shard_map/ppermute | solution.py:350
  53.2 1.1 collective-permute-done.4.other
  54.3 26.8 %all_to_all.21.parts = f32[32,16,128]{2,1,0:T(8,128)S(1)} all-to-all(f32[32,16,128]{2,1,0:T(8,128)S(1)} %shard_map.79), channel_id=1, replica_groups=mesh['gx'=8,'yh'=4,'co'=2,'af'=8] {'gx','yh'}, dimensions={0} | all-to-all | bytes 524288 | tf_op jit(solution)/shard_map/all_to_all | solution.py:352
  81.2 6.1 %all-to-all-start.2 = ((bf16[8,26,16,128]{3,2,1,0:T(8,128)(2,1)}), bf16[8,26,16,128]{3,2,1,0:T(8,128)(2,1)S(1)}, u32[]{:S(2)}, u32[]{:S(2)}) async-start(bf16[8,26,16,128]{3,2,1,0:T(8,128)(2,1)} %get-tuple-element.37), calls=%async_computation.2 | async-start | bytes 1703936 | tf_op jit(solution)/shard_map/all_to_all | solution.py:354
  87.3 1.9 %collective-permute-start.5 = (f32[16,128]{1,0:T(8,128)S(1)}, f32[16,128]{1,0:T(8,128)S(1)}, u32[]{:S(2)}, u32[]{:S(2)}) collective-permute-start(f32[16,128]{1,0:T(8,128)S(1)} %shard_map.80.mine), channel_id=1, source_target_pairs={{0,8},{8,0},{1,9},{9,1},{2,10},{10,2},{3,11},{11,3},{4,12},{12,4},... | collective-permute-start | bytes 24584 | tf_op jit(solution)/shard_map/ppermute | solution.py:356
  89.2 1.1 collective-permute-done.5.other
  90.4 0.5 shard_map.81
  90.9 3.9 %collective-permute-start.6 = (bf16[16,128]{1,0:T(8,128)(2,1)S(1)}, bf16[16,128]{1,0:T(8,128)(2,1)S(1)}, u32[]{:S(2)}, u32[]{:S(2)}) collective-permute-start(bf16[16,128]{1,0:T(8,128)(2,1)S(1)} %get-tuple-element.36), channel_id=1, source_target_pairs={{0,0},{1,64},{2,128},{3,192},{4,256},{5,320},{6,384},{7,448},{64,1... | collective-permute-start | bytes 12296 | tf_op jit(solution)/shard_map/ppermute | solution.py:358
  94.8 4.9 %collective-permute-done.6.second = bf16[16,128]{1,0:T(8,128)(2,1)S(1)} collective-permute-done((bf16[16,128]{1,0:T(8,128)(2,1)S(1)}, bf16[16,128]{1,0:T(8,128)(2,1)S(1)}, u32[]{:S(2)}, u32[]{:S(2)}) %collective-permute-start.6) | collective-permute-done | bytes 4128 | tf_op jit(solution)/shard_map/ppermute | solution.py:358
  99.7 0.0 all-to-all-done.2.middle
  99.7 0.7 shard_map.83
  100.4 0.0 copy-start.1
  100.4 7.0 %all-to-all-start.3 = ((bf16[32,32,128]{2,1,0:T(8,128)(2,1)}), bf16[32,32,128]{2,1,0:T(8,128)(2,1)S(1)}, u32[]{:S(2)}, u32[]{:S(2)}) async-start(bf16[32,32,128]{2,1,0:T(8,128)(2,1)} %shard_map.83), calls=%async_computation.3 | async-start | bytes 524288 | tf_op jit(solution)/shard_map/all_to_all | solution.py:361
  107.5 0.0 copy-done.1
  107.5 2.7 %shard_map.82 = (bf16[1,8,8,16,16]{4,3,2,1,0:T(8,128)(2,1)}, bf16[1,8,8,16,16]{4,3,2,1,0:T(8,128)(2,1)}) custom-call(bf16[8,24,16,128]{3,2,1,0:T(8,128)(2,1)S(1)} %all_to_all.20.block, bf16[8,26,16,128]{3,2,1,0:T(8,128)(2,1)S(1)} %all-to-all-done.2.middle, bf16[27,16,128]{2,1,0:T(8,128)(2,1)S(1)} %copy-done.1), custom_call_target="tpu_custom_call" | custom-call | tf_op jit(solution)/shard_map/pallas_call | solution.py:24
  110.2 10.9 %all-to-all-done.3.parts = bf16[32,32,128]{2,1,0:T(8,128)(2,1)S(1)} async-done(((bf16[32,32,128]{2,1,0:T(8,128)(2,1)}), bf16[32,32,128]{2,1,0:T(8,128)(2,1)S(1)}, u32[]{:S(2)}, u32[]{:S(2)}) %all-to-all-start.3) | async-done | bytes 262176 | tf_op jit(solution)/shard_map/all_to_all | solution.py:361
  121.1 0.9 shard_map.84
  (3 shorter events, 0.1 us)
Async XLA Ops:
  20.1 6.2 %collective-permute-start = (bf16[4,128,128]{2,1,0:T(8,128)(2,1)S(1)}, bf16[4,128,128]{2,1,0:T(8,128)(2,1)S(1)}, u32[]{:S(2)}, u32[]{:S(2)}) collective-permute-start(bf16[4,128,128]{2,1,0:T(8,128)(2,1)S(1)} %get-tuple-element.26), channel_id=1, source_target_pairs={{0,64},{64,128},{128,192},{192,256},{256,320},{320,384},{384,448},... | collective-permute-start | bytes 393224 | tf_op jit(solution)/shard_map/ppermute | solution.py:311
  23.7 7.2 %collective-permute-start.1 = (bf16[4,128,128]{2,1,0:T(8,128)(2,1)S(1)}, bf16[4,128,128]{2,1,0:T(8,128)(2,1)S(1)}, u32[]{:S(2)}, u32[]{:S(2)}) collective-permute-start(bf16[4,128,128]{2,1,0:T(8,128)(2,1)S(1)} %get-tuple-element.27), channel_id=1, source_target_pairs={{64,0},{128,64},{192,128},{256,192},{320,256},{384,320},{448,384},... | collective-permute-start | bytes 393224 | tf_op jit(solution)/shard_map/ppermute | solution.py:312
  31.0 7.9 %copy-start = (bf16[27,16,128]{2,1,0:T(8,128)(2,1)S(1)}, bf16[27,16,128]{2,1,0:T(8,128)(2,1)}, u32[]{:S(2)}) copy-start(bf16[27,16,128]{2,1,0:T(8,128)(2,1)} %get-tuple-element.30.w1rows) | copy-start | bytes 331780
  31.4 2.7 %collective-permute-start.2 = (bf16[2,3,128,128]{3,2,1,0:T(8,128)(2,1)S(1)}, bf16[2,3,128,128]{3,2,1,0:T(8,128)(2,1)S(1)}, u32[]{:S(2)}, u32[]{:S(2)}) collective-permute-start(bf16[2,3,128,128]{3,2,1,0:T(8,128)(2,1)S(1)} %get-tuple-element.28), channel_id=1, source_target_pairs={{0,8},{8,16},{16,24},{24,32},{32,40},{40,48},{48,56},{1,9},{9,17},... | collective-permute-start | bytes 589832 | tf_op jit(solution)/shard_map/ppermute | solution.py:311
  32.7 6.1 %collective-permute-start.3 = (bf16[2,3,128,128]{3,2,1,0:T(8,128)(2,1)S(1)}, bf16[2,3,128,128]{3,2,1,0:T(8,128)(2,1)S(1)}, u32[]{:S(2)}, u32[]{:S(2)}) collective-permute-start(bf16[2,3,128,128]{3,2,1,0:T(8,128)(2,1)S(1)} %get-tuple-element.29), channel_id=1, source_target_pairs={{8,0},{16,8},{24,16},{32,24},{40,32},{48,40},{56,48},{9,1},{17,9},... | collective-permute-start | bytes 589832 | tf_op jit(solution)/shard_map/ppermute | solution.py:312
  44.1 10.2 %collective-permute-start.4 = (f32[32,16,128]{2,1,0:T(8,128)S(1)}, f32[32,16,128]{2,1,0:T(8,128)S(1)}, u32[]{:S(2)}, u32[]{:S(2)}) collective-permute-start(f32[32,16,128]{2,1,0:T(8,128)S(1)} %get-tuple-element.32), channel_id=1, source_target_pairs={{0,8},{8,0},{1,9},{9,1},{2,10},{10,2},{3,11},{11,3},{4,12},{12,4},... | collective-permute-start | bytes 786440 | tf_op jit(solution)/shard_map/ppermute | solution.py:350
  81.2 18.5 %all-to-all-start.2 = ((bf16[8,26,16,128]{3,2,1,0:T(8,128)(2,1)}), bf16[8,26,16,128]{3,2,1,0:T(8,128)(2,1)S(1)}, u32[]{:S(2)}, u32[]{:S(2)}) async-start(bf16[8,26,16,128]{3,2,1,0:T(8,128)(2,1)} %get-tuple-element.37), calls=%async_computation.2 | async-start | bytes 1703936 | tf_op jit(solution)/shard_map/all_to_all | solution.py:354
  87.3 3.1 %collective-permute-start.5 = (f32[16,128]{1,0:T(8,128)S(1)}, f32[16,128]{1,0:T(8,128)S(1)}, u32[]{:S(2)}, u32[]{:S(2)}) collective-permute-start(f32[16,128]{1,0:T(8,128)S(1)} %shard_map.80.mine), channel_id=1, source_target_pairs={{0,8},{8,0},{1,9},{9,1},{2,10},{10,2},{3,11},{11,3},{4,12},{12,4},... | collective-permute-start | bytes 24584 | tf_op jit(solution)/shard_map/ppermute | solution.py:356
  90.9 8.8 %collective-permute-start.6 = (bf16[16,128]{1,0:T(8,128)(2,1)S(1)}, bf16[16,128]{1,0:T(8,128)(2,1)S(1)}, u32[]{:S(2)}, u32[]{:S(2)}) collective-permute-start(bf16[16,128]{1,0:T(8,128)(2,1)S(1)} %get-tuple-element.36), channel_id=1, source_target_pairs={{0,0},{1,64},{2,128},{3,192},{4,256},{5,320},{6,384},{7,448},{64,1... | collective-permute-start | bytes 12296 | tf_op jit(solution)/shard_map/ppermute | solution.py:358
  100.4 7.0 %copy-start.1 = (bf16[27,16,128]{2,1,0:T(8,128)(2,1)S(1)}, bf16[27,16,128]{2,1,0:T(8,128)(2,1)}, u32[]{:S(2)}) copy-start(bf16[27,16,128]{2,1,0:T(8,128)(2,1)} %get-tuple-element.39.w2rows) | copy-start | bytes 331780
  100.4 20.7 %all-to-all-start.3 = ((bf16[32,32,128]{2,1,0:T(8,128)(2,1)}), bf16[32,32,128]{2,1,0:T(8,128)(2,1)S(1)}, u32[]{:S(2)}, u32[]{:S(2)}) async-start(bf16[32,32,128]{2,1,0:T(8,128)(2,1)} %shard_map.83), calls=%async_computation.3 | async-start | bytes 524288 | tf_op jit(solution)/shard_map/all_to_all | solution.py:361

commit v2 on v1

v2 whole, which is shorter than its diff:
```python
import functools
import math

import jax
import jax.numpy as jnp
from jax import lax
from jax.experimental import pallas as pl
from jax.experimental.pallas import tpu as pltpu
from jax.sharding import PartitionSpec as P

BF = jnp.bfloat16
F32 = jnp.float32
T = 128
VMEM = pl.BlockSpec(memory_space=pltpu.VMEM)
SMEM = pl.BlockSpec(memory_space=pltpu.SMEM)
HBM = pl.BlockSpec(memory_space=pltpu.HBM)
GY = ("yh", "co")
EXT = 25 * T
MID = 21 * T
OWN = 17 * T


def call(kernel, outs, scratch=(), scalars=False, hbm=False, limit=8):
    def run(*args):
        return pl.pallas_call(
            kernel,
            out_shape=outs,
            in_specs=[HBM if hbm else SMEM if scalars and k == 0 else VMEM for k in range(len(args))],
            scratch_shapes=scratch,
            compiler_params=pltpu.CompilerParams(vmem_limit_bytes=limit << 20),
        )(*args)

    return run


def lanes(rows=16):
    return lax.broadcasted_iota(jnp.int32, (rows, T), 1)


def rolled(x, shift):
    size = x.shape[1]
    return pltpu.roll(x, shift % size, 1) if shift % size else x


def regroup(tiles):
    lane = lanes()
    tiles = list(tiles)
    for bit in (1, 2, 4):
        clear = (lane // (16 * bit)) % 2 == 0
        for u in range(8):
            if u & bit:
                continue
            first, second = tiles[u], tiles[u + bit]
            tiles[u] = jnp.where(clear, first, rolled(second, 16 * bit))
            tiles[u + bit] = jnp.where(clear, rolled(first, -16 * bit), second)
    return tiles


def pack_kernel(vol_hbm, grad_hbm, own, low, vol, grad, sems):
    copies = [
        pltpu.make_async_copy(source, target, sems.at[k])
        for k, (source, target) in enumerate(((vol_hbm, vol), (grad_hbm, grad)))
    ]
    for copy in copies:
        copy.start()
    for a, ref in enumerate((vol, grad)):
        copies[a].wait()
        for x in range(8):
            tile = ref[0, x].reshape(T, 16).astype(F32).T.astype(BF)
            own[a, x] = tile
            if x < 4:
                low[a, x] = tile


def weight_kernel(w1_hbm, w2_hbm, out, w1, w2, sems):
    copies = [
        pltpu.make_async_copy(source, target, sems.at[k])
        for k, (source, target) in enumerate(((w1_hbm, w1), (w2_hbm, w2)))
    ]
    for copy in copies:
        copy.start()
    for f, ref in enumerate((w1, w2)):
        copies[f].wait()
        for m in range(4):
            tiles = [ref[8 * m + u].astype(F32) if 8 * m + u < 27 else jnp.zeros((16, T), F32) for u in range(8)]
            for j, tile in enumerate(regroup(tiles)):
                out[j, 4 * f + m] = tile.astype(BF)


def gathered(ref, k):
    return ref[:, k].reshape(T, T)


def row_of(own, nextx, a, r):
    return (own[a, r] if r < 8 else nextx[a, r - 8]).astype(F32)


def edge_kernel(own, nextx, out):
    first = lanes() < 64
    for a in range(2):
        for p in range(6):
            odd = rolled(row_of(own, nextx, a, 2 * p + 1), 64)
            out[a, p] = jnp.where(first, row_of(own, nextx, a, 2 * p), odd).astype(BF)


def send_kernel(own, nextx, nexty, weights, send, mine):
    lane = lanes()
    for a in range(2):
        rows = [row_of(own, nextx, a, r) for r in range(12)]
        nexts = []
        for r in range(12):
            tile = nexty[a, r // 2].astype(F32)
            nexts.append(rolled(tile, 64) if r % 2 else tile)
        tiles = [rolled(jnp.where(lane < 32, nexts[r], rows[r]), -32).astype(BF) for r in range(12)]
        packed = [None] * 6
        for h in range(13):
            q, k = h % 12 // 2, h % 2
            if h < 12:
                moved = rolled(rows[h], 64 * k - 32)
                here = lane // 32 == (3 if k == 0 else 1)
                packed[q] = moved if packed[q] is None else jnp.where(here, moved, packed[q])
            if h > 0:
                moved = rolled(nexts[h - 1], 64 * k - 32)
                here = lane // 32 == 2 * k
                packed[q] = moved if packed[q] is None else jnp.where(here, moved, packed[q])
        tiles += [tile.astype(BF) for tile in packed]
        for k, tile in enumerate(tiles):
            if a == 1 and 2 <= k < 10:
                mine[k - 2] = tile
            for j in range(8):
                send[j, a * 18 + k] = tile
    for k in range(8):
        for j in range(8):
            send[j, 36 + k] = weights[j, k]


def product(left, right, out, width):
    for n in range(0, width, 640):
        size = min(640, width - n)
        out[:, n : n + size] = jnp.dot(left, right[:, n : n + size], preferred_element_type=F32)


def cells(width, first):
    lane = lax.broadcasted_iota(jnp.int32, (16, width), 1)
    tile = lane // T + first
    own = tile % 2 == 1
    inner = lane % T
    row = jnp.where(own, tile // 2, jnp.where(inner < 64, tile // 2 - 1, tile // 2))
    column = jnp.where(own, inner // 16 + 2, jnp.where(inner < 64, inner // 16 + 10, inner // 16 - 6))
    return row, column, lane % 16


def combine(prods, sign, width, first, place):
    row, column, depth = cells(width, first)
    split_x, split_y = place[0] == 7, place[1] == 7
    inside = {
        1: jnp.where((row == 7) & split_x, 0.0, 1.0),
        -1: jnp.where((row == 8) & split_x, 0.0, 1.0),
    }
    apart = {1: (column == 7) & split_y, -1: (column == 8) & split_y}
    total = None
    for e in range(3):
        part = None
        for c in range(3):
            term = None
            for a in range(3):
                t = 9 * a + 3 * c + e
                start = 256 * a if sign > 0 else 256 * (2 - a)
                piece = prods[t * 16 : t * 16 + 16, start : start + width]
                if a != 1:
                    piece = piece * inside[sign * (a - 1)]
                term = piece if term is None else term + piece
            step = sign * (c - 1)
            if step:
                term = jnp.where(apart[step], 0.0, rolled(term, -step * 16))
            part = term if part is None else part + term
        step = sign * (e - 1)
        if step:
            part = rolled(part, -step)
            part = jnp.where(depth != (15 if step > 0 else 0), part, 0.0)
        total = part if total is None else total + part
    return total


def shifted(field, place, out):
    row, column, depth = cells(OWN, 4)
    split_x, split_y = place[0] == 7, place[1] == 7
    keep = {
        0: jnp.where((row == 8) & split_x, 0.0, 1.0).astype(BF),
        2: jnp.where((row == 7) & split_x, 0.0, 1.0).astype(BF),
    }
    for c in range(3):
        moved = rolled(field, (c - 1) * 16)
        if c != 1:
            moved = jnp.where((column == (8 if c == 2 else 7)) & split_y, 0.0, moved)
        for e in range(3):
            piece = rolled(moved, e - 1)
            if e != 1:
                piece = jnp.where(depth != (0 if e == 2 else 15), piece, 0.0)
            k = (c * 3 + e) * 16
            piece = piece.astype(BF)
            for a in range(3):
                out[a, k : k + 16, :] = piece if a == 1 else piece * keep[a]


def correlate(shifts, field, base, out):
    for a in range(3):
        start = base + 256 * a
        out[a * 144 : a * 144 + 144, :] = lax.dot_general(
            shifts[a],
            field[:, start : start + OWN],
            (((1,), (1,)), ((), ())),
            preferred_element_type=F32,
        )


def gathered_filter(ref, first):
    parts = [gathered(ref, first + m).astype(F32).T.astype(BF) for m in range(4)]
    return jnp.concatenate(parts, axis=0)[0:432]


def first_kernel(place, block, w1rows, send, sums, vol, grad, prods1, prods2, shifts):
    for a, ref in enumerate((vol, grad)):
        def put(tile, value):
            ref[:, tile * T : tile * T + T] = value

        for r in range(12):
            put(2 * r + 1, gathered(block, a * 18 + r))
        for q in range(6):
            packed = gathered(block, a * 18 + 12 + q)
            for k in range(2):
                value = rolled(packed.astype(F32), -64).astype(BF) if k else packed
                put(2 * (2 * q + k), value)
                if q + k == 0:
                    put(2 * 12, value)
    product(w1rows[...].reshape(432, T), vol, prods1, EXT)
    product(gathered_filter(block, 40), grad, prods2, EXT)

    pre = combine(prods1, 1, MID, 2, place).astype(BF).astype(F32)
    sig = jax.nn.sigmoid(pre)
    hidden = (pre * sig).astype(BF).astype(F32)
    back = combine(prods2, -1, MID, 2, place)
    back = (back * sig * (1.0 + pre * (1.0 - sig))).astype(BF).astype(F32)

    narrow = lanes()
    for a, field in enumerate((hidden, back)):
        for r in range(10):
            tile_r = field[:, (2 * r + 1) * T : (2 * r + 2) * T].astype(BF)
            for j in range(8):
                send[j, a * 13 + r] = tile_r
        for q in range(3):
            packed = jnp.zeros((16, T), F32)
            for k in range(4):
                h = 4 * q + k
                if h > 10:
                    continue
                here = ((narrow + 16) % T) // 32 == k
                packed = jnp.where(here, rolled(field[:, 2 * h * T : 2 * h * T + T], 32 * k), packed)
            packed = packed.astype(BF)
            for j in range(8):
                send[j, a * 13 + 10 + q] = packed

    mine = lax.broadcasted_iota(jnp.int32, (16, OWN), 1) // T % 2 == 1
    shifted(jnp.where(mine, back[:, 2 * T : 2 * T + OWN], 0.0), place, shifts)
    correlate(shifts, vol, 2 * T, sums)


def spread(middle, a, ref):
    for r in range(10):
        ref[:, (2 * r + 1) * T : (2 * r + 2) * T] = gathered(middle, a * 13 + r)
    for h in range(11):
        value = gathered(middle, a * 13 + 10 + h // 4)
        if h % 4:
            value = rolled(value.astype(F32), -32 * (h % 4)).astype(BF)
        ref[:, 2 * h * T : 2 * h * T + T] = value


def grad_kernel(place, own, middle, sums1, hid, send, field, shifts, sums2):
    spread(middle, 0, hid)
    field[...] = jnp.zeros((16, OWN), F32)
    for x in range(8):
        field[:, (2 * x + 1) * T : (2 * x + 2) * T] = own[x].astype(F32)
    shifted(field[...], place, shifts)
    correlate(shifts, hid, 0, sums2)
    rows = jnp.concatenate([sums1[...], sums2[...], jnp.zeros((32, T), F32)], axis=0)
    send[...] = rows.astype(BF).reshape(8, 112, T)


def second_kernel(place, block, middle, hid, w2rows, keep, give, pre, prods):
    spread(middle, 1, pre)

    def store(which, value):
        for x in range(8):
            tile = value[:, (2 * x + 1) * T : (2 * x + 2) * T].astype(BF)
            if x < 6:
                keep[which, x] = tile
            else:
                give[which, x - 6] = tile

    product(w2rows[...].reshape(432, T), hid, prods, MID)
    store(0, combine(prods, 1, OWN, 4, place))
    product(gathered_filter(block, 36), pre, prods, MID)
    store(1, combine(prods, -1, OWN, 4, place))


def back_kernel(keep, taken, rows, give):
    lane = lanes()
    for a in range(2):
        tiles = [taken[a, 0], taken[a, 1]] + [keep[a, x] for x in range(6)]
        for x, tile in enumerate(tiles):
            rows[a, x] = tile
        for q in range(2):
            packed = tiles[4 * q + 3].astype(F32)
            for k in range(3):
                moved = rolled(tiles[4 * q + k].astype(F32), 32 * k + 32)
                packed = jnp.where(lane // 32 == k, moved, packed)
            give[a, q] = packed.astype(BF)


def out_kernel(rows, taken, out, vgrad):
    lane = lanes()
    for a, ref in enumerate((out, vgrad)):
        for x in range(8):
            first = rolled(taken[a, x // 4].astype(F32), -32 * (x % 4))
            tile = jnp.where(lane < 32, first, rolled(rows[a, x].astype(F32), 32))
            ref[0, x] = tile.T.astype(BF).reshape(8, 16, 16)


def sum_kernel(factor, copies, parts, out):
    total = parts[0].astype(F32)
    for k in range(1, parts.shape[0]):
        total = total + parts[k].astype(F32)
    total = total * factor
    if copies == 1:
        out[...] = total
    for j in range(copies if copies > 1 else 0):
        out[j] = total.astype(BF)


def pair_kernel(mine, other, out):
    total = (mine[...] + other[...]).astype(BF)
    for j in range(4):
        out[j] = total


def last_kernel(parts, first, second):
    rows = parts[...].reshape(896, T).astype(F32)
    first[...] = rows[0:432].reshape(27, 16, T)
    second[...] = rows[432:864].reshape(27, 16, T)


def shape(*dims, dtype=BF):
    return jax.ShapeDtypeStruct(dims, dtype)


def cyclic(x, axis, step):
    size = lax.axis_size(axis)
    return lax.ppermute(x, axis, [(i, (i + step) % size) for i in range(size)])


def on_device(volume, first_filter, second_filter, out_grad):
    factor = 1.0 / math.sqrt(64 * 64 * 16)
    place = jnp.stack([lax.axis_index("gx"), lax.axis_index(GY)]).astype(jnp.int32)
    w1 = first_filter.transpose(1, 0, 2)
    w2 = second_filter.transpose(1, 0, 2)
    two = shape(2, 8, 16, T)
    own, low = call(
        pack_kernel,
        (two, shape(2, 4, 16, T)),
        [pltpu.VMEM((1, 8, 8, 16, 16), BF)] * 2 + [pltpu.SemaphoreType.DMA((2,))],
        hbm=True,
    )(volume, out_grad)
    nextx = cyclic(low, "gx", -1)
    nexty = cyclic(call(edge_kernel, shape(2, 6, 16, T))(own, nextx), GY, -1)
    pieces = call(
        weight_kernel,
        shape(8, 8, 16, T),
        [pltpu.VMEM((27, 16, T), BF)] * 2 + [pltpu.SemaphoreType.DMA((2,))],
        hbm=True,
    )(w1, w2)
    send, mine = call(send_kernel, (shape(8, 44, 16, T), shape(8, 16, T)))(own, nextx, nexty, pieces)
    block = lax.all_to_all(send, "af", 0, 0)
    middle, sums = call(
        first_kernel,
        (shape(8, 26, 16, T), shape(432, T, dtype=F32)),
        [
            pltpu.VMEM((T, EXT), BF),
            pltpu.VMEM((T, EXT), BF),
            pltpu.VMEM((432, EXT), F32),
            pltpu.VMEM((432, EXT), F32),
            pltpu.VMEM((3, 144, OWN), BF),
        ],
        scalars=True,
        limit=28,
    )(place, block, w1)
    middle = lax.all_to_all(middle, "af", 0, 0)
    many = shape(8, 112, T)
    hid, parts = call(
        grad_kernel,
        (shape(T, MID), many),
        [pltpu.VMEM((16, OWN), F32), pltpu.VMEM((3, 144, OWN), BF), pltpu.VMEM((432, T), F32)],
        scalars=True,
        limit=16,
    )(place, mine, middle, sums)
    keep, give = call(
        second_kernel,
        (shape(2, 6, 16, T), shape(2, 2, 16, T)),
        [pltpu.VMEM((T, MID), BF), pltpu.VMEM((432, MID), F32)],
        scalars=True,
        limit=20,
    )(place, block, middle, hid, w2)
    parts = lax.all_to_all(parts, "gx", 0, 0)
    parts, keep, give = lax.optimization_barrier((parts, keep, give))
    part = call(functools.partial(sum_kernel, 1.0, 1), shape(112, T, dtype=F32))(parts)
    other = lax.ppermute(part, "co", [(0, 1), (1, 0)])
    parts = call(pair_kernel, shape(4, 112, T))(part, other)
    rows, give = call(back_kernel, (two, shape(2, 2, 16, T)))(keep, cyclic(give, "gx", 1))
    parts = lax.all_to_all(parts, "yh", 0, 0)
    parts, rows, give = lax.optimization_barrier((parts, rows, give))
    parts = call(functools.partial(sum_kernel, factor, 8), many)(parts)
    output, volume_grad = call(out_kernel, (shape(1, 8, 8, 16, 16), shape(1, 8, 8, 16, 16)))(rows, cyclic(give, GY, 1))
    parts = lax.all_to_all(parts, "gx", 0, 0)
    wide = shape(27, 16, T, dtype=F32)
    first_grad, second_grad = call(last_kernel, (wide, wide))(parts)
    return output, volume_grad, first_grad.transpose(1, 0, 2), second_grad.transpose(1, 0, 2)


def solution(mesh):
    split = jax.sharding.Mesh(mesh.devices.reshape(8, 4, 2, 8), ("gx", "yh", "co", "af"))
    cells = P(None, "gx", GY, None, "af")
    weights = P("af", None, None)
    return jax.shard_map(
        on_device,
        mesh=split,
        in_specs=(cells, weights, weights, cells),
        out_specs=(cells, cells, weights, weights),
        check_vma=False,
    )
```

time: 123 us -> 119 us (0.967)
  the two profiles are of different devices: /device:TPU:4 before, /device:TPU:2 now
where the time goes in v2:
time: 119 us
  waiting for transfers between devices  42 us (35%)
  starting transfers between devices  40.5 us (34%)
  blocking collectives  17.3 us (15%)
  Pallas kernels  14.3 us (12%)
  local copies, waits for them, and re-layouts  3.69 us (3%)
    ppermute x4, starting transfers between devices, cyclic(): return lax.ppermute(x, axis, [(i, (i + step) % size) for i in range(size)])  20.1 us
    all_to_all x1, waiting for transfers between devices, on_device(): block = lax.all_to_all(send, 'af', 0, 0)  17.8 us
    all_to_all x1, blocking collectives, on_device(): middle = lax.all_to_all(middle, 'af', 0, 0)  17.3 us
    pallas_call x13, Pallas kernels, run(): pl.pallas_call(kernel, out_shape=outs, in_specs=[HBM if hbm else SMEM if...  14.3 us
    ppermute x4, waiting for transfers between devices, cyclic(): return lax.ppermute(x, axis, [(i, (i + step) % size) for i in range(size)])  11.4 us
    all_to_all x2, waiting for transfers between devices, on_device(): parts = lax.all_to_all(parts, 'gx', 0, 0)  9.36 us
    all_to_all x2, starting transfers between devices, on_device(): parts = lax.all_to_all(parts, 'gx', 0, 0)  8.21 us
    all_to_all x1, starting transfers between devices, on_device(): parts = lax.all_to_all(parts, 'yh', 0, 0)  5.24 us
  transfers between devices with their start and end apart: 9, of which 8 were waited for; matrix products, arithmetic and copies ran while one was open for 0% of the time, Pallas kernels for 4%

profile of v2, /device:TPU:2, one launch (start us, length us, event | category | flops | bytes accessed | tf_op | source)
XLA Modules:
  0.0 118.6 jit_solution(1439727593430963203)
XLA Ops:
  0.6 0.9 copy-done.4
  1.6 0.9 copy-done.5
  2.5 0.3 shard_map.75
  2.8 10.9 %collective-permute-start = (bf16[2,4,16,128]{3,2,1,0:T(8,128)(2,1)S(1)}, bf16[2,4,16,128]{3,2,1,0:T(8,128)(2,1)S(1)}, u32[]{:S(2)}, u32[]{:S(2)}) collective-permute-start(bf16[2,4,16,128]{3,2,1,0:T(8,128)(2,1)S(1)} %get-tuple-element.27), channel_id=1, source_target_pairs={{0,448},{64,0},{128,64},{192,128},{256,192},{320,256},{384,320},{4... | collective-permute-start | bytes 98312 | tf_op jit(solution)/shard_map/ppermute | solution.py:358
  13.8 1.6 %collective-permute-done.nextx = bf16[2,4,16,128]{3,2,1,0:T(8,128)(2,1)S(1)} collective-permute-done((bf16[2,4,16,128]{3,2,1,0:T(8,128)(2,1)S(1)}, bf16[2,4,16,128]{3,2,1,0:T(8,128)(2,1)S(1)}, u32[]{:S(2)}, u32[]{:S(2)}) %collective-permute-start) | collective-permute-done | bytes 32800 | tf_op jit(solution)/shard_map/ppermute | solution.py:358
  15.4 4.7 %collective-permute-start.1 = (bf16[2,6,16,128]{3,2,1,0:T(8,128)(2,1)S(1)}, bf16[2,6,16,128]{3,2,1,0:T(8,128)(2,1)S(1)}, u32[]{:S(2)}, u32[]{:S(2)}) collective-permute-start(bf16[2,6,16,128]{3,2,1,0:T(8,128)(2,1)S(1)} %shard_map.76), channel_id=1, source_target_pairs={{0,56},{8,0},{16,8},{24,16},{32,24},{40,32},{48,40},{56,48},{1,57}... | collective-permute-start | bytes 147464 | tf_op jit(solution)/shard_map/ppermute | solution.py:358
  20.2 0.9 copy-done
  21.1 0.9 copy-done.2
  22.0 0.8 shard_map.77.weights
  22.8 1.4 %shard_map.78 = (bf16[8,44,16,128]{3,2,1,0:T(8,128)(2,1)}, bf16[8,16,128]{2,1,0:T(8,128)(2,1)S(1)}) custom-call(bf16[2,8,16,128]{3,2,1,0:T(8,128)(2,1)S(1)} %get-tuple-element.26.own, bf16[2,4,16,128]{3,2,1,0:T(8,128)(2,1)S(1)} %collective-permute-done.nextx, bf16[2,6,16,128]{3,2,1,0:T(8,128)(2,1)S(1)} %collective-permute-done.1.nexty, ...), custom_call_target="tpu_custom_call" | custom-call | tf_op jit(solution)/shard_map/pallas_call | solution.py:25
  24.2 5.1 %all-to-all-start = ((bf16[8,44,16,128]{3,2,1,0:T(8,128)(2,1)}), bf16[8,44,16,128]{3,2,1,0:T(8,128)(2,1)S(1)}, u32[]{:S(2)}, u32[]{:S(2)}) async-start(bf16[8,44,16,128]{3,2,1,0:T(8,128)(2,1)} %get-tuple-element.29), calls=%async_computation | async-start | bytes 2883584 | tf_op jit(solution)/shard_map/all_to_all | solution.py:382
  29.3 17.8 %all-to-all-done.block = bf16[8,44,16,128]{3,2,1,0:T(8,128)(2,1)S(1)} async-done(((bf16[8,44,16,128]{3,2,1,0:T(8,128)(2,1)}), bf16[8,44,16,128]{3,2,1,0:T(8,128)(2,1)S(1)}, u32[]{:S(2)}, u32[]{:S(2)}) %all-to-all-start) | async-done | bytes 1441824 | tf_op jit(solution)/shard_map/all_to_all | solution.py:382
  47.2 3.8 %shard_map.79 = (bf16[8,26,16,128]{3,2,1,0:T(8,128)(2,1)S(1)}, f32[432,128]{1,0:T(8,128)S(1)}) custom-call(s32[2]{0:T(128)S(1)} %pad_add_fusion.place, bf16[8,44,16,128]{3,2,1,0:T(8,128)(2,1)S(1)} %all-to-all-done.block, bf16[27,16,128]{2,1,0:T(8,128)(2,1)S(1)} %bitcast.7), custom_call_target="tpu_custom_call" | custom-call | tf_op jit(solution)/shard_map/pallas_call | solution.py:25
  51.0 17.3 %all_to_all.25.middle = bf16[8,26,16,128]{3,2,1,0:T(8,128)(2,1)S(1)} all-to-all(bf16[8,26,16,128]{3,2,1,0:T(8,128)(2,1)S(1)} %get-tuple-element.30), channel_id=1, replica_groups=mesh['gx'=8,'yh'=4,'co'=2,'af'=8] {'af'}, dimensions={0} | all-to-all | bytes 1703936 | tf_op jit(solution)/shard_map/all_to_all | solution.py:396
  68.3 2.2 %shard_map.80 = (bf16[128,2688]{1,0:T(8,128)(2,1)S(1)}, bf16[8,112,128]{2,1,0:T(8,128)(2,1)}) custom-call(s32[2]{0:T(128)S(1)} %pad_add_fusion.place, bf16[8,16,128]{2,1,0:T(8,128)(2,1)S(1)} %get-tuple-element.28.own, bf16[8,26,16,128]{3,2,1,0:T(8,128)(2,1)S(1)} %all_to_all.25.middle, f32[432,128]{1,0:T(8,128)S(1)} %get-tuple-element.31.sums1), custom_call_target="tpu_custom_call" | custom-call | tf_op jit(solution)/shard_map/pallas_call | solution.py:25
  70.5 4.8 %all-to-all-start.2 = ((bf16[8,112,128]{2,1,0:T(8,128)(2,1)}), bf16[8,112,128]{2,1,0:T(8,128)(2,1)S(1)}, u32[]{:S(2)}, u32[]{:S(2)}) async-start(bf16[8,112,128]{2,1,0:T(8,128)(2,1)} %get-tuple-element.32), calls=%async_computation.2 | async-start | bytes 458752 | tf_op jit(solution)/shard_map/all_to_all | solution.py:412
  75.3 2.3 %shard_map.81 = (bf16[2,6,16,128]{3,2,1,0:T(8,128)(2,1)S(1)}, bf16[2,2,16,128]{3,2,1,0:T(8,128)(2,1)S(1)}) custom-call(s32[2]{0:T(128)S(1)} %pad_add_fusion.place, bf16[8,44,16,128]{3,2,1,0:T(8,128)(2,1)S(1)} %all-to-all-done.block, bf16[8,26,16,128]{3,2,1,0:T(8,128)(2,1)S(1)} %all_to_all.25.middle, bf16[128,2688]{1,0:T(8,128)(2,1)S(1)} %get-tuple-element.33.hid, ...), custom_call_target="tpu_custom_call" | custom-call | tf_op jit(solution)/shard_map/pallas_call | solution.py:25
  77.6 7.9 %all-to-all-done.2.parts = bf16[8,112,128]{2,1,0:T(8,128)(2,1)S(1)} async-done(((bf16[8,112,128]{2,1,0:T(8,128)(2,1)}), bf16[8,112,128]{2,1,0:T(8,128)(2,1)S(1)}, u32[]{:S(2)}, u32[]{:S(2)}) %all-to-all-start.2) | async-done | bytes 229408 | tf_op jit(solution)/shard_map/all_to_all | solution.py:412
  85.5 1.9 %collective-permute-start.2 = (f32[112,128]{1,0:T(8,128)S(1)}, f32[112,128]{1,0:T(8,128)S(1)}, u32[]{:S(2)}, u32[]{:S(2)}) collective-permute-start(f32[112,128]{1,0:T(8,128)S(1)} %shard_map.82.mine), channel_id=1, source_target_pairs={{0,8},{8,0},{1,9},{9,1},{2,10},{10,2},{3,11},{11,3},{4,12},{12,4},... | collective-permute-start | bytes 172040 | tf_op jit(solution)/shard_map/ppermute | solution.py:415
  87.4 1.2 %collective-permute-done.2.other = f32[112,128]{1,0:T(8,128)S(1)} collective-permute-done((f32[112,128]{1,0:T(8,128)S(1)}, f32[112,128]{1,0:T(8,128)S(1)}, u32[]{:S(2)}, u32[]{:S(2)}) %collective-permute-start.2) | collective-permute-done | bytes 57376 | tf_op jit(solution)/shard_map/ppermute | solution.py:415
  88.6 0.7 shard_map.83
  89.3 5.2 %all-to-all-start.3 = ((bf16[4,112,128]{2,1,0:T(8,128)(2,1)}), bf16[4,112,128]{2,1,0:T(8,128)(2,1)S(1)}, u32[]{:S(2)}, u32[]{:S(2)}) async-start(bf16[4,112,128]{2,1,0:T(8,128)(2,1)} %shard_map.83), calls=%async_computation.3 | async-start | bytes 229376 | tf_op jit(solution)/shard_map/all_to_all | solution.py:418
  94.5 2.5 %collective-permute-start.3 = (bf16[2,2,16,128]{3,2,1,0:T(8,128)(2,1)S(1)}, bf16[2,2,16,128]{3,2,1,0:T(8,128)(2,1)S(1)}, u32[]{:S(2)}, u32[]{:S(2)}) collective-permute-start(bf16[2,2,16,128]{3,2,1,0:T(8,128)(2,1)S(1)} %get-tuple-element.38), channel_id=1, source_target_pairs={{0,64},{64,128},{128,192},{192,256},{256,320},{320,384},{384,448},... | collective-permute-start | bytes 49160 | tf_op jit(solution)/shard_map/ppermute | solution.py:358
  97.0 4.4 %collective-permute-done.3.taken = bf16[2,2,16,128]{3,2,1,0:T(8,128)(2,1)S(1)} collective-permute-done((bf16[2,2,16,128]{3,2,1,0:T(8,128)(2,1)S(1)}, bf16[2,2,16,128]{3,2,1,0:T(8,128)(2,1)S(1)}, u32[]{:S(2)}, u32[]{:S(2)}) %collective-permute-start.3) | collective-permute-done | bytes 16416 | tf_op jit(solution)/shard_map/ppermute | solution.py:358
  101.4 2.2 %all-to-all-done.3.parts = bf16[4,112,128]{2,1,0:T(8,128)(2,1)S(1)} async-done(((bf16[4,112,128]{2,1,0:T(8,128)(2,1)}), bf16[4,112,128]{2,1,0:T(8,128)(2,1)S(1)}, u32[]{:S(2)}, u32[]{:S(2)}) %all-to-all-start.3) | async-done | bytes 114720 | tf_op jit(solution)/shard_map/all_to_all | solution.py:418
  103.7 0.7 shard_map.86
  104.4 3.4 %all-to-all-start.4 = ((bf16[8,112,128]{2,1,0:T(8,128)(2,1)}), bf16[8,112,128]{2,1,0:T(8,128)(2,1)S(1)}, u32[]{:S(2)}, u32[]{:S(2)}) async-start(bf16[8,112,128]{2,1,0:T(8,128)(2,1)} %shard_map.86), calls=%async_computation.4 | async-start | bytes 458752 | tf_op jit(solution)/shard_map/all_to_all | solution.py:422
  107.8 1.9 %collective-permute-start.4 = (bf16[2,2,16,128]{3,2,1,0:T(8,128)(2,1)S(1)}, bf16[2,2,16,128]{3,2,1,0:T(8,128)(2,1)S(1)}, u32[]{:S(2)}, u32[]{:S(2)}) collective-permute-start(bf16[2,2,16,128]{3,2,1,0:T(8,128)(2,1)S(1)} %get-tuple-element.42), channel_id=1, source_target_pairs={{0,8},{8,16},{16,24},{24,32},{32,40},{40,48},{48,56},{56,0},{1,9},... | collective-permute-start | bytes 49160 | tf_op jit(solution)/shard_map/ppermute | solution.py:358
  109.7 5.4 %collective-permute-done.4.taken = bf16[2,2,16,128]{3,2,1,0:T(8,128)(2,1)S(1)} collective-permute-done((bf16[2,2,16,128]{3,2,1,0:T(8,128)(2,1)S(1)}, bf16[2,2,16,128]{3,2,1,0:T(8,128)(2,1)S(1)}, u32[]{:S(2)}, u32[]{:S(2)}) %collective-permute-start.4) | collective-permute-done | bytes 16416 | tf_op jit(solution)/shard_map/ppermute | solution.py:358
  115.1 1.2 %shard_map.85 = (bf16[1,8,8,16,16]{4,3,2,1,0:T(8,128)(2,1)}, bf16[1,8,8,16,16]{4,3,2,1,0:T(8,128)(2,1)}) custom-call(bf16[2,8,16,128]{3,2,1,0:T(8,128)(2,1)S(1)} %get-tuple-element.41.rows, bf16[2,2,16,128]{3,2,1,0:T(8,128)(2,1)S(1)} %collective-permute-done.4.taken), custom_call_target="tpu_custom_call" | custom-call | tf_op jit(solution)/shard_map/pallas_call | solution.py:25
  116.3 1.5 %all-to-all-done.4.parts = bf16[8,112,128]{2,1,0:T(8,128)(2,1)S(1)} async-done(((bf16[8,112,128]{2,1,0:T(8,128)(2,1)}), bf16[8,112,128]{2,1,0:T(8,128)(2,1)S(1)}, u32[]{:S(2)}, u32[]{:S(2)}) %all-to-all-start.4) | async-done | bytes 229408 | tf_op jit(solution)/shard_map/all_to_all | solution.py:422
  117.8 0.8 shard_map.87
  (13 shorter events, 0.3 us)
Async XLA Ops:
  0.6 1.0 copy-start.4
  1.6 0.9 copy-start.5
  2.8 12.5 %collective-permute-start = (bf16[2,4,16,128]{3,2,1,0:T(8,128)(2,1)S(1)}, bf16[2,4,16,128]{3,2,1,0:T(8,128)(2,1)S(1)}, u32[]{:S(2)}, u32[]{:S(2)}) collective-permute-start(bf16[2,4,16,128]{3,2,1,0:T(8,128)(2,1)S(1)} %get-tuple-element.27), channel_id=1, source_target_pairs={{0,448},{64,0},{128,64},{192,128},{256,192},{320,256},{384,320},{4... | collective-permute-start | bytes 98312 | tf_op jit(solution)/shard_map/ppermute | solution.py:358
  15.4 7.4 %collective-permute-start.1 = (bf16[2,6,16,128]{3,2,1,0:T(8,128)(2,1)S(1)}, bf16[2,6,16,128]{3,2,1,0:T(8,128)(2,1)S(1)}, u32[]{:S(2)}, u32[]{:S(2)}) collective-permute-start(bf16[2,6,16,128]{3,2,1,0:T(8,128)(2,1)S(1)} %shard_map.76), channel_id=1, source_target_pairs={{0,56},{8,0},{16,8},{24,16},{32,24},{40,32},{48,40},{56,48},{1,57}... | collective-permute-start | bytes 147464 | tf_op jit(solution)/shard_map/ppermute | solution.py:358
  20.2 0.9 copy-start
  21.1 0.9 copy-start.2
  24.2 23.0 %copy-start.1 = (bf16[16,27,128]{2,0,1:T(8,128)(2,1)S(1)}, bf16[16,27,128]{2,0,1:T(8,128)(2,1)}, u32[]{:S(2)}) copy-start(bf16[16,27,128]{2,0,1:T(8,128)(2,1)} %param.5) | copy-start | bytes 331780
  24.2 23.0 %all-to-all-start = ((bf16[8,44,16,128]{3,2,1,0:T(8,128)(2,1)}), bf16[8,44,16,128]{3,2,1,0:T(8,128)(2,1)S(1)}, u32[]{:S(2)}, u32[]{:S(2)}) async-start(bf16[8,44,16,128]{3,2,1,0:T(8,128)(2,1)} %get-tuple-element.29), calls=%async_computation | async-start | bytes 2883584 | tf_op jit(solution)/shard_map/all_to_all | solution.py:382
  51.0 24.3 %copy-start.3 = (bf16[16,27,128]{2,0,1:T(8,128)(2,1)S(1)}, bf16[16,27,128]{2,0,1:T(8,128)(2,1)}, u32[]{:S(2)}) copy-start(bf16[16,27,128]{2,0,1:T(8,128)(2,1)} %param.6) | copy-start | bytes 331780
  70.5 14.9 %all-to-all-start.2 = ((bf16[8,112,128]{2,1,0:T(8,128)(2,1)}), bf16[8,112,128]{2,1,0:T(8,128)(2,1)S(1)}, u32[]{:S(2)}, u32[]{:S(2)}) async-start(bf16[8,112,128]{2,1,0:T(8,128)(2,1)} %get-tuple-element.32), calls=%async_computation.2 | async-start | bytes 458752 | tf_op jit(solution)/shard_map/all_to_all | solution.py:412
  85.5 3.1 %collective-permute-start.2 = (f32[112,128]{1,0:T(8,128)S(1)}, f32[112,128]{1,0:T(8,128)S(1)}, u32[]{:S(2)}, u32[]{:S(2)}) collective-permute-start(f32[112,128]{1,0:T(8,128)S(1)} %shard_map.82.mine), channel_id=1, source_target_pairs={{0,8},{8,0},{1,9},{9,1},{2,10},{10,2},{3,11},{11,3},{4,12},{12,4},... | collective-permute-start | bytes 172040 | tf_op jit(solution)/shard_map/ppermute | solution.py:415
  89.3 14.4 %all-to-all-start.3 = ((bf16[4,112,128]{2,1,0:T(8,128)(2,1)}), bf16[4,112,128]{2,1,0:T(8,128)(2,1)S(1)}, u32[]{:S(2)}, u32[]{:S(2)}) async-start(bf16[4,112,128]{2,1,0:T(8,128)(2,1)} %shard_map.83), calls=%async_computation.3 | async-start | bytes 229376 | tf_op jit(solution)/shard_map/all_to_all | solution.py:418
  94.5 6.8 %collective-permute-start.3 = (bf16[2,2,16,128]{3,2,1,0:T(8,128)(2,1)S(1)}, bf16[2,2,16,128]{3,2,1,0:T(8,128)(2,1)S(1)}, u32[]{:S(2)}, u32[]{:S(2)}) collective-permute-start(bf16[2,2,16,128]{3,2,1,0:T(8,128)(2,1)S(1)} %get-tuple-element.38), channel_id=1, source_target_pairs={{0,64},{64,128},{128,192},{192,256},{256,320},{320,384},{384,448},... | collective-permute-start | bytes 49160 | tf_op jit(solution)/shard_map/ppermute | solution.py:358
  104.4 13.5 %all-to-all-start.4 = ((bf16[8,112,128]{2,1,0:T(8,128)(2,1)}), bf16[8,112,128]{2,1,0:T(8,128)(2,1)S(1)}, u32[]{:S(2)}, u32[]{:S(2)}) async-start(bf16[8,112,128]{2,1,0:T(8,128)(2,1)} %shard_map.86), calls=%async_computation.4 | async-start | bytes 458752 | tf_op jit(solution)/shard_map/all_to_all | solution.py:422
  107.8 7.3 %collective-permute-start.4 = (bf16[2,2,16,128]{3,2,1,0:T(8,128)(2,1)S(1)}, bf16[2,2,16,128]{3,2,1,0:T(8,128)(2,1)S(1)}, u32[]{:S(2)}, u32[]{:S(2)}) collective-permute-start(bf16[2,2,16,128]{3,2,1,0:T(8,128)(2,1)S(1)} %get-tuple-element.42), channel_id=1, source_target_pairs={{0,8},{8,16},{16,24},{24,32},{32,40},{40,48},{48,56},{56,0},{1,9},... | collective-permute-start | bytes 49160 | tf_op jit(solution)/shard_map/ppermute | solution.py:358

commit v3 on v2

v3 whole, which is shorter than its diff:
```python
import functools
import math

import jax
import jax.numpy as jnp
from jax import lax
from jax.experimental import pallas as pl
from jax.experimental.pallas import tpu as pltpu
from jax.sharding import PartitionSpec as P

BF = jnp.bfloat16
F32 = jnp.float32
T = 128
VMEM = pl.BlockSpec(memory_space=pltpu.VMEM)
SMEM = pl.BlockSpec(memory_space=pltpu.SMEM)
HBM = pl.BlockSpec(memory_space=pltpu.HBM)
GY = ("yh", "co")
EXT = 24 * T
MID = 20 * T
OWN = 16 * T


def call(kernel, outs, scratch=(), scalars=False, hbm=False, limit=8):
    def run(*args):
        return pl.pallas_call(
            kernel,
            out_shape=outs,
            in_specs=[HBM if hbm else SMEM if scalars and k == 0 else VMEM for k in range(len(args))],
            scratch_shapes=scratch,
            compiler_params=pltpu.CompilerParams(vmem_limit_bytes=limit << 20),
        )(*args)

    return run


def lanes(rows=16):
    return lax.broadcasted_iota(jnp.int32, (rows, T), 1)


def rolled(x, shift):
    size = x.shape[1]
    return pltpu.roll(x, shift % size, 1) if shift % size else x


def regroup(tiles):
    lane = lanes()
    tiles = list(tiles)
    for bit in (1, 2, 4):
        clear = (lane // (16 * bit)) % 2 == 0
        for u in range(8):
            if u & bit:
                continue
            first, second = tiles[u], tiles[u + bit]
            tiles[u] = jnp.where(clear, first, rolled(second, 16 * bit))
            tiles[u + bit] = jnp.where(clear, rolled(first, -16 * bit), second)
    return tiles


def pack_kernel(vol_hbm, grad_hbm, own, low, vol, grad, sems):
    copies = [
        pltpu.make_async_copy(source, target, sems.at[k])
        for k, (source, target) in enumerate(((vol_hbm, vol), (grad_hbm, grad)))
    ]
    for copy in copies:
        copy.start()
    for a, ref in enumerate((vol, grad)):
        copies[a].wait()
        for x in range(8):
            tile = ref[0, x].reshape(T, 16).astype(F32).T.astype(BF)
            own[a, x] = tile
            if x < 4:
                low[a, x] = tile


def weight_kernel(w1_hbm, w2_hbm, out, w1, w2, sems):
    copies = [
        pltpu.make_async_copy(source, target, sems.at[k])
        for k, (source, target) in enumerate(((w1_hbm, w1), (w2_hbm, w2)))
    ]
    for copy in copies:
        copy.start()
    for f, ref in enumerate((w1, w2)):
        copies[f].wait()
        for m in range(4):
            tiles = [ref[8 * m + u].astype(F32) if 8 * m + u < 27 else jnp.zeros((16, T), F32) for u in range(8)]
            for j, tile in enumerate(regroup(tiles)):
                out[j, 4 * f + m] = tile.astype(BF)


def gathered(ref, k):
    return ref[:, k].reshape(T, T)


def row_of(own, nextx, a, r):
    return (own[a, r] if r < 8 else nextx[a, r - 8]).astype(F32)


def edge_kernel(own, nextx, out):
    first = lanes() < 64
    for a in range(2):
        for p in range(6):
            odd = rolled(row_of(own, nextx, a, 2 * p + 1), 64)
            out[a, p] = jnp.where(first, row_of(own, nextx, a, 2 * p), odd).astype(BF)


def send_kernel(own, nextx, nexty, weights, send):
    for j in range(8):
        for a in range(2):
            for k in range(18):
                send[j, 18 * a + k] = own[a, k] if k < 8 else nextx[a, k - 8] if k < 12 else nexty[a, k - 12]
        for k in range(8):
            send[j, 36 + k] = weights[j, k]


def product(left, right, out, width):
    for n in range(0, width, 640):
        size = min(640, width - n)
        out[:, n : n + size] = jnp.dot(left, right[:, n : n + size], preferred_element_type=F32)


def cells(width):
    lane = lax.broadcasted_iota(jnp.int32, (16, width), 1)
    return lane % 256 // 16, lane % 16


def combine(prods, sign, width, first, place):
    column, depth = cells(width)
    split_y = place[1] == 7
    for step, r in ((1, 8), (-1, 7)):
        a = (1 + sign * step) * 144
        at = 256 * (r - first)
        part = prods[a : a + 144, at : at + 256]
        prods[a : a + 144, at : at + 256] = jnp.where(place[0] == 7, 0.0, part)
    apart = {1: (column == 7) & split_y, -1: (column == 8) & split_y}
    total = None
    for e in range(3):
        part = None
        for c in range(3):
            term = None
            for a in range(3):
                t = 9 * a + 3 * c + e
                start = 256 * a if sign > 0 else 256 * (2 - a)
                piece = prods[t * 16 : t * 16 + 16, start : start + width]
                term = piece if term is None else term + piece
            step = sign * (c - 1)
            if step:
                term = jnp.where(apart[step], 0.0, rolled(term, -step * 16))
            part = term if part is None else part + term
        step = sign * (e - 1)
        if step:
            part = rolled(part, -step)
            part = jnp.where(depth != (15 if step > 0 else 0), part, 0.0)
        total = part if total is None else total + part
    return total


def shifted(field, place, out):
    column, depth = cells(OWN)
    split_y = place[1] == 7
    for c in range(3):
        moved = rolled(field, (c - 1) * 16)
        if c != 1:
            moved = jnp.where((column == (8 if c == 2 else 7)) & split_y, 0.0, moved)
        for e in range(3):
            piece = rolled(moved, e - 1)
            if e != 1:
                piece = jnp.where(depth != (0 if e == 2 else 15), piece, 0.0)
            k = (c * 3 + e) * 16
            out[k : k + 16, :] = piece.astype(BF)


def correlate(place, shifts, field, base, out):
    def product_of(at, start, width):
        return lax.dot_general(
            shifts[:, at : at + width],
            field[:, start : start + width],
            (((1,), (1,)), ((), ())),
            preferred_element_type=F32,
        )

    for a in range(3):
        total = product_of(0, base + 256 * a, OWN)
        if a != 1:
            at = 256 * (5 if a == 2 else 6)
            across = product_of(at, base + 256 * a + at, 256)
            total = total - jnp.where(place[0] == 7, across, 0.0)
        out[a * 144 : a * 144 + 144, :] = total


def gathered_filter(ref, first):
    parts = [gathered(ref, first + m).astype(F32).T.astype(BF) for m in range(4)]
    return jnp.concatenate(parts, axis=0)[0:432]


def first_kernel(place, block, w1rows, send, sums, vol, grad, prods1, prods2, shifts):
    for a, ref in enumerate((vol, grad)):
        def put(tile, value):
            ref[:, tile * T : tile * T + T] = value

        for r in range(12):
            put(2 * r, gathered(block, 18 * a + r))
            value = gathered(block, 18 * a + 12 + r // 2)
            put(2 * r + 1, rolled(value.astype(F32), 64).astype(BF) if r % 2 else value)
    product(w1rows[...].reshape(432, T), vol, prods1, EXT)
    product(gathered_filter(block, 40), grad, prods2, EXT)

    pre = combine(prods1, 1, MID, 0, place).astype(BF).astype(F32)
    sig = jax.nn.sigmoid(pre)
    hidden = (pre * sig).astype(BF).astype(F32)
    back = combine(prods2, -1, MID, 0, place)
    back = (back * sig * (1.0 + pre * (1.0 - sig))).astype(BF).astype(F32)

    narrow = lanes()
    for a, field in enumerate((hidden, back)):
        packed = [None] * 3
        for r in range(10):
            inner = field[:, 2 * r * T : (2 * r + 1) * T]
            outer = field[:, (2 * r + 1) * T : (2 * r + 2) * T]
            tile_r = jnp.where(narrow < 16, rolled(outer, -32), inner).astype(BF)
            q, k = r // 4, r % 4
            moved = rolled(outer, 32 * k)
            packed[q] = moved if packed[q] is None else jnp.where(narrow // 32 == k, moved, packed[q])
            for j in range(8):
                send[j, a * 13 + r] = tile_r
        for q in range(3):
            tile_q = packed[q].astype(BF)
            for j in range(8):
                send[j, a * 13 + 10 + q] = tile_q

    column, _ = cells(OWN)
    inside = (column >= 2) & (column < 10)
    shifted(jnp.where(inside, back[:, 2 * T : 2 * T + OWN], 0.0), place, shifts)
    correlate(place, shifts, vol, 2 * T, sums)


def spread(middle, a, ref):
    lane = lanes(T)
    for r in range(10):
        inner = gathered(middle, a * 13 + r)
        outer = rolled(gathered(middle, a * 13 + 10 + r // 4).astype(F32), -32 * (r % 4))
        ref[:, 2 * r * T : (2 * r + 1) * T] = inner
        outer = jnp.where(lane < 32, outer, rolled(inner.astype(F32), 32))
        ref[:, (2 * r + 1) * T : (2 * r + 2) * T] = outer.astype(BF)


def grad_kernel(place, own, nextx, nexty, middle, sums1, hid, send, field, shifts, sums2):
    spread(middle, 0, hid)
    lane = lanes()
    for r in range(2, 10):
        field[:, (2 * r - 4) * T : (2 * r - 3) * T] = jnp.where(lane >= 32, row_of(own, nextx, 1, r), 0.0)
        tile = nexty[1, r // 2].astype(F32)
        tile = rolled(tile, 64) if r % 2 else tile
        field[:, (2 * r - 3) * T : (2 * r - 2) * T] = jnp.where(lane < 32, tile, 0.0)
    shifted(field[...], place, shifts)
    correlate(place, shifts, hid, 0, sums2)
    rows = jnp.concatenate([sums1[...], sums2[...], jnp.zeros((32, T), F32)], axis=0)
    send[...] = rows.astype(BF).reshape(8, 112, T)


def second_kernel(place, block, middle, hid, w2rows, keep, give, pre, prods):
    spread(middle, 1, pre)

    def store(which, value):
        for x in range(8):
            for side in range(2):
                tile = value[:, (2 * x + side) * T : (2 * x + side + 1) * T].astype(BF)
                if x < 6:
                    keep[which, x, side] = tile
                else:
                    give[which, x - 6, side] = tile

    product(w2rows[...].reshape(432, T), hid, prods, MID)
    store(0, combine(prods, 1, OWN, 1, place))
    product(gathered_filter(block, 36), pre, prods, MID)
    store(1, combine(prods, -1, OWN, 1, place))


def back_kernel(keep, taken, rows, give):
    lane = lanes()
    for a in range(2):
        for q in range(2):
            packed = None
            for k in range(4):
                x = 4 * q + k
                tiles = taken.at[a, x] if x < 2 else keep.at[a, x - 2]
                rows[a, x] = tiles[0]
                moved = rolled(tiles[1].astype(F32), 32 * k)
                packed = moved if packed is None else jnp.where(lane // 32 == k, moved, packed)
            give[a, q] = packed.astype(BF)


def out_kernel(rows, taken, out, vgrad):
    lane = lanes()
    for a, ref in enumerate((out, vgrad)):
        for x in range(8):
            first = rolled(taken[a, x // 4].astype(F32), -32 * (x % 4))
            tile = jnp.where(lane < 32, first, rows[a, x].astype(F32))
            ref[0, x] = tile.T.astype(BF).reshape(8, 16, 16)


def sum_kernel(factor, parts, out):
    total = parts[0].astype(F32)
    for k in range(1, parts.shape[0]):
        total = total + parts[k].astype(F32)
    total = total * factor
    if out.shape == total.shape:
        out[...] = total
    else:
        for j in range(out.shape[0]):
            out[j] = total.astype(BF)


def last_kernel(parts, first, second):
    rows = parts[...].reshape(896, T).astype(F32)
    first[...] = rows[0:432].reshape(27, 16, T)
    second[...] = rows[432:864].reshape(27, 16, T)


def shape(*dims, dtype=BF):
    return jax.ShapeDtypeStruct(dims, dtype)


def cyclic(x, axis, step):
    size = lax.axis_size(axis)
    return lax.ppermute(x, axis, [(i, (i + step) % size) for i in range(size)])


def on_device(volume, first_filter, second_filter, out_grad):
    factor = 1.0 / math.sqrt(64 * 64 * 16)
    place = jnp.stack([lax.axis_index("gx"), lax.axis_index(GY)]).astype(jnp.int32)
    w1 = first_filter.transpose(1, 0, 2)
    w2 = second_filter.transpose(1, 0, 2)
    two = shape(2, 8, 16, T)
    own, low = call(
        pack_kernel,
        (two, shape(2, 4, 16, T)),
        [pltpu.VMEM((1, 8, 8, 16, 16), BF)] * 2 + [pltpu.SemaphoreType.DMA((2,))],
        hbm=True,
    )(volume, out_grad)
    nextx = cyclic(low, "gx", -1)
    pieces = call(
        weight_kernel,
        shape(8, 8, 16, T),
        [pltpu.VMEM((27, 16, T), BF)] * 2 + [pltpu.SemaphoreType.DMA((2,))],
        hbm=True,
    )(w1, w2)
    nextx, pieces = lax.optimization_barrier((nextx, pieces))
    nexty = cyclic(call(edge_kernel, shape(2, 6, 16, T))(own, nextx), GY, -1)
    nexty, place = lax.optimization_barrier((nexty, place))
    block = lax.all_to_all(call(send_kernel, shape(8, 44, 16, T))(own, nextx, nexty, pieces), "af", 0, 0)
    middle, sums = call(
        first_kernel,
        (shape(8, 26, 16, T), shape(432, T, dtype=F32)),
        [
            pltpu.VMEM((T, EXT), BF),
            pltpu.VMEM((T, EXT), BF),
            pltpu.VMEM((432, EXT), F32),
            pltpu.VMEM((432, EXT), F32),
            pltpu.VMEM((144, OWN), BF),
        ],
        scalars=True,
        limit=28,
    )(place, block, w1)
    middle = lax.all_to_all(middle, "af", 0, 0)
    many = shape(8, 112, T)
    hid, parts = call(
        grad_kernel,
        (shape(T, MID), many),
        [pltpu.VMEM((16, OWN), F32), pltpu.VMEM((144, OWN), BF), pltpu.VMEM((432, T), F32)],
        scalars=True,
        limit=16,
    )(place, own, nextx, nexty, middle, sums)
    keep, give = call(
        second_kernel,
        (shape(2, 6, 2, 16, T), shape(2, 2, 2, 16, T)),
        [pltpu.VMEM((T, MID), BF), pltpu.VMEM((432, MID), F32)],
        scalars=True,
        limit=20,
    )(place, block, middle, hid, w2)
    parts = lax.all_to_all(parts, "gx", 0, 0)
    parts, keep, give = lax.optimization_barrier((parts, keep, give))
    parts = call(functools.partial(sum_kernel, 1.0), many)(parts)
    rows, give = call(back_kernel, (two, shape(2, 2, 16, T)))(keep, cyclic(give, "gx", 1))
    parts = lax.all_to_all(parts, GY, 0, 0)
    parts, rows, give = lax.optimization_barrier((parts, rows, give))
    parts = call(functools.partial(sum_kernel, factor), many)(parts)
    output, volume_grad = call(out_kernel, (shape(1, 8, 8, 16, 16), shape(1, 8, 8, 16, 16)))(rows, cyclic(give, GY, 1))
    parts = lax.all_to_all(parts, "gx", 0, 0)
    wide = shape(27, 16, T, dtype=F32)
    first_grad, second_grad = call(last_kernel, (wide, wide))(parts)
    return output, volume_grad, first_grad.transpose(1, 0, 2), second_grad.transpose(1, 0, 2)


def solution(mesh):
    split = jax.sharding.Mesh(mesh.devices.reshape(8, 4, 2, 8), ("gx", "yh", "co", "af"))
    cells = P(None, "gx", GY, None, "af")
    weights = P("af", None, None)
    return jax.shard_map(
        on_device,
        mesh=split,
        in_specs=(cells, weights, weights, cells),
        out_specs=(cells, cells, weights, weights),
        check_vma=False,
    )
```

time: 119 us -> 118 us (level)
  blocking collectives: 17.3 us -> 38.9 us
  waiting for transfers between devices: 42 us -> 26.6 us
  starting transfers between devices: 40.5 us -> 33.9 us
  Pallas kernels: 14.3 us -> 13 us
    all_to_all x0 -> x1, blocking collectives: none -> 23.4 us  [on_device(): lax.all_to_all(call(send_kernel, shape(8, 44, 16, T))(own, nextx, nexty,...]
    all_to_all x2 -> x1, waiting for transfers between devices: 20.1 us -> 4.95 us  [on_device(): parts = lax.all_to_all(parts, GY, 0, 0)]
    all_to_all x2 -> x1, starting transfers between devices: 10.3 us -> 5.13 us  [on_device(): parts = lax.all_to_all(parts, GY, 0, 0)]
    ppermute x1 -> x0, starting transfers between devices: 1.92 us -> none  [on_device(): other = lax.ppermute(part, 'co', [(0, 1), (1, 0)])]
    all_to_all x1, blocking collectives: 17.3 us -> 15.5 us  [on_device(): middle = lax.all_to_all(middle, 'af', 0, 0)]
    pallas_call x13 -> x12, Pallas kernels: 14.3 us -> 13 us  [run(): pl.pallas_call(kernel, out_shape=outs, in_specs=[HBM if hbm else SMEM if...]
    ppermute x1 -> x0, waiting for transfers between devices: 1.21 us -> none  [on_device(): other = lax.ppermute(part, 'co', [(0, 1), (1, 0)])]
  transfers between devices with their start and end apart: 9 -> 7, of which waited for: 8 -> 6; matrix products, arithmetic and copies ran while one was open for 0% -> 0% of each run, Pallas kernels for 4% -> 4%
where the time goes in v3:
time: 118 us; the launch traced here: 117 us
  blocking collectives  38.9 us (33%)
  starting transfers between devices  33.9 us (29%)
  waiting for transfers between devices  26.6 us (23%)
  Pallas kernels  13 us (11%)
  local copies, waits for them, and re-layouts  3.69 us (3%)
    all_to_all x1, blocking collectives, on_device(): lax.all_to_all(call(send_kernel, shape(8, 44, 16, T))(own, nextx, nexty,...  23.4 us
    ppermute x4, starting transfers between devices, cyclic(): return lax.ppermute(x, axis, [(i, (i + step) % size) for i in range(size)])  20.6 us
    all_to_all x1, blocking collectives, on_device(): middle = lax.all_to_all(middle, 'af', 0, 0)  15.5 us
    pallas_call x12, Pallas kernels, run(): pl.pallas_call(kernel, out_shape=outs, in_specs=[HBM if hbm else SMEM if...  13 us
    ppermute x4, waiting for transfers between devices, cyclic(): return lax.ppermute(x, axis, [(i, (i + step) % size) for i in range(size)])  11.9 us
    all_to_all x2, waiting for transfers between devices, on_device(): parts = lax.all_to_all(parts, 'gx', 0, 0)  9.77 us
    all_to_all x2, starting transfers between devices, on_device(): parts = lax.all_to_all(parts, 'gx', 0, 0)  8.17 us
    all_to_all x1, starting transfers between devices, on_device(): parts = lax.all_to_all(parts, GY, 0, 0)  5.13 us
  transfers between devices with their start and end apart: 7, of which 6 were waited for; matrix products, arithmetic and copies ran while one was open for 0% of the time, Pallas kernels for 4%

profile of v3, /device:TPU:2, one launch (start us, length us, event | category | flops | bytes accessed | tf_op | source)
XLA Modules:
  0.0 117.0 jit_solution(13267930857219385790)
XLA Ops:
  0.6 0.9 copy-done.4
  1.6 0.9 copy-done.5
  2.5 0.3 shard_map.75
  2.8 10.9 %collective-permute-start = (bf16[2,4,16,128]{3,2,1,0:T(8,128)(2,1)S(1)}, bf16[2,4,16,128]{3,2,1,0:T(8,128)(2,1)S(1)}, u32[]{:S(2)}, u32[]{:S(2)}) collective-permute-start(bf16[2,4,16,128]{3,2,1,0:T(8,128)(2,1)S(1)} %get-tuple-element.29), channel_id=1, source_target_pairs={{0,448},{64,0},{128,64},{192,128},{256,192},{320,256},{384,320},{4... | collective-permute-start | bytes 98312 | tf_op jit(solution)/shard_map/ppermute | solution.py:325
  13.8 0.9 copy-done
  14.7 0.9 copy-done.2
  15.6 0.8 shard_map.76.weights
  16.4 0.1 shard_map.77
  16.5 5.3 %collective-permute-start.1 = (bf16[2,6,16,128]{3,2,1,0:T(8,128)(2,1)S(1)}, bf16[2,6,16,128]{3,2,1,0:T(8,128)(2,1)S(1)}, u32[]{:S(2)}, u32[]{:S(2)}) collective-permute-start(bf16[2,6,16,128]{3,2,1,0:T(8,128)(2,1)S(1)} %shard_map.77), channel_id=1, source_target_pairs={{0,56},{8,0},{16,8},{24,16},{32,24},{40,32},{48,40},{56,48},{1,57}... | collective-permute-start | bytes 147464 | tf_op jit(solution)/shard_map/ppermute | solution.py:325
  21.8 0.1 pad_add_fusion.place
  21.9 2.1 %collective-permute-done.1.nexty = bf16[2,6,16,128]{3,2,1,0:T(8,128)(2,1)S(1)} collective-permute-done((bf16[2,6,16,128]{3,2,1,0:T(8,128)(2,1)S(1)}, bf16[2,6,16,128]{3,2,1,0:T(8,128)(2,1)S(1)}, u32[]{:S(2)}, u32[]{:S(2)}) %collective-permute-start.1) | collective-permute-done | bytes 49184 | tf_op jit(solution)/shard_map/ppermute | solution.py:325
  24.0 0.2 shard_map.78
  24.2 23.4 %all_to_all.25.block = bf16[8,44,16,128]{3,2,1,0:T(8,128)(2,1)S(1)} all-to-all(bf16[8,44,16,128]{3,2,1,0:T(8,128)(2,1)S(1)} %shard_map.78), channel_id=1, replica_groups=mesh['gx'=8,'yh'=4,'co'=2,'af'=8] {'af'}, dimensions={0} | all-to-all | bytes 2883584 | tf_op jit(solution)/shard_map/all_to_all | solution.py:350
  47.6 3.7 %shard_map.79 = (bf16[8,26,16,128]{3,2,1,0:T(8,128)(2,1)S(1)}, f32[432,128]{1,0:T(8,128)S(1)}) custom-call(s32[2]{0:T(128)S(1)} %pad_add_fusion.place, bf16[8,44,16,128]{3,2,1,0:T(8,128)(2,1)S(1)} %all_to_all.25.block, bf16[27,16,128]{2,1,0:T(8,128)(2,1)S(1)} %bitcast.7), custom_call_target="tpu_custom_call" | custom-call | tf_op jit(solution)/shard_map/pallas_call | solution.py:25
  51.3 15.5 %all_to_all.26.middle = bf16[8,26,16,128]{3,2,1,0:T(8,128)(2,1)S(1)} all-to-all(bf16[8,26,16,128]{3,2,1,0:T(8,128)(2,1)S(1)} %get-tuple-element.34), channel_id=1, replica_groups=mesh['gx'=8,'yh'=4,'co'=2,'af'=8] {'af'}, dimensions={0} | all-to-all | bytes 1703936 | tf_op jit(solution)/shard_map/all_to_all | solution.py:364
  66.8 2.2 %shard_map.80 = (bf16[128,2560]{1,0:T(8,128)(2,1)S(1)}, bf16[8,112,128]{2,1,0:T(8,128)(2,1)}) custom-call(s32[2]{0:T(128)S(1)} %pad_add_fusion.place, bf16[2,8,16,128]{3,2,1,0:T(8,128)(2,1)S(1)} %get-tuple-element.28.own, bf16[2,4,16,128]{3,2,1,0:T(8,128)(2,1)S(1)} %collective-permute-done.nextx, bf16[2,6,16,128]{3,2,1,0:T(8,128)(2,1)S(1)} %collective-permute-done.1.nexty, ...), custom_call_target="tpu_custom_call" | custom-call | tf_op jit(solution)/shard_map/pallas_call | solution.py:25
  69.0 4.8 %all-to-all-start.2 = ((bf16[8,112,128]{2,1,0:T(8,128)(2,1)}), bf16[8,112,128]{2,1,0:T(8,128)(2,1)S(1)}, u32[]{:S(2)}, u32[]{:S(2)}) async-start(bf16[8,112,128]{2,1,0:T(8,128)(2,1)} %get-tuple-element.36), calls=%async_computation.2 | async-start | bytes 458752 | tf_op jit(solution)/shard_map/all_to_all | solution.py:380
  73.8 2.2 %shard_map.81 = (bf16[2,6,2,16,128]{4,3,2,1,0:T(8,128)(2,1)S(1)}, bf16[2,2,2,16,128]{4,3,2,1,0:T(8,128)(2,1)S(1)}) custom-call(s32[2]{0:T(128)S(1)} %pad_add_fusion.place, bf16[8,44,16,128]{3,2,1,0:T(8,128)(2,1)S(1)} %all_to_all.25.block, bf16[8,26,16,128]{3,2,1,0:T(8,128)(2,1)S(1)} %all_to_all.26.middle, bf16[128,2560]{1,0:T(8,128)(2,1)S(1)} %get-tuple-element.37.hid, ...), custom_call_target="tpu_custom_call" | custom-call | tf_op jit(solution)/shard_map/pallas_call | solution.py:25
  76.1 7.9 %all-to-all-done.2.parts = bf16[8,112,128]{2,1,0:T(8,128)(2,1)S(1)} async-done(((bf16[8,112,128]{2,1,0:T(8,128)(2,1)}), bf16[8,112,128]{2,1,0:T(8,128)(2,1)S(1)}, u32[]{:S(2)}, u32[]{:S(2)}) %all-to-all-start.2) | async-done | bytes 229408 | tf_op jit(solution)/shard_map/all_to_all | solution.py:380
  83.9 0.7 shard_map.82
  84.7 5.1 %all-to-all-start.3 = ((bf16[8,112,128]{2,1,0:T(8,128)(2,1)}), bf16[8,112,128]{2,1,0:T(8,128)(2,1)S(1)}, u32[]{:S(2)}, u32[]{:S(2)}) async-start(bf16[8,112,128]{2,1,0:T(8,128)(2,1)} %shard_map.82), calls=%async_computation.3 | async-start | bytes 458752 | tf_op jit(solution)/shard_map/all_to_all | solution.py:384
  89.8 2.4 %collective-permute-start.2 = (bf16[2,2,2,16,128]{4,3,2,1,0:T(8,128)(2,1)S(1)}, bf16[2,2,2,16,128]{4,3,2,1,0:T(8,128)(2,1)S(1)}, u32[]{:S(2)}, u32[]{:S(2)}) collective-permute-start(bf16[2,2,2,16,128]{4,3,2,1,0:T(8,128)(2,1)S(1)} %get-tuple-element.42), channel_id=1, source_target_pairs={{0,64},{64,128},{128,192},{192,256},{256,320},{320,384},{384,448},... | collective-permute-start | bytes 98312 | tf_op jit(solution)/shard_map/ppermute | solution.py:325
  92.2 4.6 %collective-permute-done.2.taken = bf16[2,2,2,16,128]{4,3,2,1,0:T(8,128)(2,1)S(1)} collective-permute-done((bf16[2,2,2,16,128]{4,3,2,1,0:T(8,128)(2,1)S(1)}, bf16[2,2,2,16,128]{4,3,2,1,0:T(8,128)(2,1)S(1)}, u32[]{:S(2)}, u32[]{:S(2)}) %collective-permute-start.2) | collective-permute-done | bytes 32800 | tf_op jit(solution)/shard_map/ppermute | solution.py:325
  96.8 0.1 shard_map.83
  96.9 5.0 %all-to-all-done.3.parts = bf16[8,112,128]{2,1,0:T(8,128)(2,1)S(1)} async-done(((bf16[8,112,128]{2,1,0:T(8,128)(2,1)}), bf16[8,112,128]{2,1,0:T(8,128)(2,1)S(1)}, u32[]{:S(2)}, u32[]{:S(2)}) %all-to-all-start.3) | async-done | bytes 229408 | tf_op jit(solution)/shard_map/all_to_all | solution.py:384
  101.8 0.7 shard_map.85
  102.6 3.4 %all-to-all-start.4 = ((bf16[8,112,128]{2,1,0:T(8,128)(2,1)}), bf16[8,112,128]{2,1,0:T(8,128)(2,1)S(1)}, u32[]{:S(2)}, u32[]{:S(2)}) async-start(bf16[8,112,128]{2,1,0:T(8,128)(2,1)} %shard_map.85), calls=%async_computation.4 | async-start | bytes 458752 | tf_op jit(solution)/shard_map/all_to_all | solution.py:388
  106.0 1.9 %collective-permute-start.3 = (bf16[2,2,16,128]{3,2,1,0:T(8,128)(2,1)S(1)}, bf16[2,2,16,128]{3,2,1,0:T(8,128)(2,1)S(1)}, u32[]{:S(2)}, u32[]{:S(2)}) collective-permute-start(bf16[2,2,16,128]{3,2,1,0:T(8,128)(2,1)S(1)} %get-tuple-element.46), channel_id=1, source_target_pairs={{0,8},{8,16},{16,24},{24,32},{32,40},{40,48},{48,56},{56,0},{1,9},... | collective-permute-start | bytes 49160 | tf_op jit(solution)/shard_map/ppermute | solution.py:325
  107.9 5.2 %collective-permute-done.3.taken = bf16[2,2,16,128]{3,2,1,0:T(8,128)(2,1)S(1)} collective-permute-done((bf16[2,2,16,128]{3,2,1,0:T(8,128)(2,1)S(1)}, bf16[2,2,16,128]{3,2,1,0:T(8,128)(2,1)S(1)}, u32[]{:S(2)}, u32[]{:S(2)}) %collective-permute-start.3) | collective-permute-done | bytes 16416 | tf_op jit(solution)/shard_map/ppermute | solution.py:325
  113.2 1.2 shard_map.84
  114.3 1.9 %all-to-all-done.4.parts = bf16[8,112,128]{2,1,0:T(8,128)(2,1)S(1)} async-done(((bf16[8,112,128]{2,1,0:T(8,128)(2,1)}), bf16[8,112,128]{2,1,0:T(8,128)(2,1)S(1)}, u32[]{:S(2)}, u32[]{:S(2)}) %all-to-all-start.4) | async-done | bytes 229408 | tf_op jit(solution)/shard_map/all_to_all | solution.py:388
  116.2 0.8 shard_map.86
  (9 shorter events, 0.0 us)
Async XLA Ops:
  0.6 1.0 copy-start.4
  1.6 0.9 copy-start.5
  2.8 13.6 %collective-permute-start = (bf16[2,4,16,128]{3,2,1,0:T(8,128)(2,1)S(1)}, bf16[2,4,16,128]{3,2,1,0:T(8,128)(2,1)S(1)}, u32[]{:S(2)}, u32[]{:S(2)}) collective-permute-start(bf16[2,4,16,128]{3,2,1,0:T(8,128)(2,1)S(1)} %get-tuple-element.29), channel_id=1, source_target_pairs={{0,448},{64,0},{128,64},{192,128},{256,192},{320,256},{384,320},{4... | collective-permute-start | bytes 98312 | tf_op jit(solution)/shard_map/ppermute | solution.py:325
  13.8 0.9 copy-start
  14.7 0.9 copy-start.2
  16.5 7.5 %collective-permute-start.1 = (bf16[2,6,16,128]{3,2,1,0:T(8,128)(2,1)S(1)}, bf16[2,6,16,128]{3,2,1,0:T(8,128)(2,1)S(1)}, u32[]{:S(2)}, u32[]{:S(2)}) collective-permute-start(bf16[2,6,16,128]{3,2,1,0:T(8,128)(2,1)S(1)} %shard_map.77), channel_id=1, source_target_pairs={{0,56},{8,0},{16,8},{24,16},{32,24},{40,32},{48,40},{56,48},{1,57}... | collective-permute-start | bytes 147464 | tf_op jit(solution)/shard_map/ppermute | solution.py:325
  24.1 23.4 %copy-start.1 = (bf16[16,27,128]{2,0,1:T(8,128)(2,1)S(1)}, bf16[16,27,128]{2,0,1:T(8,128)(2,1)}, u32[]{:S(2)}) copy-start(bf16[16,27,128]{2,0,1:T(8,128)(2,1)} %param.5) | copy-start | bytes 331780
  51.3 22.5 %copy-start.3 = (bf16[16,27,128]{2,0,1:T(8,128)(2,1)S(1)}, bf16[16,27,128]{2,0,1:T(8,128)(2,1)}, u32[]{:S(2)}) copy-start(bf16[16,27,128]{2,0,1:T(8,128)(2,1)} %param.6) | copy-start | bytes 331780
  69.0 14.9 %all-to-all-start.2 = ((bf16[8,112,128]{2,1,0:T(8,128)(2,1)}), bf16[8,112,128]{2,1,0:T(8,128)(2,1)S(1)}, u32[]{:S(2)}, u32[]{:S(2)}) async-start(bf16[8,112,128]{2,1,0:T(8,128)(2,1)} %get-tuple-element.36), calls=%async_computation.2 | async-start | bytes 458752 | tf_op jit(solution)/shard_map/all_to_all | solution.py:380
  84.7 17.2 %all-to-all-start.3 = ((bf16[8,112,128]{2,1,0:T(8,128)(2,1)}), bf16[8,112,128]{2,1,0:T(8,128)(2,1)S(1)}, u32[]{:S(2)}, u32[]{:S(2)}) async-start(bf16[8,112,128]{2,1,0:T(8,128)(2,1)} %shard_map.82), calls=%async_computation.3 | async-start | bytes 458752 | tf_op jit(solution)/shard_map/all_to_all | solution.py:384
  89.8 7.0 %collective-permute-start.2 = (bf16[2,2,2,16,128]{4,3,2,1,0:T(8,128)(2,1)S(1)}, bf16[2,2,2,16,128]{4,3,2,1,0:T(8,128)(2,1)S(1)}, u32[]{:S(2)}, u32[]{:S(2)}) collective-permute-start(bf16[2,2,2,16,128]{4,3,2,1,0:T(8,128)(2,1)S(1)} %get-tuple-element.42), channel_id=1, source_target_pairs={{0,64},{64,128},{128,192},{192,256},{256,320},{320,384},{384,448},... | collective-permute-start | bytes 98312 | tf_op jit(solution)/shard_map/ppermute | solution.py:325
  102.6 13.6 %all-to-all-start.4 = ((bf16[8,112,128]{2,1,0:T(8,128)(2,1)}), bf16[8,112,128]{2,1,0:T(8,128)(2,1)S(1)}, u32[]{:S(2)}, u32[]{:S(2)}) async-start(bf16[8,112,128]{2,1,0:T(8,128)(2,1)} %shard_map.85), calls=%async_computation.4 | async-start | bytes 458752 | tf_op jit(solution)/shard_map/all_to_all | solution.py:388
  106.0 7.2 %collective-permute-start.3 = (bf16[2,2,16,128]{3,2,1,0:T(8,128)(2,1)S(1)}, bf16[2,2,16,128]{3,2,1,0:T(8,128)(2,1)S(1)}, u32[]{:S(2)}, u32[]{:S(2)}) collective-permute-start(bf16[2,2,16,128]{3,2,1,0:T(8,128)(2,1)S(1)} %get-tuple-element.46), channel_id=1, source_target_pairs={{0,8},{8,16},{16,24},{24,32},{32,40},{40,48},{48,56},{56,0},{1,9},... | collective-permute-start | bytes 49160 | tf_op jit(solution)/shard_map/ppermute | solution.py:325

commit v4 on v3

--- a/solution.py
+++ b/solution.py
@@ -15,7 +15,6 @@
 SMEM = pl.BlockSpec(memory_space=pltpu.SMEM)
 HBM = pl.BlockSpec(memory_space=pltpu.HBM)
 GY = ("yh", "co")
-EXT = 24 * T
 MID = 20 * T
 OWN = 16 * T
 
@@ -123,25 +122,29 @@
     return lane % 256 // 16, lane % 16
 
 
-def combine(prods, sign, width, first, place):
+def stacked(place, ref, first, count, r, side, value):
+    for b in range(3):
+        out_row = r - b + 1
+        if not first <= out_row < first + count:
+            continue
+        if (b, out_row) in ((2, 7), (0, 8)):
+            tile = (value.astype(F32) * jnp.where(place[0] == 7, 0.0, 1.0)).astype(BF)
+        else:
+            tile = value
+        at = (2 * (out_row - first) + side) * T
+        ref[b * T : b * T + T, at : at + T] = tile
+
+
+def combine(prods, sign, width, place):
     column, depth = cells(width)
     split_y = place[1] == 7
-    for step, r in ((1, 8), (-1, 7)):
-        a = (1 + sign * step) * 144
-        at = 256 * (r - first)
-        part = prods[a : a + 144, at : at + 256]
-        prods[a : a + 144, at : at + 256] = jnp.where(place[0] == 7, 0.0, part)
     apart = {1: (column == 7) & split_y, -1: (column == 8) & split_y}
     total = None
     for e in range(3):
         part = None
         for c in range(3):
-            term = None
-            for a in range(3):
-                t = 9 * a + 3 * c + e
-                start = 256 * a if sign > 0 else 256 * (2 - a)
-                piece = prods[t * 16 : t * 16 + 16, start : start + width]
-                term = piece if term is None else term + piece
+            k = (3 * c + e) * 16
+            term = prods[k : k + 16, :]
             step = sign * (c - 1)
             if step:
                 term = jnp.where(apart[step], 0.0, rolled(term, -step * 16))
@@ -169,22 +172,15 @@
             out[k : k + 16, :] = piece.astype(BF)
 
 
-def correlate(place, shifts, field, base, out):
-    def product_of(at, start, width):
-        return lax.dot_general(
-            shifts[:, at : at + width],
-            field[:, start : start + width],
-            (((1,), (1,)), ((), ())),
-            preferred_element_type=F32,
-        )
-
+def correlate(shifts, field, out):
+    total = lax.dot_general(shifts[...], field, (((1,), (1,)), ((), ())), preferred_element_type=F32)
     for a in range(3):
-        total = product_of(0, base + 256 * a, OWN)
-        if a != 1:
-            at = 256 * (5 if a == 2 else 6)
-            across = product_of(at, base + 256 * a + at, 256)
-            total = total - jnp.where(place[0] == 7, across, 0.0)
-        out[a * 144 : a * 144 + 144, :] = total
+        out[a * 144 : a * 144 + 144, :] = total[:, a * T : a * T + T]
+
+
+def by_tap(filters, sign):
+    parts = [filters[a * 144 : a * 144 + 144] for a in range(3)]
+    return jnp.concatenate(parts[::sign], axis=1)
 
 
 def gathered_filter(ref, first):
@@ -194,20 +190,18 @@
 
 def first_kernel(place, block, w1rows, send, sums, vol, grad, prods1, prods2, shifts):
     for a, ref in enumerate((vol, grad)):
-        def put(tile, value):
-            ref[:, tile * T : tile * T + T] = value
-
         for r in range(12):
-            put(2 * r, gathered(block, 18 * a + r))
             value = gathered(block, 18 * a + 12 + r // 2)
-            put(2 * r + 1, rolled(value.astype(F32), 64).astype(BF) if r % 2 else value)
-    product(w1rows[...].reshape(432, T), vol, prods1, EXT)
-    product(gathered_filter(block, 40), grad, prods2, EXT)
-
-    pre = combine(prods1, 1, MID, 0, place).astype(BF).astype(F32)
+            value = rolled(value.astype(F32), 64).astype(BF) if r % 2 else value
+            stacked(place, ref, 1, 10, r, 0, gathered(block, 18 * a + r))
+            stacked(place, ref, 1, 10, r, 1, value)
+    product(by_tap(w1rows[...].reshape(432, T), 1), vol, prods1, MID)
+    product(by_tap(gathered_filter(block, 40), -1), grad, prods2, MID)
+
+    pre = combine(prods1, 1, MID, place).astype(BF).astype(F32)
     sig = jax.nn.sigmoid(pre)
     hidden = (pre * sig).astype(BF).astype(F32)
-    back = combine(prods2, -1, MID, 0, place)
+    back = combine(prods2, -1, MID, place)
     back = (back * sig * (1.0 + pre * (1.0 - sig))).astype(BF).astype(F32)
 
     narrow = lanes()
@@ -230,21 +224,21 @@
     column, _ = cells(OWN)
     inside = (column >= 2) & (column < 10)
     shifted(jnp.where(inside, back[:, 2 * T : 2 * T + OWN], 0.0), place, shifts)
-    correlate(place, shifts, vol, 2 * T, sums)
-
-
-def spread(middle, a, ref):
+    correlate(shifts, vol[:, 2 * T : 2 * T + OWN], sums)
+
+
+def spread(place, middle, a, ref):
     lane = lanes(T)
     for r in range(10):
         inner = gathered(middle, a * 13 + r)
         outer = rolled(gathered(middle, a * 13 + 10 + r // 4).astype(F32), -32 * (r % 4))
-        ref[:, 2 * r * T : (2 * r + 1) * T] = inner
-        outer = jnp.where(lane < 32, outer, rolled(inner.astype(F32), 32))
-        ref[:, (2 * r + 1) * T : (2 * r + 2) * T] = outer.astype(BF)
-
-
-def grad_kernel(place, own, nextx, nexty, middle, sums1, hid, send, field, shifts, sums2):
-    spread(middle, 0, hid)
+        outer = jnp.where(lane < 32, outer, rolled(inner.astype(F32), 32)).astype(BF)
+        stacked(place, ref, 2, 8, r + 1, 0, inner)
+        stacked(place, ref, 2, 8, r + 1, 1, outer)
+
+
+def grad_kernel(place, own, nextx, nexty, middle, sums1, send, hid, field, shifts, sums2):
+    spread(place, middle, 0, hid)
     lane = lanes()
     for r in range(2, 10):
         field[:, (2 * r - 4) * T : (2 * r - 3) * T] = jnp.where(lane >= 32, row_of(own, nextx, 1, r), 0.0)
@@ -252,13 +246,14 @@
         tile = rolled(tile, 64) if r % 2 else tile
         field[:, (2 * r - 3) * T : (2 * r - 2) * T] = jnp.where(lane < 32, tile, 0.0)
     shifted(field[...], place, shifts)
-    correlate(place, shifts, hid, 0, sums2)
+    correlate(shifts, hid[...], sums2)
     rows = jnp.concatenate([sums1[...], sums2[...], jnp.zeros((32, T), F32)], axis=0)
     send[...] = rows.astype(BF).reshape(8, 112, T)
 
 
-def second_kernel(place, block, middle, hid, w2rows, keep, give, pre, prods):
-    spread(middle, 1, pre)
+def second_kernel(place, block, middle, w2rows, keep, give, hid, pre, prods):
+    spread(place, middle, 0, hid)
+    spread(place, middle, 1, pre)
 
     def store(which, value):
         for x in range(8):
@@ -269,10 +264,10 @@
                 else:
                     give[which, x - 6, side] = tile
 
-    product(w2rows[...].reshape(432, T), hid, prods, MID)
-    store(0, combine(prods, 1, OWN, 1, place))
-    product(gathered_filter(block, 36), pre, prods, MID)
-    store(1, combine(prods, -1, OWN, 1, place))
+    product(by_tap(w2rows[...].reshape(432, T), 1), hid, prods, OWN)
+    store(0, combine(prods, 1, OWN, place))
+    product(by_tap(gathered_filter(block, 36), -1), pre, prods, OWN)
+    store(1, combine(prods, -1, OWN, place))
 
 
 def back_kernel(keep, taken, rows, give):
@@ -352,10 +347,10 @@
         first_kernel,
         (shape(8, 26, 16, T), shape(432, T, dtype=F32)),
         [
-            pltpu.VMEM((T, EXT), BF),
-            pltpu.VMEM((T, EXT), BF),
-            pltpu.VMEM((432, EXT), F32),
-            pltpu.VMEM((432, EXT), F32),
+            pltpu.VMEM((3 * T, MID), BF),
+            pltpu.VMEM((3 * T, MID), BF),
+            pltpu.VMEM((144, MID), F32),
+            pltpu.VMEM((144, MID), F32),
             pltpu.VMEM((144, OWN), BF),
         ],
         scalars=True,
@@ -363,20 +358,25 @@
     )(place, block, w1)
     middle = lax.all_to_all(middle, "af", 0, 0)
     many = shape(8, 112, T)
-    hid, parts = call(
+    parts = call(
         grad_kernel,
-        (shape(T, MID), many),
-        [pltpu.VMEM((16, OWN), F32), pltpu.VMEM((144, OWN), BF), pltpu.VMEM((432, T), F32)],
+        many,
+        [
+            pltpu.VMEM((3 * T, OWN), BF),
+            pltpu.VMEM((16, OWN), F32),
+            pltpu.VMEM((144, OWN), BF),
+            pltpu.VMEM((432, T), F32),
+        ],
         scalars=True,
         limit=16,
     )(place, own, nextx, nexty, middle, sums)
     keep, give = call(
         second_kernel,
         (shape(2, 6, 2, 16, T), shape(2, 2, 2, 16, T)),
-        [pltpu.VMEM((T, MID), BF), pltpu.VMEM((432, MID), F32)],
+        [pltpu.VMEM((3 * T, OWN), BF)] * 2 + [pltpu.VMEM((144, OWN), F32)],
         scalars=True,
         limit=20,
-    )(place, block, middle, hid, w2)
+    )(place, block, middle, w2)
     parts = lax.all_to_all(parts, "gx", 0, 0)
     parts, keep, give = lax.optimization_barrier((parts, keep, give))
     parts = call(functools.partial(sum_kernel, 1.0), many)(parts)

time: 118 us -> 117 us (level)
  no operation moved by 1% of the time
where the time goes in v4:
time: 117 us; the launch traced here: 116 us
  blocking collectives  38.9 us (33%)
  starting transfers between devices  33.9 us (29%)
  waiting for transfers between devices  26.8 us (23%)
  Pallas kernels  11.9 us (10%)
  local copies, waits for them, and re-layouts  3.69 us (3%)
    all_to_all x1, blocking collectives, on_device(): lax.all_to_all(call(send_kernel, shape(8, 44, 16, T))(own, nextx, nexty,...  23.4 us
    ppermute x4, starting transfers between devices, cyclic(): return lax.ppermute(x, axis, [(i, (i + step) % size) for i in range(size)])  20.6 us
    all_to_all x1, blocking collectives, on_device(): middle = lax.all_to_all(middle, 'af', 0, 0)  15.5 us
    ppermute x4, waiting for transfers between devices, cyclic(): return lax.ppermute(x, axis, [(i, (i + step) % size) for i in range(size)])  11.9 us
    pallas_call x12, Pallas kernels, run(): pl.pallas_call(kernel, out_shape=outs, in_specs=[HBM if hbm else SMEM if...  11.9 us
    all_to_all x2, waiting for transfers between devices, on_device(): parts = lax.all_to_all(parts, 'gx', 0, 0)  9.99 us
    all_to_all x2, starting transfers between devices, on_device(): parts = lax.all_to_all(parts, 'gx', 0, 0)  8.17 us
    all_to_all x1, starting transfers between devices, on_device(): parts = lax.all_to_all(parts, GY, 0, 0)  5.12 us
  transfers between devices with their start and end apart: 7, of which 6 were waited for; matrix products, arithmetic and copies ran while one was open for 0% of the time, Pallas kernels for 4%

profile of v4, /device:TPU:2, one launch (start us, length us, event | category | flops | bytes accessed | tf_op | source)
XLA Modules:
  0.0 116.1 jit_solution(6168363361482543279)
XLA Ops:
  0.6 0.9 copy-done.4
  1.6 0.9 copy-done.5
  2.5 0.3 shard_map.75
  2.8 10.9 %collective-permute-start = (bf16[2,4,16,128]{3,2,1,0:T(8,128)(2,1)S(1)}, bf16[2,4,16,128]{3,2,1,0:T(8,128)(2,1)S(1)}, u32[]{:S(2)}, u32[]{:S(2)}) collective-permute-start(bf16[2,4,16,128]{3,2,1,0:T(8,128)(2,1)S(1)} %get-tuple-element.27), channel_id=1, source_target_pairs={{0,448},{64,0},{128,64},{192,128},{256,192},{320,256},{384,320},{4... | collective-permute-start | bytes 98312 | tf_op jit(solution)/shard_map/ppermute | solution.py:320
  13.8 0.9 copy-done
  14.7 0.9 copy-done.2
  15.6 0.8 shard_map.76.weights
  16.4 0.1 shard_map.77
  16.5 5.3 %collective-permute-start.1 = (bf16[2,6,16,128]{3,2,1,0:T(8,128)(2,1)S(1)}, bf16[2,6,16,128]{3,2,1,0:T(8,128)(2,1)S(1)}, u32[]{:S(2)}, u32[]{:S(2)}) collective-permute-start(bf16[2,6,16,128]{3,2,1,0:T(8,128)(2,1)S(1)} %shard_map.77), channel_id=1, source_target_pairs={{0,56},{8,0},{16,8},{24,16},{32,24},{40,32},{48,40},{56,48},{1,57}... | collective-permute-start | bytes 147464 | tf_op jit(solution)/shard_map/ppermute | solution.py:320
  21.8 0.1 pad_add_fusion.place
  21.9 2.1 %collective-permute-done.1.nexty = bf16[2,6,16,128]{3,2,1,0:T(8,128)(2,1)S(1)} collective-permute-done((bf16[2,6,16,128]{3,2,1,0:T(8,128)(2,1)S(1)}, bf16[2,6,16,128]{3,2,1,0:T(8,128)(2,1)S(1)}, u32[]{:S(2)}, u32[]{:S(2)}) %collective-permute-start.1) | collective-permute-done | bytes 49184 | tf_op jit(solution)/shard_map/ppermute | solution.py:320
  24.0 0.2 shard_map.78
  24.2 23.4 %all_to_all.25.block = bf16[8,44,16,128]{3,2,1,0:T(8,128)(2,1)S(1)} all-to-all(bf16[8,44,16,128]{3,2,1,0:T(8,128)(2,1)S(1)} %shard_map.78), channel_id=1, replica_groups=mesh['gx'=8,'yh'=4,'co'=2,'af'=8] {'af'}, dimensions={0} | all-to-all | bytes 2883584 | tf_op jit(solution)/shard_map/all_to_all | solution.py:345
  47.6 2.8 %shard_map.79 = (bf16[8,26,16,128]{3,2,1,0:T(8,128)(2,1)S(1)}, f32[432,128]{1,0:T(8,128)S(1)}) custom-call(s32[2]{0:T(128)S(1)} %pad_add_fusion.place, bf16[8,44,16,128]{3,2,1,0:T(8,128)(2,1)S(1)} %all_to_all.25.block, bf16[27,16,128]{2,1,0:T(8,128)(2,1)S(1)} %bitcast.7), custom_call_target="tpu_custom_call" | custom-call | tf_op jit(solution)/shard_map/pallas_call | solution.py:24
  50.4 15.5 %all_to_all.26.middle = bf16[8,26,16,128]{3,2,1,0:T(8,128)(2,1)S(1)} all-to-all(bf16[8,26,16,128]{3,2,1,0:T(8,128)(2,1)S(1)} %get-tuple-element.32), channel_id=1, replica_groups=mesh['gx'=8,'yh'=4,'co'=2,'af'=8] {'af'}, dimensions={0} | all-to-all | bytes 1703936 | tf_op jit(solution)/shard_map/all_to_all | solution.py:359
  65.9 2.2 %shard_map.80 = bf16[8,112,128]{2,1,0:T(8,128)(2,1)} custom-call(s32[2]{0:T(128)S(1)} %pad_add_fusion.place, bf16[2,8,16,128]{3,2,1,0:T(8,128)(2,1)S(1)} %get-tuple-element.26.own, bf16[2,4,16,128]{3,2,1,0:T(8,128)(2,1)S(1)} %collective-permute-done.nextx, bf16[2,6,16,128]{3,2,1,0:T(8,128)(2,1)S(1)} %collective-permute-done.1.nexty, ...), custom_call_target="tpu_custom_call" | custom-call | tf_op jit(solution)/shard_map/pallas_call | solution.py:24
  68.1 4.8 %all-to-all-start.2 = ((bf16[8,112,128]{2,1,0:T(8,128)(2,1)}), bf16[8,112,128]{2,1,0:T(8,128)(2,1)S(1)}, u32[]{:S(2)}, u32[]{:S(2)}) async-start(bf16[8,112,128]{2,1,0:T(8,128)(2,1)} %shard_map.80), calls=%async_computation.2 | async-start | bytes 458752 | tf_op jit(solution)/shard_map/all_to_all | solution.py:380
  72.9 2.0 %shard_map.81 = (bf16[2,6,2,16,128]{4,3,2,1,0:T(8,128)(2,1)S(1)}, bf16[2,2,2,16,128]{4,3,2,1,0:T(8,128)(2,1)S(1)}) custom-call(s32[2]{0:T(128)S(1)} %pad_add_fusion.place, bf16[8,44,16,128]{3,2,1,0:T(8,128)(2,1)S(1)} %all_to_all.25.block, bf16[8,26,16,128]{3,2,1,0:T(8,128)(2,1)S(1)} %all_to_all.26.middle, bf16[27,16,128]{2,1,0:T(8,128)(2,1)S(1)} %bitcast.9), custom_call_target="tpu_custom_call" | custom-call | tf_op jit(solution)/shard_map/pallas_call | solution.py:24
  74.9 8.1 %all-to-all-done.2.parts = bf16[8,112,128]{2,1,0:T(8,128)(2,1)S(1)} async-done(((bf16[8,112,128]{2,1,0:T(8,128)(2,1)}), bf16[8,112,128]{2,1,0:T(8,128)(2,1)S(1)}, u32[]{:S(2)}, u32[]{:S(2)}) %all-to-all-start.2) | async-done | bytes 229408 | tf_op jit(solution)/shard_map/all_to_all | solution.py:380
  83.0 0.7 shard_map.82
  83.8 5.1 %all-to-all-start.3 = ((bf16[8,112,128]{2,1,0:T(8,128)(2,1)}), bf16[8,112,128]{2,1,0:T(8,128)(2,1)S(1)}, u32[]{:S(2)}, u32[]{:S(2)}) async-start(bf16[8,112,128]{2,1,0:T(8,128)(2,1)} %shard_map.82), calls=%async_computation.3 | async-start | bytes 458752 | tf_op jit(solution)/shard_map/all_to_all | solution.py:384
  88.9 2.4 %collective-permute-start.2 = (bf16[2,2,2,16,128]{4,3,2,1,0:T(8,128)(2,1)S(1)}, bf16[2,2,2,16,128]{4,3,2,1,0:T(8,128)(2,1)S(1)}, u32[]{:S(2)}, u32[]{:S(2)}) collective-permute-start(bf16[2,2,2,16,128]{4,3,2,1,0:T(8,128)(2,1)S(1)} %get-tuple-element.38), channel_id=1, source_target_pairs={{0,64},{64,128},{128,192},{192,256},{256,320},{320,384},{384,448},... | collective-permute-start | bytes 98312 | tf_op jit(solution)/shard_map/ppermute | solution.py:320
  91.3 4.6 %collective-permute-done.2.taken = bf16[2,2,2,16,128]{4,3,2,1,0:T(8,128)(2,1)S(1)} collective-permute-done((bf16[2,2,2,16,128]{4,3,2,1,0:T(8,128)(2,1)S(1)}, bf16[2,2,2,16,128]{4,3,2,1,0:T(8,128)(2,1)S(1)}, u32[]{:S(2)}, u32[]{:S(2)}) %collective-permute-start.2) | collective-permute-done | bytes 32800 | tf_op jit(solution)/shard_map/ppermute | solution.py:320
  95.9 0.1 shard_map.83
  96.0 5.0 %all-to-all-done.3.parts = bf16[8,112,128]{2,1,0:T(8,128)(2,1)S(1)} async-done(((bf16[8,112,128]{2,1,0:T(8,128)(2,1)}), bf16[8,112,128]{2,1,0:T(8,128)(2,1)S(1)}, u32[]{:S(2)}, u32[]{:S(2)}) %all-to-all-start.3) | async-done | bytes 229408 | tf_op jit(solution)/shard_map/all_to_all | solution.py:384
  100.9 0.7 shard_map.85
  101.7 3.4 %all-to-all-start.4 = ((bf16[8,112,128]{2,1,0:T(8,128)(2,1)}), bf16[8,112,128]{2,1,0:T(8,128)(2,1)S(1)}, u32[]{:S(2)}, u32[]{:S(2)}) async-start(bf16[8,112,128]{2,1,0:T(8,128)(2,1)} %shard_map.85), calls=%async_computation.4 | async-start | bytes 458752 | tf_op jit(solution)/shard_map/all_to_all | solution.py:388
  105.1 1.9 %collective-permute-start.3 = (bf16[2,2,16,128]{3,2,1,0:T(8,128)(2,1)S(1)}, bf16[2,2,16,128]{3,2,1,0:T(8,128)(2,1)S(1)}, u32[]{:S(2)}, u32[]{:S(2)}) collective-permute-start(bf16[2,2,16,128]{3,2,1,0:T(8,128)(2,1)S(1)} %get-tuple-element.42), channel_id=1, source_target_pairs={{0,8},{8,16},{16,24},{24,32},{32,40},{40,48},{48,56},{56,0},{1,9},... | collective-permute-start | bytes 49160 | tf_op jit(solution)/shard_map/ppermute | solution.py:320
  107.0 5.2 %collective-permute-done.3.taken = bf16[2,2,16,128]{3,2,1,0:T(8,128)(2,1)S(1)} collective-permute-done((bf16[2,2,16,128]{3,2,1,0:T(8,128)(2,1)S(1)}, bf16[2,2,16,128]{3,2,1,0:T(8,128)(2,1)S(1)}, u32[]{:S(2)}, u32[]{:S(2)}) %collective-permute-start.3) | collective-permute-done | bytes 16416 | tf_op jit(solution)/shard_map/ppermute | solution.py:320
  112.2 1.2 shard_map.84
  113.4 1.9 %all-to-all-done.4.parts = bf16[8,112,128]{2,1,0:T(8,128)(2,1)S(1)} async-done(((bf16[8,112,128]{2,1,0:T(8,128)(2,1)}), bf16[8,112,128]{2,1,0:T(8,128)(2,1)S(1)}, u32[]{:S(2)}, u32[]{:S(2)}) %all-to-all-start.4) | async-done | bytes 229408 | tf_op jit(solution)/shard_map/all_to_all | solution.py:388
  115.3 0.8 shard_map.86
  (9 shorter events, 0.0 us)
Async XLA Ops:
  0.6 1.0 copy-start.4
  1.6 0.9 copy-start.5
  2.8 13.6 %collective-permute-start = (bf16[2,4,16,128]{3,2,1,0:T(8,128)(2,1)S(1)}, bf16[2,4,16,128]{3,2,1,0:T(8,128)(2,1)S(1)}, u32[]{:S(2)}, u32[]{:S(2)}) collective-permute-start(bf16[2,4,16,128]{3,2,1,0:T(8,128)(2,1)S(1)} %get-tuple-element.27), channel_id=1, source_target_pairs={{0,448},{64,0},{128,64},{192,128},{256,192},{320,256},{384,320},{4... | collective-permute-start | bytes 98312 | tf_op jit(solution)/shard_map/ppermute | solution.py:320
  13.8 0.9 copy-start
  14.7 0.9 copy-start.2
  16.5 7.5 %collective-permute-start.1 = (bf16[2,6,16,128]{3,2,1,0:T(8,128)(2,1)S(1)}, bf16[2,6,16,128]{3,2,1,0:T(8,128)(2,1)S(1)}, u32[]{:S(2)}, u32[]{:S(2)}) collective-permute-start(bf16[2,6,16,128]{3,2,1,0:T(8,128)(2,1)S(1)} %shard_map.77), channel_id=1, source_target_pairs={{0,56},{8,0},{16,8},{24,16},{32,24},{40,32},{48,40},{56,48},{1,57}... | collective-permute-start | bytes 147464 | tf_op jit(solution)/shard_map/ppermute | solution.py:320
  24.1 23.4 %copy-start.1 = (bf16[16,27,128]{2,0,1:T(8,128)(2,1)S(1)}, bf16[16,27,128]{2,0,1:T(8,128)(2,1)}, u32[]{:S(2)}) copy-start(bf16[16,27,128]{2,0,1:T(8,128)(2,1)} %param.5) | copy-start | bytes 331780
  50.4 22.5 %copy-start.3 = (bf16[16,27,128]{2,0,1:T(8,128)(2,1)S(1)}, bf16[16,27,128]{2,0,1:T(8,128)(2,1)}, u32[]{:S(2)}) copy-start(bf16[16,27,128]{2,0,1:T(8,128)(2,1)} %param.6) | copy-start | bytes 331780
  68.1 14.9 %all-to-all-start.2 = ((bf16[8,112,128]{2,1,0:T(8,128)(2,1)}), bf16[8,112,128]{2,1,0:T(8,128)(2,1)S(1)}, u32[]{:S(2)}, u32[]{:S(2)}) async-start(bf16[8,112,128]{2,1,0:T(8,128)(2,1)} %shard_map.80), calls=%async_computation.2 | async-start | bytes 458752 | tf_op jit(solution)/shard_map/all_to_all | solution.py:380
  83.8 17.2 %all-to-all-start.3 = ((bf16[8,112,128]{2,1,0:T(8,128)(2,1)}), bf16[8,112,128]{2,1,0:T(8,128)(2,1)S(1)}, u32[]{:S(2)}, u32[]{:S(2)}) async-start(bf16[8,112,128]{2,1,0:T(8,128)(2,1)} %shard_map.82), calls=%async_computation.3 | async-start | bytes 458752 | tf_op jit(solution)/shard_map/all_to_all | solution.py:384
  88.9 7.0 %collective-permute-start.2 = (bf16[2,2,2,16,128]{4,3,2,1,0:T(8,128)(2,1)S(1)}, bf16[2,2,2,16,128]{4,3,2,1,0:T(8,128)(2,1)S(1)}, u32[]{:S(2)}, u32[]{:S(2)}) collective-permute-start(bf16[2,2,2,16,128]{4,3,2,1,0:T(8,128)(2,1)S(1)} %get-tuple-element.38), channel_id=1, source_target_pairs={{0,64},{64,128},{128,192},{192,256},{256,320},{320,384},{384,448},... | collective-permute-start | bytes 98312 | tf_op jit(solution)/shard_map/ppermute | solution.py:320
  101.7 13.6 %all-to-all-start.4 = ((bf16[8,112,128]{2,1,0:T(8,128)(2,1)}), bf16[8,112,128]{2,1,0:T(8,128)(2,1)S(1)}, u32[]{:S(2)}, u32[]{:S(2)}) async-start(bf16[8,112,128]{2,1,0:T(8,128)(2,1)} %shard_map.85), calls=%async_computation.4 | async-start | bytes 458752 | tf_op jit(solution)/shard_map/all_to_all | solution.py:388
  105.1 7.2 %collective-permute-start.3 = (bf16[2,2,16,128]{3,2,1,0:T(8,128)(2,1)S(1)}, bf16[2,2,16,128]{3,2,1,0:T(8,128)(2,1)S(1)}, u32[]{:S(2)}, u32[]{:S(2)}) collective-permute-start(bf16[2,2,16,128]{3,2,1,0:T(8,128)(2,1)S(1)} %get-tuple-element.42), channel_id=1, source_target_pairs={{0,8},{8,16},{16,24},{24,32},{32,40},{40,48},{48,56},{56,0},{1,9},... | collective-permute-start | bytes 49160 | tf_op jit(solution)/shard_map/ppermute | solution.py:320

commit v5 on v4

--- a/solution.py
+++ b/solution.py
@@ -377,7 +377,7 @@
         scalars=True,
         limit=20,
     )(place, block, middle, w2)
-    parts = lax.all_to_all(parts, "gx", 0, 0)
+    parts = lax.all_to_all(parts, "gx", 0, 0, axis_index_groups=[[0, 4, 1, 5, 2, 6, 3, 7]])
     parts, keep, give = lax.optimization_barrier((parts, keep, give))
     parts = call(functools.partial(sum_kernel, 1.0), many)(parts)
     rows, give = call(back_kernel, (two, shape(2, 2, 16, T)))(keep, cyclic(give, "gx", 1))
@@ -385,7 +385,7 @@
     parts, rows, give = lax.optimization_barrier((parts, rows, give))
     parts = call(functools.partial(sum_kernel, factor), many)(parts)
     output, volume_grad = call(out_kernel, (shape(1, 8, 8, 16, 16), shape(1, 8, 8, 16, 16)))(rows, cyclic(give, GY, 1))
-    parts = lax.all_to_all(parts, "gx", 0, 0)
+    parts = lax.all_to_all(parts, "gx", 0, 0, axis_index_groups=[[0, 4, 1, 5, 2, 6, 3, 7]])
     wide = shape(27, 16, T, dtype=F32)
     first_grad, second_grad = call(last_kernel, (wide, wide))(parts)
     return output, volume_grad, first_grad.transpose(1, 0, 2), second_grad.transpose(1, 0, 2)

time: 117 us -> 113 us (0.966)
  the two profiles are of different devices: /device:TPU:2 before, /device:TPU:8 now
where the time goes in v5:
time: 113 us
  blocking collectives  40.2 us (36%)
  starting transfers between devices  35.1 us (31%)
  waiting for transfers between devices  21.1 us (19%)
  Pallas kernels  11.9 us (11%)
  local copies, waits for them, and re-layouts  3.69 us (3%)
    all_to_all x1, blocking collectives, on_device(): lax.all_to_all(call(send_kernel, shape(8, 44, 16, T))(own, nextx, nexty,...  24.7 us
    ppermute x4, starting transfers between devices, cyclic(): return lax.ppermute(x, axis, [(i, (i + step) % size) for i in range(size)])  21.6 us
    all_to_all x1, blocking collectives, on_device(): middle = lax.all_to_all(middle, 'af', 0, 0)  15.5 us
    pallas_call x12, Pallas kernels, run(): pl.pallas_call(kernel, out_shape=outs, in_specs=[HBM if hbm else SMEM if...  11.9 us
    ppermute x4, waiting for transfers between devices, cyclic(): return lax.ppermute(x, axis, [(i, (i + step) % size) for i in range(size)])  9.55 us
    all_to_all x2, starting transfers between devices, on_device(): lax.all_to_all(parts, 'gx', 0, 0, axis_index_groups=[[0, 4, 1, 5, 2, 6, 3...  8.94 us
    all_to_all x2, waiting for transfers between devices, on_device(): lax.all_to_all(parts, 'gx', 0, 0, axis_index_groups=[[0, 4, 1, 5, 2, 6, 3...  6.57 us
    all_to_all x1, waiting for transfers between devices, on_device(): parts = lax.all_to_all(parts, GY, 0, 0)  4.95 us
  transfers between devices with their start and end apart: 7, of which 5 were waited for; matrix products, arithmetic and copies ran while one was open for 0% of the time, Pallas kernels for 4%

profile of v5, /device:TPU:8, one launch (start us, length us, event | category | flops | bytes accessed | tf_op | source)
XLA Modules:
  0.0 112.8 jit_solution(14980298659652878279)
XLA Ops:
  0.6 0.9 copy-done.4
  1.6 0.9 copy-done.5
  2.5 0.3 shard_map.75
  2.8 10.9 %collective-permute-start = (bf16[2,4,16,128]{3,2,1,0:T(8,128)(2,1)S(1)}, bf16[2,4,16,128]{3,2,1,0:T(8,128)(2,1)S(1)}, u32[]{:S(2)}, u32[]{:S(2)}) collective-permute-start(bf16[2,4,16,128]{3,2,1,0:T(8,128)(2,1)S(1)} %get-tuple-element.27), channel_id=1, source_target_pairs={{0,448},{64,0},{128,64},{192,128},{256,192},{320,256},{384,320},{4... | collective-permute-start | bytes 98312 | tf_op jit(solution)/shard_map/ppermute | solution.py:320
  13.8 0.9 copy-done
  14.7 0.9 copy-done.2
  15.6 0.8 shard_map.76.weights
  16.4 0.1 shard_map.77
  16.5 4.4 %collective-permute-start.1 = (bf16[2,6,16,128]{3,2,1,0:T(8,128)(2,1)S(1)}, bf16[2,6,16,128]{3,2,1,0:T(8,128)(2,1)S(1)}, u32[]{:S(2)}, u32[]{:S(2)}) collective-permute-start(bf16[2,6,16,128]{3,2,1,0:T(8,128)(2,1)S(1)} %shard_map.77), channel_id=1, source_target_pairs={{0,56},{8,0},{16,8},{24,16},{32,24},{40,32},{48,40},{56,48},{1,57}... | collective-permute-start | bytes 147464 | tf_op jit(solution)/shard_map/ppermute | solution.py:320
  20.9 0.1 pad_add_fusion.place
  21.0 1.7 %collective-permute-done.1.nexty = bf16[2,6,16,128]{3,2,1,0:T(8,128)(2,1)S(1)} collective-permute-done((bf16[2,6,16,128]{3,2,1,0:T(8,128)(2,1)S(1)}, bf16[2,6,16,128]{3,2,1,0:T(8,128)(2,1)S(1)}, u32[]{:S(2)}, u32[]{:S(2)}) %collective-permute-start.1) | collective-permute-done | bytes 49184 | tf_op jit(solution)/shard_map/ppermute | solution.py:320
  22.7 0.2 shard_map.78
  22.8 24.7 %all_to_all.25.block = bf16[8,44,16,128]{3,2,1,0:T(8,128)(2,1)S(1)} all-to-all(bf16[8,44,16,128]{3,2,1,0:T(8,128)(2,1)S(1)} %shard_map.78), channel_id=1, replica_groups=mesh['gx'=8,'yh'=4,'co'=2,'af'=8] {'af'}, dimensions={0} | all-to-all | bytes 2883584 | tf_op jit(solution)/shard_map/all_to_all | solution.py:345
  47.5 2.8 %shard_map.79 = (bf16[8,26,16,128]{3,2,1,0:T(8,128)(2,1)S(1)}, f32[432,128]{1,0:T(8,128)S(1)}) custom-call(s32[2]{0:T(128)S(1)} %pad_add_fusion.place, bf16[8,44,16,128]{3,2,1,0:T(8,128)(2,1)S(1)} %all_to_all.25.block, bf16[27,16,128]{2,1,0:T(8,128)(2,1)S(1)} %bitcast.7), custom_call_target="tpu_custom_call" | custom-call | tf_op jit(solution)/shard_map/pallas_call | solution.py:24
  50.4 0.0 copy-start.3
  50.4 15.5 %all_to_all.26.middle = bf16[8,26,16,128]{3,2,1,0:T(8,128)(2,1)S(1)} all-to-all(bf16[8,26,16,128]{3,2,1,0:T(8,128)(2,1)S(1)} %get-tuple-element.32), channel_id=1, replica_groups=mesh['gx'=8,'yh'=4,'co'=2,'af'=8] {'af'}, dimensions={0} | all-to-all | bytes 1703936 | tf_op jit(solution)/shard_map/all_to_all | solution.py:359
  65.9 2.2 %shard_map.80 = bf16[8,112,128]{2,1,0:T(8,128)(2,1)} custom-call(s32[2]{0:T(128)S(1)} %pad_add_fusion.place, bf16[2,8,16,128]{3,2,1,0:T(8,128)(2,1)S(1)} %get-tuple-element.26.own, bf16[2,4,16,128]{3,2,1,0:T(8,128)(2,1)S(1)} %collective-permute-done.nextx, bf16[2,6,16,128]{3,2,1,0:T(8,128)(2,1)S(1)} %collective-permute-done.1.nexty, ...), custom_call_target="tpu_custom_call" | custom-call | tf_op jit(solution)/shard_map/pallas_call | solution.py:24
  68.1 4.8 %all-to-all-start.2 = ((bf16[8,112,128]{2,1,0:T(8,128)(2,1)}), bf16[8,112,128]{2,1,0:T(8,128)(2,1)S(1)}, u32[]{:S(2)}, u32[]{:S(2)}) async-start(bf16[8,112,128]{2,1,0:T(8,128)(2,1)} %shard_map.80), calls=%async_computation.2 | async-start | bytes 458752 | tf_op jit(solution)/shard_map/all_to_all | solution.py:380
  72.9 2.0 %shard_map.81 = (bf16[2,6,2,16,128]{4,3,2,1,0:T(8,128)(2,1)S(1)}, bf16[2,2,2,16,128]{4,3,2,1,0:T(8,128)(2,1)S(1)}) custom-call(s32[2]{0:T(128)S(1)} %pad_add_fusion.place, bf16[8,44,16,128]{3,2,1,0:T(8,128)(2,1)S(1)} %all_to_all.25.block, bf16[8,26,16,128]{3,2,1,0:T(8,128)(2,1)S(1)} %all_to_all.26.middle, bf16[27,16,128]{2,1,0:T(8,128)(2,1)S(1)} %bitcast.9), custom_call_target="tpu_custom_call" | custom-call | tf_op jit(solution)/shard_map/pallas_call | solution.py:24
  74.9 6.6 %all-to-all-done.2.parts = bf16[8,112,128]{2,1,0:T(8,128)(2,1)S(1)} async-done(((bf16[8,112,128]{2,1,0:T(8,128)(2,1)}), bf16[8,112,128]{2,1,0:T(8,128)(2,1)S(1)}, u32[]{:S(2)}, u32[]{:S(2)}) %all-to-all-start.2) | async-done | bytes 229408 | tf_op jit(solution)/shard_map/all_to_all | solution.py:380
  81.5 0.7 shard_map.82
  82.2 4.6 %all-to-all-start.3 = ((bf16[8,112,128]{2,1,0:T(8,128)(2,1)}), bf16[8,112,128]{2,1,0:T(8,128)(2,1)S(1)}, u32[]{:S(2)}, u32[]{:S(2)}) async-start(bf16[8,112,128]{2,1,0:T(8,128)(2,1)} %shard_map.82), calls=%async_computation.3 | async-start | bytes 458752 | tf_op jit(solution)/shard_map/all_to_all | solution.py:384
  86.8 4.4 %collective-permute-start.2 = (bf16[2,2,2,16,128]{4,3,2,1,0:T(8,128)(2,1)S(1)}, bf16[2,2,2,16,128]{4,3,2,1,0:T(8,128)(2,1)S(1)}, u32[]{:S(2)}, u32[]{:S(2)}) collective-permute-start(bf16[2,2,2,16,128]{4,3,2,1,0:T(8,128)(2,1)S(1)} %get-tuple-element.38), channel_id=1, source_target_pairs={{0,64},{64,128},{128,192},{192,256},{256,320},{320,384},{384,448},... | collective-permute-start | bytes 98312 | tf_op jit(solution)/shard_map/ppermute | solution.py:320
  91.1 2.6 %collective-permute-done.2.taken = bf16[2,2,2,16,128]{4,3,2,1,0:T(8,128)(2,1)S(1)} collective-permute-done((bf16[2,2,2,16,128]{4,3,2,1,0:T(8,128)(2,1)S(1)}, bf16[2,2,2,16,128]{4,3,2,1,0:T(8,128)(2,1)S(1)}, u32[]{:S(2)}, u32[]{:S(2)}) %collective-permute-start.2) | collective-permute-done | bytes 32800 | tf_op jit(solution)/shard_map/ppermute | solution.py:320
  93.8 0.1 shard_map.83
  93.9 4.9 %all-to-all-done.3.parts = bf16[8,112,128]{2,1,0:T(8,128)(2,1)S(1)} async-done(((bf16[8,112,128]{2,1,0:T(8,128)(2,1)}), bf16[8,112,128]{2,1,0:T(8,128)(2,1)S(1)}, u32[]{:S(2)}, u32[]{:S(2)}) %all-to-all-start.3) | async-done | bytes 229408 | tf_op jit(solution)/shard_map/all_to_all | solution.py:384
  98.8 0.7 shard_map.85
  99.5 4.1 %all-to-all-start.4 = ((bf16[8,112,128]{2,1,0:T(8,128)(2,1)}), bf16[8,112,128]{2,1,0:T(8,128)(2,1)S(1)}, u32[]{:S(2)}, u32[]{:S(2)}) async-start(bf16[8,112,128]{2,1,0:T(8,128)(2,1)} %shard_map.85), calls=%async_computation.4 | async-start | bytes 458752 | tf_op jit(solution)/shard_map/all_to_all | solution.py:388
  103.7 1.9 %collective-permute-start.3 = (bf16[2,2,16,128]{3,2,1,0:T(8,128)(2,1)S(1)}, bf16[2,2,16,128]{3,2,1,0:T(8,128)(2,1)S(1)}, u32[]{:S(2)}, u32[]{:S(2)}) collective-permute-start(bf16[2,2,16,128]{3,2,1,0:T(8,128)(2,1)S(1)} %get-tuple-element.42), channel_id=1, source_target_pairs={{0,8},{8,16},{16,24},{24,32},{32,40},{40,48},{48,56},{56,0},{1,9},... | collective-permute-start | bytes 49160 | tf_op jit(solution)/shard_map/ppermute | solution.py:320
  105.6 5.2 %collective-permute-done.3.taken = bf16[2,2,16,128]{3,2,1,0:T(8,128)(2,1)S(1)} collective-permute-done((bf16[2,2,16,128]{3,2,1,0:T(8,128)(2,1)S(1)}, bf16[2,2,16,128]{3,2,1,0:T(8,128)(2,1)S(1)}, u32[]{:S(2)}, u32[]{:S(2)}) %collective-permute-start.3) | collective-permute-done | bytes 16416 | tf_op jit(solution)/shard_map/ppermute | solution.py:320
  110.8 1.2 %shard_map.84 = (bf16[1,8,8,16,16]{4,3,2,1,0:T(8,128)(2,1)}, bf16[1,8,8,16,16]{4,3,2,1,0:T(8,128)(2,1)}) custom-call(bf16[2,8,16,128]{3,2,1,0:T(8,128)(2,1)S(1)} %get-tuple-element.41.rows, bf16[2,2,16,128]{3,2,1,0:T(8,128)(2,1)S(1)} %collective-permute-done.3.taken), custom_call_target="tpu_custom_call" | custom-call | tf_op jit(solution)/shard_map/pallas_call | solution.py:24
  112.0 0.8 shard_map.86
  (9 shorter events, 0.0 us)
Async XLA Ops:
  0.6 1.0 copy-start.4
  1.6 0.9 copy-start.5
  2.8 13.6 %collective-permute-start = (bf16[2,4,16,128]{3,2,1,0:T(8,128)(2,1)S(1)}, bf16[2,4,16,128]{3,2,1,0:T(8,128)(2,1)S(1)}, u32[]{:S(2)}, u32[]{:S(2)}) collective-permute-start(bf16[2,4,16,128]{3,2,1,0:T(8,128)(2,1)S(1)} %get-tuple-element.27), channel_id=1, source_target_pairs={{0,448},{64,0},{128,64},{192,128},{256,192},{320,256},{384,320},{4... | collective-permute-start | bytes 98312 | tf_op jit(solution)/shard_map/ppermute | solution.py:320
  13.8 0.9 copy-start
  14.7 0.9 copy-start.2
  16.5 6.2 %collective-permute-start.1 = (bf16[2,6,16,128]{3,2,1,0:T(8,128)(2,1)S(1)}, bf16[2,6,16,128]{3,2,1,0:T(8,128)(2,1)S(1)}, u32[]{:S(2)}, u32[]{:S(2)}) collective-permute-start(bf16[2,6,16,128]{3,2,1,0:T(8,128)(2,1)S(1)} %shard_map.77), channel_id=1, source_target_pairs={{0,56},{8,0},{16,8},{24,16},{32,24},{40,32},{48,40},{56,48},{1,57}... | collective-permute-start | bytes 147464 | tf_op jit(solution)/shard_map/ppermute | solution.py:320
  22.8 24.7 %copy-start.1 = (bf16[16,27,128]{2,0,1:T(8,128)(2,1)S(1)}, bf16[16,27,128]{2,0,1:T(8,128)(2,1)}, u32[]{:S(2)}) copy-start(bf16[16,27,128]{2,0,1:T(8,128)(2,1)} %param.5) | copy-start | bytes 331780
  50.4 22.5 %copy-start.3 = (bf16[16,27,128]{2,0,1:T(8,128)(2,1)S(1)}, bf16[16,27,128]{2,0,1:T(8,128)(2,1)}, u32[]{:S(2)}) copy-start(bf16[16,27,128]{2,0,1:T(8,128)(2,1)} %param.6) | copy-start | bytes 331780
  68.1 13.4 %all-to-all-start.2 = ((bf16[8,112,128]{2,1,0:T(8,128)(2,1)}), bf16[8,112,128]{2,1,0:T(8,128)(2,1)S(1)}, u32[]{:S(2)}, u32[]{:S(2)}) async-start(bf16[8,112,128]{2,1,0:T(8,128)(2,1)} %shard_map.80), calls=%async_computation.2 | async-start | bytes 458752 | tf_op jit(solution)/shard_map/all_to_all | solution.py:380
  82.2 16.6 %all-to-all-start.3 = ((bf16[8,112,128]{2,1,0:T(8,128)(2,1)}), bf16[8,112,128]{2,1,0:T(8,128)(2,1)S(1)}, u32[]{:S(2)}, u32[]{:S(2)}) async-start(bf16[8,112,128]{2,1,0:T(8,128)(2,1)} %shard_map.82), calls=%async_computation.3 | async-start | bytes 458752 | tf_op jit(solution)/shard_map/all_to_all | solution.py:384
  86.8 7.0 %collective-permute-start.2 = (bf16[2,2,2,16,128]{4,3,2,1,0:T(8,128)(2,1)S(1)}, bf16[2,2,2,16,128]{4,3,2,1,0:T(8,128)(2,1)S(1)}, u32[]{:S(2)}, u32[]{:S(2)}) collective-permute-start(bf16[2,2,2,16,128]{4,3,2,1,0:T(8,128)(2,1)S(1)} %get-tuple-element.38), channel_id=1, source_target_pairs={{0,64},{64,128},{128,192},{192,256},{256,320},{320,384},{384,448},... | collective-permute-start | bytes 98312 | tf_op jit(solution)/shard_map/ppermute | solution.py:320
  99.5 12.5 %all-to-all-start.4 = ((bf16[8,112,128]{2,1,0:T(8,128)(2,1)}), bf16[8,112,128]{2,1,0:T(8,128)(2,1)S(1)}, u32[]{:S(2)}, u32[]{:S(2)}) async-start(bf16[8,112,128]{2,1,0:T(8,128)(2,1)} %shard_map.85), calls=%async_computation.4 | async-start | bytes 458752 | tf_op jit(solution)/shard_map/all_to_all | solution.py:388
  103.7 7.2 %collective-permute-start.3 = (bf16[2,2,16,128]{3,2,1,0:T(8,128)(2,1)S(1)}, bf16[2,2,16,128]{3,2,1,0:T(8,128)(2,1)S(1)}, u32[]{:S(2)}, u32[]{:S(2)}) collective-permute-start(bf16[2,2,16,128]{3,2,1,0:T(8,128)(2,1)S(1)} %get-tuple-element.42), channel_id=1, source_target_pairs={{0,8},{8,16},{16,24},{24,32},{32,40},{40,48},{48,56},{56,0},{1,9},... | collective-permute-start | bytes 49160 | tf_op jit(solution)/shard_map/ppermute | solution.py:320

commit v6 on v5

--- a/solution.py
+++ b/solution.py
@@ -14,7 +14,7 @@
 VMEM = pl.BlockSpec(memory_space=pltpu.VMEM)
 SMEM = pl.BlockSpec(memory_space=pltpu.SMEM)
 HBM = pl.BlockSpec(memory_space=pltpu.HBM)
-GY = ("yh", "co")
+GY = ("y1", "y0", "co")
 MID = 20 * T
 OWN = 16 * T
 
@@ -381,7 +381,7 @@
     parts, keep, give = lax.optimization_barrier((parts, keep, give))
     parts = call(functools.partial(sum_kernel, 1.0), many)(parts)
     rows, give = call(back_kernel, (two, shape(2, 2, 16, T)))(keep, cyclic(give, "gx", 1))
-    parts = lax.all_to_all(parts, GY, 0, 0)
+    parts = lax.all_to_all(parts, ("y0", "y1", "co"), 0, 0)
     parts, rows, give = lax.optimization_barrier((parts, rows, give))
     parts = call(functools.partial(sum_kernel, factor), many)(parts)
     output, volume_grad = call(out_kernel, (shape(1, 8, 8, 16, 16), shape(1, 8, 8, 16, 16)))(rows, cyclic(give, GY, 1))
@@ -392,7 +392,7 @@
 
 
 def solution(mesh):
-    split = jax.sharding.Mesh(mesh.devices.reshape(8, 4, 2, 8), ("gx", "yh", "co", "af"))
+    split = jax.sharding.Mesh(mesh.devices.reshape(8, 2, 2, 2, 8), ("gx", "y1", "y0", "co", "af"))
     cells = P(None, "gx", GY, None, "af")
     weights = P("af", None, None)
     return jax.shard_map(

time: 113 us -> 113 us (level)
  the two profiles are of different devices: /device:TPU:8 before, /device:TPU:80 now
where the time goes in v6:
time: 113 us; the launch traced here: 112 us
  blocking collectives  43.1 us (38%)
  starting transfers between devices  29.1 us (26%)
  waiting for transfers between devices  23.7 us (21%)
  Pallas kernels  11.9 us (11%)
  local copies, waits for them, and re-layouts  3.69 us (3%)
    all_to_all x1, blocking collectives, on_device(): lax.all_to_all(call(send_kernel, shape(8, 44, 16, T))(own, nextx, nexty,...  24.3 us
    all_to_all x1, blocking collectives, on_device(): middle = lax.all_to_all(middle, 'af', 0, 0)  18.8 us
    all_to_all x2, starting transfers between devices, on_device(): lax.all_to_all(parts, 'gx', 0, 0, axis_index_groups=[[0, 4, 1, 5, 2, 6, 3...  14.5 us
    pallas_call x12, Pallas kernels, run(): pl.pallas_call(kernel, out_shape=outs, in_specs=[HBM if hbm else SMEM if...  11.9 us
    ppermute x4, waiting for transfers between devices, cyclic(): return lax.ppermute(x, axis, [(i, (i + step) % size) for i in range(size)])  10.3 us
    all_to_all x2, waiting for transfers between devices, on_device(): lax.all_to_all(parts, 'gx', 0, 0, axis_index_groups=[[0, 4, 1, 5, 2, 6, 3...  9.63 us
    ppermute x4, starting transfers between devices, cyclic(): return lax.ppermute(x, axis, [(i, (i + step) % size) for i in range(size)])  8.52 us
    all_to_all x1, starting transfers between devices, on_device(): parts = lax.all_to_all(parts, ('y0', 'y1', 'co'), 0, 0)  6.03 us
  transfers between devices with their start and end apart: 7, of which 7 were waited for; matrix products, arithmetic and copies ran while one was open for 0% of the time, Pallas kernels for 4%

profile of v6, /device:TPU:80, one launch (start us, length us, event | category | flops | bytes accessed | tf_op | source)
XLA Modules:
  0.0 112.2 jit_solution(3251007675659163458)
XLA Ops:
  0.6 0.9 copy-done.4
  1.6 0.9 copy-done.5
  2.5 0.3 shard_map.75
  2.8 1.9 %collective-permute-start = (bf16[2,4,16,128]{3,2,1,0:T(8,128)(2,1)S(1)}, bf16[2,4,16,128]{3,2,1,0:T(8,128)(2,1)S(1)}, u32[]{:S(2)}, u32[]{:S(2)}) collective-permute-start(bf16[2,4,16,128]{3,2,1,0:T(8,128)(2,1)S(1)} %get-tuple-element.27), channel_id=1, source_target_pairs={{0,448},{64,0},{128,64},{192,128},{256,192},{320,256},{384,320},{4... | collective-permute-start | bytes 98312 | tf_op jit(solution)/shard_map/ppermute | solution.py:320
  4.8 0.9 copy-done
  5.7 0.9 copy-done.2
  6.6 0.8 shard_map.76.weights
  7.4 1.6 %collective-permute-done.nextx = bf16[2,4,16,128]{3,2,1,0:T(8,128)(2,1)S(1)} collective-permute-done((bf16[2,4,16,128]{3,2,1,0:T(8,128)(2,1)S(1)}, bf16[2,4,16,128]{3,2,1,0:T(8,128)(2,1)S(1)}, u32[]{:S(2)}, u32[]{:S(2)}) %collective-permute-start) | collective-permute-done | bytes 32800 | tf_op jit(solution)/shard_map/ppermute | solution.py:320
  9.0 0.1 shard_map.77
  9.1 1.9 %collective-permute-start.1 = (bf16[2,6,16,128]{3,2,1,0:T(8,128)(2,1)S(1)}, bf16[2,6,16,128]{3,2,1,0:T(8,128)(2,1)S(1)}, u32[]{:S(2)}, u32[]{:S(2)}) collective-permute-start(bf16[2,6,16,128]{3,2,1,0:T(8,128)(2,1)S(1)} %shard_map.77), channel_id=1, source_target_pairs={{0,56},{8,0},{16,8},{24,16},{32,24},{40,32},{48,40},{56,48},{1,57}... | collective-permute-start | bytes 147464 | tf_op jit(solution)/shard_map/ppermute | solution.py:320
  11.1 1.6 %collective-permute-done.1.nexty = bf16[2,6,16,128]{3,2,1,0:T(8,128)(2,1)S(1)} collective-permute-done((bf16[2,6,16,128]{3,2,1,0:T(8,128)(2,1)S(1)}, bf16[2,6,16,128]{3,2,1,0:T(8,128)(2,1)S(1)}, u32[]{:S(2)}, u32[]{:S(2)}) %collective-permute-start.1) | collective-permute-done | bytes 49184 | tf_op jit(solution)/shard_map/ppermute | solution.py:320
  12.7 0.2 shard_map.78
  12.9 24.3 %all_to_all.25.block = bf16[8,44,16,128]{3,2,1,0:T(8,128)(2,1)S(1)} all-to-all(bf16[8,44,16,128]{3,2,1,0:T(8,128)(2,1)S(1)} %shard_map.78), channel_id=1, replica_groups=mesh['gx'=8,'y1'=2,'y0'=2,'co'=2,'af'=8] {'af'}, dimensions={0} | all-to-all | bytes 2883584 | tf_op jit(solution)/shard_map/all_to_all | solution.py:345
  37.2 2.8 %shard_map.79 = (bf16[8,26,16,128]{3,2,1,0:T(8,128)(2,1)S(1)}, f32[432,128]{1,0:T(8,128)S(1)}) custom-call(s32[2]{0:T(128)S(1)} %pad_add_fusion.place, bf16[8,44,16,128]{3,2,1,0:T(8,128)(2,1)S(1)} %all_to_all.25.block, bf16[27,16,128]{2,1,0:T(8,128)(2,1)S(1)} %bitcast.7), custom_call_target="tpu_custom_call" | custom-call | tf_op jit(solution)/shard_map/pallas_call | solution.py:24
  40.0 18.8 %all_to_all.26.middle = bf16[8,26,16,128]{3,2,1,0:T(8,128)(2,1)S(1)} all-to-all(bf16[8,26,16,128]{3,2,1,0:T(8,128)(2,1)S(1)} %get-tuple-element.32), channel_id=1, replica_groups=mesh['gx'=8,'y1'=2,'y0'=2,'co'=2,'af'=8] {'af'}, dimensions={0} | all-to-all | bytes 1703936 | tf_op jit(solution)/shard_map/all_to_all | solution.py:359
  58.8 2.2 %shard_map.80 = bf16[8,112,128]{2,1,0:T(8,128)(2,1)} custom-call(s32[2]{0:T(128)S(1)} %pad_add_fusion.place, bf16[2,8,16,128]{3,2,1,0:T(8,128)(2,1)S(1)} %get-tuple-element.26.own, bf16[2,4,16,128]{3,2,1,0:T(8,128)(2,1)S(1)} %collective-permute-done.nextx, bf16[2,6,16,128]{3,2,1,0:T(8,128)(2,1)S(1)} %collective-permute-done.1.nexty, ...), custom_call_target="tpu_custom_call" | custom-call | tf_op jit(solution)/shard_map/pallas_call | solution.py:24
  61.0 10.8 %all-to-all-start.2 = ((bf16[8,112,128]{2,1,0:T(8,128)(2,1)}), bf16[8,112,128]{2,1,0:T(8,128)(2,1)S(1)}, u32[]{:S(2)}, u32[]{:S(2)}) async-start(bf16[8,112,128]{2,1,0:T(8,128)(2,1)} %shard_map.80), calls=%async_computation.2 | async-start | bytes 458752 | tf_op jit(solution)/shard_map/all_to_all | solution.py:380
  71.8 2.0 %shard_map.81 = (bf16[2,6,2,16,128]{4,3,2,1,0:T(8,128)(2,1)S(1)}, bf16[2,2,2,16,128]{4,3,2,1,0:T(8,128)(2,1)S(1)}) custom-call(s32[2]{0:T(128)S(1)} %pad_add_fusion.place, bf16[8,44,16,128]{3,2,1,0:T(8,128)(2,1)S(1)} %all_to_all.25.block, bf16[8,26,16,128]{3,2,1,0:T(8,128)(2,1)S(1)} %all_to_all.26.middle, bf16[27,16,128]{2,1,0:T(8,128)(2,1)S(1)} %bitcast.9), custom_call_target="tpu_custom_call" | custom-call | tf_op jit(solution)/shard_map/pallas_call | solution.py:24
  73.9 7.5 %all-to-all-done.2.parts = bf16[8,112,128]{2,1,0:T(8,128)(2,1)S(1)} async-done(((bf16[8,112,128]{2,1,0:T(8,128)(2,1)}), bf16[8,112,128]{2,1,0:T(8,128)(2,1)S(1)}, u32[]{:S(2)}, u32[]{:S(2)}) %all-to-all-start.2) | async-done | bytes 229408 | tf_op jit(solution)/shard_map/all_to_all | solution.py:380
  81.4 0.7 shard_map.82
  82.1 6.0 %all-to-all-start.3 = ((bf16[8,112,128]{2,1,0:T(8,128)(2,1)}), bf16[8,112,128]{2,1,0:T(8,128)(2,1)S(1)}, u32[]{:S(2)}, u32[]{:S(2)}) async-start(bf16[8,112,128]{2,1,0:T(8,128)(2,1)} %shard_map.82), calls=%async_computation.3 | async-start | bytes 458752 | tf_op jit(solution)/shard_map/all_to_all | solution.py:384
  88.1 2.8 %collective-permute-start.2 = (bf16[2,2,2,16,128]{4,3,2,1,0:T(8,128)(2,1)S(1)}, bf16[2,2,2,16,128]{4,3,2,1,0:T(8,128)(2,1)S(1)}, u32[]{:S(2)}, u32[]{:S(2)}) collective-permute-start(bf16[2,2,2,16,128]{4,3,2,1,0:T(8,128)(2,1)S(1)} %get-tuple-element.38), channel_id=1, source_target_pairs={{0,64},{64,128},{128,192},{192,256},{256,320},{320,384},{384,448},... | collective-permute-start | bytes 98312 | tf_op jit(solution)/shard_map/ppermute | solution.py:320
  90.9 3.0 %collective-permute-done.2.taken = bf16[2,2,2,16,128]{4,3,2,1,0:T(8,128)(2,1)S(1)} collective-permute-done((bf16[2,2,2,16,128]{4,3,2,1,0:T(8,128)(2,1)S(1)}, bf16[2,2,2,16,128]{4,3,2,1,0:T(8,128)(2,1)S(1)}, u32[]{:S(2)}, u32[]{:S(2)}) %collective-permute-start.2) | collective-permute-done | bytes 32800 | tf_op jit(solution)/shard_map/ppermute | solution.py:320
  93.9 0.1 shard_map.83
  94.0 3.8 %all-to-all-done.3.parts = bf16[8,112,128]{2,1,0:T(8,128)(2,1)S(1)} async-done(((bf16[8,112,128]{2,1,0:T(8,128)(2,1)}), bf16[8,112,128]{2,1,0:T(8,128)(2,1)S(1)}, u32[]{:S(2)}, u32[]{:S(2)}) %all-to-all-start.3) | async-done | bytes 229408 | tf_op jit(solution)/shard_map/all_to_all | solution.py:384
  97.8 0.7 shard_map.85
  98.5 3.7 %all-to-all-start.4 = ((bf16[8,112,128]{2,1,0:T(8,128)(2,1)}), bf16[8,112,128]{2,1,0:T(8,128)(2,1)S(1)}, u32[]{:S(2)}, u32[]{:S(2)}) async-start(bf16[8,112,128]{2,1,0:T(8,128)(2,1)} %shard_map.85), calls=%async_computation.4 | async-start | bytes 458752 | tf_op jit(solution)/shard_map/all_to_all | solution.py:388
  102.2 1.9 %collective-permute-start.3 = (bf16[2,2,16,128]{3,2,1,0:T(8,128)(2,1)S(1)}, bf16[2,2,16,128]{3,2,1,0:T(8,128)(2,1)S(1)}, u32[]{:S(2)}, u32[]{:S(2)}) collective-permute-start(bf16[2,2,16,128]{3,2,1,0:T(8,128)(2,1)S(1)} %get-tuple-element.42), channel_id=1, source_target_pairs={{0,8},{8,16},{16,24},{24,32},{32,40},{40,48},{48,56},{56,0},{1,9},... | collective-permute-start | bytes 49160 | tf_op jit(solution)/shard_map/ppermute | solution.py:320
  104.2 4.0 %collective-permute-done.3.taken = bf16[2,2,16,128]{3,2,1,0:T(8,128)(2,1)S(1)} collective-permute-done((bf16[2,2,16,128]{3,2,1,0:T(8,128)(2,1)S(1)}, bf16[2,2,16,128]{3,2,1,0:T(8,128)(2,1)S(1)}, u32[]{:S(2)}, u32[]{:S(2)}) %collective-permute-start.3) | collective-permute-done | bytes 16416 | tf_op jit(solution)/shard_map/ppermute | solution.py:320
  108.2 1.2 %shard_map.84 = (bf16[1,8,8,16,16]{4,3,2,1,0:T(8,128)(2,1)}, bf16[1,8,8,16,16]{4,3,2,1,0:T(8,128)(2,1)}) custom-call(bf16[2,8,16,128]{3,2,1,0:T(8,128)(2,1)S(1)} %get-tuple-element.41.rows, bf16[2,2,16,128]{3,2,1,0:T(8,128)(2,1)S(1)} %collective-permute-done.3.taken), custom_call_target="tpu_custom_call" | custom-call | tf_op jit(solution)/shard_map/pallas_call | solution.py:24
  109.3 2.1 %all-to-all-done.4.parts = bf16[8,112,128]{2,1,0:T(8,128)(2,1)S(1)} async-done(((bf16[8,112,128]{2,1,0:T(8,128)(2,1)}), bf16[8,112,128]{2,1,0:T(8,128)(2,1)S(1)}, u32[]{:S(2)}, u32[]{:S(2)}) %all-to-all-start.4) | async-done | bytes 229408 | tf_op jit(solution)/shard_map/all_to_all | solution.py:388
  111.5 0.8 shard_map.86
  (9 shorter events, 0.1 us)
Async XLA Ops:
  0.6 1.0 copy-start.4
  1.6 0.9 copy-start.5
  2.8 6.2 %collective-permute-start = (bf16[2,4,16,128]{3,2,1,0:T(8,128)(2,1)S(1)}, bf16[2,4,16,128]{3,2,1,0:T(8,128)(2,1)S(1)}, u32[]{:S(2)}, u32[]{:S(2)}) collective-permute-start(bf16[2,4,16,128]{3,2,1,0:T(8,128)(2,1)S(1)} %get-tuple-element.27), channel_id=1, source_target_pairs={{0,448},{64,0},{128,64},{192,128},{256,192},{320,256},{384,320},{4... | collective-permute-start | bytes 98312 | tf_op jit(solution)/shard_map/ppermute | solution.py:320
  4.8 0.9 copy-start
  5.7 0.9 copy-start.2
  9.1 3.7 %collective-permute-start.1 = (bf16[2,6,16,128]{3,2,1,0:T(8,128)(2,1)S(1)}, bf16[2,6,16,128]{3,2,1,0:T(8,128)(2,1)S(1)}, u32[]{:S(2)}, u32[]{:S(2)}) collective-permute-start(bf16[2,6,16,128]{3,2,1,0:T(8,128)(2,1)S(1)} %shard_map.77), channel_id=1, source_target_pairs={{0,56},{8,0},{16,8},{24,16},{32,24},{40,32},{48,40},{56,48},{1,57}... | collective-permute-start | bytes 147464 | tf_op jit(solution)/shard_map/ppermute | solution.py:320
  12.9 24.3 %copy-start.1 = (bf16[16,27,128]{2,0,1:T(8,128)(2,1)S(1)}, bf16[16,27,128]{2,0,1:T(8,128)(2,1)}, u32[]{:S(2)}) copy-start(bf16[16,27,128]{2,0,1:T(8,128)(2,1)} %param.5) | copy-start | bytes 331780
  40.0 31.8 %copy-start.3 = (bf16[16,27,128]{2,0,1:T(8,128)(2,1)S(1)}, bf16[16,27,128]{2,0,1:T(8,128)(2,1)}, u32[]{:S(2)}) copy-start(bf16[16,27,128]{2,0,1:T(8,128)(2,1)} %param.6) | copy-start | bytes 331780
  61.0 20.4 %all-to-all-start.2 = ((bf16[8,112,128]{2,1,0:T(8,128)(2,1)}), bf16[8,112,128]{2,1,0:T(8,128)(2,1)S(1)}, u32[]{:S(2)}, u32[]{:S(2)}) async-start(bf16[8,112,128]{2,1,0:T(8,128)(2,1)} %shard_map.80), calls=%async_computation.2 | async-start | bytes 458752 | tf_op jit(solution)/shard_map/all_to_all | solution.py:380
  82.1 15.7 %all-to-all-start.3 = ((bf16[8,112,128]{2,1,0:T(8,128)(2,1)}), bf16[8,112,128]{2,1,0:T(8,128)(2,1)S(1)}, u32[]{:S(2)}, u32[]{:S(2)}) async-start(bf16[8,112,128]{2,1,0:T(8,128)(2,1)} %shard_map.82), calls=%async_computation.3 | async-start | bytes 458752 | tf_op jit(solution)/shard_map/all_to_all | solution.py:384
  88.1 5.8 %collective-permute-start.2 = (bf16[2,2,2,16,128]{4,3,2,1,0:T(8,128)(2,1)S(1)}, bf16[2,2,2,16,128]{4,3,2,1,0:T(8,128)(2,1)S(1)}, u32[]{:S(2)}, u32[]{:S(2)}) collective-permute-start(bf16[2,2,2,16,128]{4,3,2,1,0:T(8,128)(2,1)S(1)} %get-tuple-element.38), channel_id=1, source_target_pairs={{0,64},{64,128},{128,192},{192,256},{256,320},{320,384},{384,448},... | collective-permute-start | bytes 98312 | tf_op jit(solution)/shard_map/ppermute | solution.py:320
  98.5 12.9 %all-to-all-start.4 = ((bf16[8,112,128]{2,1,0:T(8,128)(2,1)}), bf16[8,112,128]{2,1,0:T(8,128)(2,1)S(1)}, u32[]{:S(2)}, u32[]{:S(2)}) async-start(bf16[8,112,128]{2,1,0:T(8,128)(2,1)} %shard_map.85), calls=%async_computation.4 | async-start | bytes 458752 | tf_op jit(solution)/shard_map/all_to_all | solution.py:388
  102.2 5.9 %collective-permute-start.3 = (bf16[2,2,16,128]{3,2,1,0:T(8,128)(2,1)S(1)}, bf16[2,2,16,128]{3,2,1,0:T(8,128)(2,1)S(1)}, u32[]{:S(2)}, u32[]{:S(2)}) collective-permute-start(bf16[2,2,16,128]{3,2,1,0:T(8,128)(2,1)S(1)} %get-tuple-element.42), channel_id=1, source_target_pairs={{0,8},{8,16},{16,24},{24,32},{32,40},{40,48},{48,56},{56,0},{1,9},... | collective-permute-start | bytes 49160 | tf_op jit(solution)/shard_map/ppermute | solution.py:320

commit v7 on v6

--- a/solution.py
+++ b/solution.py
@@ -381,7 +381,7 @@
     parts, keep, give = lax.optimization_barrier((parts, keep, give))
     parts = call(functools.partial(sum_kernel, 1.0), many)(parts)
     rows, give = call(back_kernel, (two, shape(2, 2, 16, T)))(keep, cyclic(give, "gx", 1))
-    parts = lax.all_to_all(parts, ("y0", "y1", "co"), 0, 0)
+    parts = lax.all_to_all(parts, ("y0", "co", "y1"), 0, 0)
     parts, rows, give = lax.optimization_barrier((parts, rows, give))
     parts = call(functools.partial(sum_kernel, factor), many)(parts)
     output, volume_grad = call(out_kernel, (shape(1, 8, 8, 16, 16), shape(1, 8, 8, 16, 16)))(rows, cyclic(give, GY, 1))

time: 113 us -> 114 us (level)
  the two profiles are of different devices: /device:TPU:80 before, /device:TPU:73 now
where the time goes in v7:
time: 114 us; the launch traced here: 113 us
  blocking collectives  39.6 us (35%)
  starting transfers between devices  32.2 us (28%)
  waiting for transfers between devices  24.8 us (22%)
  Pallas kernels  11.9 us (10%)
  local copies, waits for them, and re-layouts  3.69 us (3%)
    all_to_all x1, blocking collectives, on_device(): lax.all_to_all(call(send_kernel, shape(8, 44, 16, T))(own, nextx, nexty,...  23.5 us
    all_to_all x1, blocking collectives, on_device(): middle = lax.all_to_all(middle, 'af', 0, 0)  16 us
    all_to_all x2, starting transfers between devices, on_device(): lax.all_to_all(parts, 'gx', 0, 0, axis_index_groups=[[0, 4, 1, 5, 2, 6, 3...  13.8 us
    pallas_call x12, Pallas kernels, run(): pl.pallas_call(kernel, out_shape=outs, in_specs=[HBM if hbm else SMEM if...  11.9 us
    all_to_all x2, waiting for transfers between devices, on_device(): lax.all_to_all(parts, 'gx', 0, 0, axis_index_groups=[[0, 4, 1, 5, 2, 6, 3...  10.5 us
    ppermute x4, starting transfers between devices, cyclic(): return lax.ppermute(x, axis, [(i, (i + step) % size) for i in range(size)])  10 us
    all_to_all x1, starting transfers between devices, on_device(): parts = lax.all_to_all(parts, ('y0', 'co', 'y1'), 0, 0)  8.45 us
    ppermute x4, waiting for transfers between devices, cyclic(): return lax.ppermute(x, axis, [(i, (i + step) % size) for i in range(size)])  7.97 us
  transfers between devices with their start and end apart: 7, of which 7 were waited for; matrix products, arithmetic and copies ran while one was open for 0% of the time, Pallas kernels for 4%

profile of v7, /device:TPU:73, one launch (start us, length us, event | category | flops | bytes accessed | tf_op | source)
XLA Modules:
  0.0 113.0 jit_solution(2926780718018317855)
XLA Ops:
  0.6 0.9 copy-done.4
  1.6 0.9 copy-done.5
  2.5 0.3 shard_map.75
  2.8 1.9 %collective-permute-start = (bf16[2,4,16,128]{3,2,1,0:T(8,128)(2,1)S(1)}, bf16[2,4,16,128]{3,2,1,0:T(8,128)(2,1)S(1)}, u32[]{:S(2)}, u32[]{:S(2)}) collective-permute-start(bf16[2,4,16,128]{3,2,1,0:T(8,128)(2,1)S(1)} %get-tuple-element.27), channel_id=1, source_target_pairs={{0,448},{64,0},{128,64},{192,128},{256,192},{320,256},{384,320},{4... | collective-permute-start | bytes 98312 | tf_op jit(solution)/shard_map/ppermute | solution.py:320
  4.8 0.9 copy-done
  5.7 0.9 copy-done.2
  6.6 0.8 shard_map.76.weights
  7.4 0.7 collective-permute-done.nextx
  8.1 0.1 shard_map.77
  8.2 3.5 %collective-permute-start.1 = (bf16[2,6,16,128]{3,2,1,0:T(8,128)(2,1)S(1)}, bf16[2,6,16,128]{3,2,1,0:T(8,128)(2,1)S(1)}, u32[]{:S(2)}, u32[]{:S(2)}) collective-permute-start(bf16[2,6,16,128]{3,2,1,0:T(8,128)(2,1)S(1)} %shard_map.77), channel_id=1, source_target_pairs={{0,56},{8,0},{16,8},{24,16},{32,24},{40,32},{48,40},{56,48},{1,57}... | collective-permute-start | bytes 147464 | tf_op jit(solution)/shard_map/ppermute | solution.py:320
  11.7 3.9 %collective-permute-done.1.nexty = bf16[2,6,16,128]{3,2,1,0:T(8,128)(2,1)S(1)} collective-permute-done((bf16[2,6,16,128]{3,2,1,0:T(8,128)(2,1)S(1)}, bf16[2,6,16,128]{3,2,1,0:T(8,128)(2,1)S(1)}, u32[]{:S(2)}, u32[]{:S(2)}) %collective-permute-start.1) | collective-permute-done | bytes 49184 | tf_op jit(solution)/shard_map/ppermute | solution.py:320
  15.6 0.2 shard_map.78
  15.8 23.5 %all_to_all.25.block = bf16[8,44,16,128]{3,2,1,0:T(8,128)(2,1)S(1)} all-to-all(bf16[8,44,16,128]{3,2,1,0:T(8,128)(2,1)S(1)} %shard_map.78), channel_id=1, replica_groups=mesh['gx'=8,'y1'=2,'y0'=2,'co'=2,'af'=8] {'af'}, dimensions={0} | all-to-all | bytes 2883584 | tf_op jit(solution)/shard_map/all_to_all | solution.py:345
  39.3 2.8 %shard_map.79 = (bf16[8,26,16,128]{3,2,1,0:T(8,128)(2,1)S(1)}, f32[432,128]{1,0:T(8,128)S(1)}) custom-call(s32[2]{0:T(128)S(1)} %pad_add_fusion.place, bf16[8,44,16,128]{3,2,1,0:T(8,128)(2,1)S(1)} %all_to_all.25.block, bf16[27,16,128]{2,1,0:T(8,128)(2,1)S(1)} %bitcast.7), custom_call_target="tpu_custom_call" | custom-call | tf_op jit(solution)/shard_map/pallas_call | solution.py:24
  42.2 16.0 %all_to_all.26.middle = bf16[8,26,16,128]{3,2,1,0:T(8,128)(2,1)S(1)} all-to-all(bf16[8,26,16,128]{3,2,1,0:T(8,128)(2,1)S(1)} %get-tuple-element.32), channel_id=1, replica_groups=mesh['gx'=8,'y1'=2,'y0'=2,'co'=2,'af'=8] {'af'}, dimensions={0} | all-to-all | bytes 1703936 | tf_op jit(solution)/shard_map/all_to_all | solution.py:359
  58.2 2.2 %shard_map.80 = bf16[8,112,128]{2,1,0:T(8,128)(2,1)} custom-call(s32[2]{0:T(128)S(1)} %pad_add_fusion.place, bf16[2,8,16,128]{3,2,1,0:T(8,128)(2,1)S(1)} %get-tuple-element.26.own, bf16[2,4,16,128]{3,2,1,0:T(8,128)(2,1)S(1)} %collective-permute-done.nextx, bf16[2,6,16,128]{3,2,1,0:T(8,128)(2,1)S(1)} %collective-permute-done.1.nexty, ...), custom_call_target="tpu_custom_call" | custom-call | tf_op jit(solution)/shard_map/pallas_call | solution.py:24
  60.4 10.4 %all-to-all-start.2 = ((bf16[8,112,128]{2,1,0:T(8,128)(2,1)}), bf16[8,112,128]{2,1,0:T(8,128)(2,1)S(1)}, u32[]{:S(2)}, u32[]{:S(2)}) async-start(bf16[8,112,128]{2,1,0:T(8,128)(2,1)} %shard_map.80), calls=%async_computation.2 | async-start | bytes 458752 | tf_op jit(solution)/shard_map/all_to_all | solution.py:380
  70.9 2.0 %shard_map.81 = (bf16[2,6,2,16,128]{4,3,2,1,0:T(8,128)(2,1)S(1)}, bf16[2,2,2,16,128]{4,3,2,1,0:T(8,128)(2,1)S(1)}) custom-call(s32[2]{0:T(128)S(1)} %pad_add_fusion.place, bf16[8,44,16,128]{3,2,1,0:T(8,128)(2,1)S(1)} %all_to_all.25.block, bf16[8,26,16,128]{3,2,1,0:T(8,128)(2,1)S(1)} %all_to_all.26.middle, bf16[27,16,128]{2,1,0:T(8,128)(2,1)S(1)} %bitcast.9), custom_call_target="tpu_custom_call" | custom-call | tf_op jit(solution)/shard_map/pallas_call | solution.py:24
  72.9 5.5 %all-to-all-done.2.parts = bf16[8,112,128]{2,1,0:T(8,128)(2,1)S(1)} async-done(((bf16[8,112,128]{2,1,0:T(8,128)(2,1)}), bf16[8,112,128]{2,1,0:T(8,128)(2,1)S(1)}, u32[]{:S(2)}, u32[]{:S(2)}) %all-to-all-start.2) | async-done | bytes 229408 | tf_op jit(solution)/shard_map/all_to_all | solution.py:380
  78.3 0.7 shard_map.82
  79.1 8.4 %all-to-all-start.3 = ((bf16[8,112,128]{2,1,0:T(8,128)(2,1)}), bf16[8,112,128]{2,1,0:T(8,128)(2,1)S(1)}, u32[]{:S(2)}, u32[]{:S(2)}) async-start(bf16[8,112,128]{2,1,0:T(8,128)(2,1)} %shard_map.82), calls=%async_computation.3 | async-start | bytes 458752 | tf_op jit(solution)/shard_map/all_to_all | solution.py:384
  87.5 2.5 %collective-permute-start.2 = (bf16[2,2,2,16,128]{4,3,2,1,0:T(8,128)(2,1)S(1)}, bf16[2,2,2,16,128]{4,3,2,1,0:T(8,128)(2,1)S(1)}, u32[]{:S(2)}, u32[]{:S(2)}) collective-permute-start(bf16[2,2,2,16,128]{4,3,2,1,0:T(8,128)(2,1)S(1)} %get-tuple-element.38), channel_id=1, source_target_pairs={{0,64},{64,128},{128,192},{192,256},{256,320},{320,384},{384,448},... | collective-permute-start | bytes 98312 | tf_op jit(solution)/shard_map/ppermute | solution.py:320
  90.0 2.4 %collective-permute-done.2.taken = bf16[2,2,2,16,128]{4,3,2,1,0:T(8,128)(2,1)S(1)} collective-permute-done((bf16[2,2,2,16,128]{4,3,2,1,0:T(8,128)(2,1)S(1)}, bf16[2,2,2,16,128]{4,3,2,1,0:T(8,128)(2,1)S(1)}, u32[]{:S(2)}, u32[]{:S(2)}) %collective-permute-start.2) | collective-permute-done | bytes 32800 | tf_op jit(solution)/shard_map/ppermute | solution.py:320
  92.5 0.1 shard_map.83
  92.6 6.3 %all-to-all-done.3.parts = bf16[8,112,128]{2,1,0:T(8,128)(2,1)S(1)} async-done(((bf16[8,112,128]{2,1,0:T(8,128)(2,1)}), bf16[8,112,128]{2,1,0:T(8,128)(2,1)S(1)}, u32[]{:S(2)}, u32[]{:S(2)}) %all-to-all-start.3) | async-done | bytes 229408 | tf_op jit(solution)/shard_map/all_to_all | solution.py:384
  98.9 0.7 shard_map.85
  99.6 3.4 %all-to-all-start.4 = ((bf16[8,112,128]{2,1,0:T(8,128)(2,1)}), bf16[8,112,128]{2,1,0:T(8,128)(2,1)S(1)}, u32[]{:S(2)}, u32[]{:S(2)}) async-start(bf16[8,112,128]{2,1,0:T(8,128)(2,1)} %shard_map.85), calls=%async_computation.4 | async-start | bytes 458752 | tf_op jit(solution)/shard_map/all_to_all | solution.py:388
  103.0 2.2 %collective-permute-start.3 = (bf16[2,2,16,128]{3,2,1,0:T(8,128)(2,1)S(1)}, bf16[2,2,16,128]{3,2,1,0:T(8,128)(2,1)S(1)}, u32[]{:S(2)}, u32[]{:S(2)}) collective-permute-start(bf16[2,2,16,128]{3,2,1,0:T(8,128)(2,1)S(1)} %get-tuple-element.42), channel_id=1, source_target_pairs={{0,8},{8,16},{16,24},{24,32},{32,40},{40,48},{48,56},{56,0},{1,9},... | collective-permute-start | bytes 49160 | tf_op jit(solution)/shard_map/ppermute | solution.py:320
  105.1 0.9 collective-permute-done.3.taken
  106.0 1.2 %shard_map.84 = (bf16[1,8,8,16,16]{4,3,2,1,0:T(8,128)(2,1)}, bf16[1,8,8,16,16]{4,3,2,1,0:T(8,128)(2,1)}) custom-call(bf16[2,8,16,128]{3,2,1,0:T(8,128)(2,1)S(1)} %get-tuple-element.41.rows, bf16[2,2,16,128]{3,2,1,0:T(8,128)(2,1)S(1)} %collective-permute-done.3.taken), custom_call_target="tpu_custom_call" | custom-call | tf_op jit(solution)/shard_map/pallas_call | solution.py:24
  107.2 5.0 %all-to-all-done.4.parts = bf16[8,112,128]{2,1,0:T(8,128)(2,1)S(1)} async-done(((bf16[8,112,128]{2,1,0:T(8,128)(2,1)}), bf16[8,112,128]{2,1,0:T(8,128)(2,1)S(1)}, u32[]{:S(2)}, u32[]{:S(2)}) %all-to-all-start.4) | async-done | bytes 229408 | tf_op jit(solution)/shard_map/all_to_all | solution.py:388
  112.2 0.8 shard_map.86
  (9 shorter events, 0.1 us)
Async XLA Ops:
  0.6 1.0 copy-start.4
  1.6 0.9 copy-start.5
  2.8 5.3 %collective-permute-start = (bf16[2,4,16,128]{3,2,1,0:T(8,128)(2,1)S(1)}, bf16[2,4,16,128]{3,2,1,0:T(8,128)(2,1)S(1)}, u32[]{:S(2)}, u32[]{:S(2)}) collective-permute-start(bf16[2,4,16,128]{3,2,1,0:T(8,128)(2,1)S(1)} %get-tuple-element.27), channel_id=1, source_target_pairs={{0,448},{64,0},{128,64},{192,128},{256,192},{320,256},{384,320},{4... | collective-permute-start | bytes 98312 | tf_op jit(solution)/shard_map/ppermute | solution.py:320
  4.8 0.9 copy-start
  5.7 0.9 copy-start.2
  8.2 7.4 %collective-permute-start.1 = (bf16[2,6,16,128]{3,2,1,0:T(8,128)(2,1)S(1)}, bf16[2,6,16,128]{3,2,1,0:T(8,128)(2,1)S(1)}, u32[]{:S(2)}, u32[]{:S(2)}) collective-permute-start(bf16[2,6,16,128]{3,2,1,0:T(8,128)(2,1)S(1)} %shard_map.77), channel_id=1, source_target_pairs={{0,56},{8,0},{16,8},{24,16},{32,24},{40,32},{48,40},{56,48},{1,57}... | collective-permute-start | bytes 147464 | tf_op jit(solution)/shard_map/ppermute | solution.py:320
  15.8 23.5 %copy-start.1 = (bf16[16,27,128]{2,0,1:T(8,128)(2,1)S(1)}, bf16[16,27,128]{2,0,1:T(8,128)(2,1)}, u32[]{:S(2)}) copy-start(bf16[16,27,128]{2,0,1:T(8,128)(2,1)} %param.5) | copy-start | bytes 331780
  42.2 28.7 %copy-start.3 = (bf16[16,27,128]{2,0,1:T(8,128)(2,1)S(1)}, bf16[16,27,128]{2,0,1:T(8,128)(2,1)}, u32[]{:S(2)}) copy-start(bf16[16,27,128]{2,0,1:T(8,128)(2,1)} %param.6) | copy-start | bytes 331780
  60.4 17.9 %all-to-all-start.2 = ((bf16[8,112,128]{2,1,0:T(8,128)(2,1)}), bf16[8,112,128]{2,1,0:T(8,128)(2,1)S(1)}, u32[]{:S(2)}, u32[]{:S(2)}) async-start(bf16[8,112,128]{2,1,0:T(8,128)(2,1)} %shard_map.80), calls=%async_computation.2 | async-start | bytes 458752 | tf_op jit(solution)/shard_map/all_to_all | solution.py:380
  79.1 19.8 %all-to-all-start.3 = ((bf16[8,112,128]{2,1,0:T(8,128)(2,1)}), bf16[8,112,128]{2,1,0:T(8,128)(2,1)S(1)}, u32[]{:S(2)}, u32[]{:S(2)}) async-start(bf16[8,112,128]{2,1,0:T(8,128)(2,1)} %shard_map.82), calls=%async_computation.3 | async-start | bytes 458752 | tf_op jit(solution)/shard_map/all_to_all | solution.py:384
  87.5 4.9 %collective-permute-start.2 = (bf16[2,2,2,16,128]{4,3,2,1,0:T(8,128)(2,1)S(1)}, bf16[2,2,2,16,128]{4,3,2,1,0:T(8,128)(2,1)S(1)}, u32[]{:S(2)}, u32[]{:S(2)}) collective-permute-start(bf16[2,2,2,16,128]{4,3,2,1,0:T(8,128)(2,1)S(1)} %get-tuple-element.38), channel_id=1, source_target_pairs={{0,64},{64,128},{128,192},{192,256},{256,320},{320,384},{384,448},... | collective-permute-start | bytes 98312 | tf_op jit(solution)/shard_map/ppermute | solution.py:320
  99.6 12.6 %all-to-all-start.4 = ((bf16[8,112,128]{2,1,0:T(8,128)(2,1)}), bf16[8,112,128]{2,1,0:T(8,128)(2,1)S(1)}, u32[]{:S(2)}, u32[]{:S(2)}) async-start(bf16[8,112,128]{2,1,0:T(8,128)(2,1)} %shard_map.85), calls=%async_computation.4 | async-start | bytes 458752 | tf_op jit(solution)/shard_map/all_to_all | solution.py:388
  103.0 3.1 %collective-permute-start.3 = (bf16[2,2,16,128]{3,2,1,0:T(8,128)(2,1)S(1)}, bf16[2,2,16,128]{3,2,1,0:T(8,128)(2,1)S(1)}, u32[]{:S(2)}, u32[]{:S(2)}) collective-permute-start(bf16[2,2,16,128]{3,2,1,0:T(8,128)(2,1)S(1)} %get-tuple-element.42), channel_id=1, source_target_pairs={{0,8},{8,16},{16,24},{24,32},{32,40},{40,48},{48,56},{56,0},{1,9},... | collective-permute-start | bytes 49160 | tf_op jit(solution)/shard_map/ppermute | solution.py:320
